TPU v7x, 32 devices: a whole 2x2x4 slice. The times are simulated.
32 devices in a mesh: lon: 8 (over y, x, core), head: 4 (over z).
Axes of the slice: x: 2, y: 2, z: 4, core: 2. Of those that a mesh axis runs over, the one named last changes fastest.
Arguments:
- activations: bfloat16 [16384, 1024], P('lon')
- qkv_weight: bfloat16 [1024, 3072], P(None, 'head'), may hold values from -0.1875 to 0.1875
- attn_grad: bfloat16 [16384, 1024], P('lon', 'head'), may hold values from -6 to 6
- pos_bias: float32 [16, 128, 128], P('head'), may hold values from -4 to 4
- key_counts: int32 [128], P('lon'), may hold values from 32 to 128, as said below
Outputs:
- input_grad: bfloat16 [16384, 1024], P(('lon', 'head'))
- weight_grad: float32 [1024, 3072], P(None, 'head')
Inputs may be any that keep to these rules, and one draw needn't show every extreme that they name: key_counts[g] is the number of valid keys of shifted window g; windows of window row 0 and of the last window row may hold fewer than 128, all others hold 128.
All inputs are finite; a program needn't handle non-finite values.
Results may differ from a plain program's by a relative error of at most 0.019.
The roundings to bfloat16 on the way count: a program that leaves them out, or rounds other values in their place, can miss the bound.
Values may be sent and summed in bfloat16 or wider, within the bound.
No kernel may reach another device: no remote copies, remote signals or barrier semaphores. Data moves between devices by JAX's collectives and lax.ppermute only.
A program may use at most 64 MiB of HBM per device.

v0:
```python
import math

import jax
import jax.numpy as jnp
from jax import lax
from jax.sharding import PartitionSpec as P

HEAD_DIM = 64
WIN = 128
WIN_ROWS = 8
WIN_COLS = 2


def passed_along(shard, axis, by):
    size = lax.axis_size(axis)
    return lax.ppermute(shard, axis, [(i, (i + by) % size) for i in range(size)])


def assemble(block_grid, far_rows):
    first_part = block_grid[:, :, 1]
    second_part = jnp.concatenate([block_grid[:, 1:, 0], far_rows[:, None]], axis=1)
    return jnp.concatenate([first_part, second_part], axis=2)


def window_grads(proj_win, delta_win, pos_bias, valid_count):
    scale_factor = 1.0 / math.sqrt(proj_win.shape[-1])
    queries = proj_win[:, :, :, 0]
    keys_part = proj_win[:, :, :, 1]
    values_part = proj_win[:, :, :, 2]
    scores = (
        jnp.einsum("nqhe,nkhe->nhqk", queries, keys_part, preferred_element_type=jnp.float32)
        * scale_factor
        + pos_bias[None]
    )
    positions = jnp.arange(proj_win.shape[1], dtype=jnp.int32)
    valid_keys = positions[None, :] < valid_count[:, None]
    scores = jnp.where(valid_keys[:, None, None, :], scores, -jnp.inf)
    row_max = jnp.max(scores, axis=-1, keepdims=True)
    weights = jnp.exp(scores - row_max)
    probs = weights / jnp.sum(weights, axis=-1, keepdims=True)
    grad_probs = jnp.einsum(
        "nqhe,nkhe->nhqk", delta_win, values_part, preferred_element_type=jnp.float32
    )
    grad_scores = probs * (grad_probs - jnp.sum(probs * grad_probs, axis=-1, keepdims=True))
    probs_low = probs.astype(jnp.bfloat16)
    grads_low = grad_scores.astype(jnp.bfloat16)
    grad_values = jnp.einsum(
        "nhqk,nqhe->nkhe", probs_low, delta_win, preferred_element_type=jnp.float32
    )
    grad_queries = (
        jnp.einsum("nhqk,nkhe->nqhe", grads_low, keys_part, preferred_element_type=jnp.float32)
        * scale_factor
    )
    grad_keys = (
        jnp.einsum("nhqk,nqhe->nkhe", grads_low, queries, preferred_element_type=jnp.float32)
        * scale_factor
    )
    return jnp.stack([grad_queries, grad_keys, grad_values], axis=3).astype(jnp.bfloat16)


def shards(activations, qkv_weight, attn_grad, pos_bias, key_counts):
    heads_here = pos_bias.shape[0]
    width_all = qkv_weight.shape[1]
    delta_width = attn_grad.shape[1]
    half_len = WIN // 2
    projected = jnp.dot(activations, qkv_weight, preferred_element_type=jnp.float32).astype(
        jnp.bfloat16
    )
    proj_grid = projected.reshape(WIN_ROWS, WIN_COLS, 2, half_len, width_all)
    delta_grid = attn_grad.reshape(WIN_ROWS, WIN_COLS, 2, half_len, delta_width)
    outgoing = jnp.concatenate([proj_grid[:, 0, 0], delta_grid[:, 0, 0]], axis=2)
    incoming = passed_along(outgoing, "lon", -1)
    proj_win = assemble(proj_grid, incoming[:, :, :width_all])
    delta_win = assemble(delta_grid, incoming[:, :, width_all:])
    gradients = window_grads(
        proj_win.reshape(WIN_ROWS * WIN_COLS, WIN, heads_here, 3, HEAD_DIM),
        delta_win.reshape(WIN_ROWS * WIN_COLS, WIN, heads_here, HEAD_DIM),
        pos_bias,
        key_counts,
    ).reshape(WIN_ROWS, WIN_COLS, WIN, width_all)
    leading = gradients[:, :, :half_len]
    trailing = gradients[:, :, half_len:]
    returned = passed_along(trailing[:, WIN_COLS - 1], "lon", 1)
    first_halves = jnp.concatenate([returned[:, None], trailing[:, : WIN_COLS - 1]], axis=1)
    grad_proj = jnp.stack([first_halves, leading], axis=2).reshape(
        WIN_ROWS * WIN_COLS * WIN, width_all
    )
    local_grad = lax.dot_general(
        activations, grad_proj, (((0,), (0,)), ((), ())), preferred_element_type=jnp.float32
    )
    total_tokens = activations.shape[0] * lax.axis_size("lon")
    weight_grad = lax.psum(local_grad, "lon") / math.sqrt(total_tokens)
    partial_grad = lax.dot_general(
        grad_proj, qkv_weight, (((1,), (1,)), ((), ())), preferred_element_type=jnp.float32
    )
    partial_low = lax.optimization_barrier(partial_grad.astype(jnp.bfloat16)).astype(jnp.float32)
    input_grad = lax.psum_scatter(
        partial_low.astype(jnp.bfloat16), "head", scatter_dimension=0, tiled=True
    )
    return (input_grad, weight_grad)


def solution(mesh):
    placed = (P("lon", None), P(None, "head"), P("lon", "head"), P("head", None, None), P("lon"))
    return jax.shard_map(
        shards,
        mesh=mesh,
        in_specs=placed,
        out_specs=(P(("lon", "head"), None), P(None, "head")),
        check_vma=False,
    )
```

profile of v0, /device:TPU:0, one launch (start us, length us, event | category | flops | bytes accessed | tf_op | source)
XLA Modules:
  0.0 206.8 jit_solution(4192289267020894862)
XLA Ops:
  8.1 1.9 slice_bitcast_fusion.7
  9.9 5.6 %convolution_convert_fusion.1 = bf16[2048,768]{1,0:T(8,128)(2,1)S(1)} fusion(bf16[2048,1024]{1,0:T(8,128)(2,1)} %param.5, bf16[1024,768]{1,0:T(8,128)(2,1)S(1)} %copy-done), kind=kOutput, calls=%fused_computation.7 | convolution fusion | flops 3222798336 | bytes 8912896 | tf_op jit(solution)/shard_map/dot_general | solution.py:66
  15.6 1.6 copy-done.5
  19.4 3.3 %collective-permute-start = (bf16[8,64,1024]{2,1,0:T(8,128)(2,1)}, bf16[8,64,1024]{2,1,0:T(8,128)(2,1)}, u32[]{:S(2)}, u32[]{:S(2)}) collective-permute-start(bf16[8,64,1024]{2,1,0:T(8,128)(2,1)} %pad_maximum_fusion.4), channel_id=1, source_target_pairs={{0,28},{4,0},{8,4},{12,8},{16,12},{20,16},{24,20},{28,24},{1,29},{... | collective-permute-start | bytes 3145736 | tf_op jit(solution)/shard_map/ppermute | solution.py:16
  25.8 4.9 %concatenate.28 = bf16[16,64,4,3,64]{4,3,2,1,0:T(4,128)(2,1)} reshape(bf16[8,2,1,64,768]{4,3,1,0,2:T(8,128)(2,1)S(1)} %slice_bitcast_fusion.2) | data formatting | bytes 3145728 | tf_op jit(solution)/shard_map/concatenate | solution.py:22
  30.7 7.5 %copy.39 = bf16[16,64,4,3,64]{1,4,2,0,3:T(8,128)(2,1)} copy(bf16[16,64,4,3,64]{4,3,2,1,0:T(4,128)(2,1)} %concatenate.28) | data formatting | bytes 3145728 | tf_op jit(solution)/shard_map/concatenate | solution.py:22
  43.2 4.9 %concatenate.31 = bf16[16,64,4,3,64]{4,3,2,1,0:T(4,128)(2,1)} reshape(bf16[8,2,64,768]{3,2,1,0:T(8,128)(2,1)S(1)} %pad_maximum_fusion.2) | data formatting | bytes 3145728 | tf_op jit(solution)/shard_map/concatenate | solution.py:22
  48.1 7.5 %copy.40 = bf16[16,64,4,3,64]{1,4,2,0,3:T(8,128)(2,1)} copy(bf16[16,64,4,3,64]{4,3,2,1,0:T(4,128)(2,1)} %concatenate.31) | data formatting | bytes 3145728 | tf_op jit(solution)/shard_map/concatenate | solution.py:22
  55.6 5.8 %fusion.40 = (f32[16,4,128]{2,1,0:T(4,128)S(1)}, f32[16,4,128,128]{2,3,1,0:T(8,128)}) fusion(f32[4,128,128]{1,2,0:T(8,128)S(1)} %copy.41, pred[16,128]{1,0:T(8,128)(4,1)S(1)} %iota_compare_fusion, bf16[16,64,4,3,64]{1,4,2,0,3:T(8,128)(2,1)} %copy.39, bf16[16,64,4,3,64]{1,4,2,0,3:T(8,128)(2,1)} %copy.40), kind=kOutput, calls=%fused_computation.57 | convolution fusion | flops 143655040 | bytes 17074176 | tf_op jit(solution)/shard_map/sub | solution.py:39
  61.4 4.2 %fusion.11 = bf16[16,128,4,1,64]{1,4,2,0,3:T(8,128)(2,1)S(1)} fusion(bf16[16,64,4,64]{1,3,2,0:T(8,128)(2,1)} %bitcast.99, bf16[16,64,4,64]{1,3,2,0:T(8,128)(2,1)S(1)} %bitcast.97, f32[16,4,128,128]{2,3,1,0:T(8,128)} %get-tuple-element.15, f32[16,4,128]{2,1,0:T(4,128)S(1)} %get-tuple-element.14), kind=kOutput, calls=%fused_computation.31 | convolution fusion | flops 138936320 | bytes 6324224 | tf_op jit(solution)/shard_map/nhqk,nqhe->nkhe/dot_general | solution.py:47
  67.2 2.3 %multiply_reduce_fusion = (f32[16,4,128]{2,1,0:T(4,128)S(1)}, f32[16,4,128,128]{2,3,1,0:T(8,128)S(1)}) fusion(f32[16,4,128,128]{2,3,1,0:T(8,128)S(1)} %copy-done.4, f32[16,4,128]{2,1,0:T(4,128)S(1)} %get-tuple-element.14, bf16[16,64,4,3,64]{1,4,2,0,3:T(8,128)(2,1)S(1)} %copy-done.2, bf16[16,64,4,3,64]{1,4,2,0,3:T(8,128)(2,1)S(1)} %copy-done.1, ...), kind=kOutput, calls=%fused_computation.3 | convolution fusion | flops 141549568 | bytes 12648448 | tf_op jit(solution)/shard_map/nqhe,nkhe->nhqk/dot_general | solution.py:41
  74.6 2.2 %slice_bitcast_fusion.1 = (bf16[8,64,768]{1,2,0:T(8,128)(2,1)}, bf16[8,1,64,768]{2,3,1,0:T(8,128)(2,1)S(1)}) fusion(bf16[8,2,128,768]{2,3,1,0:T(8,128)(2,1)S(1)} %bitcast.90), kind=kLoop, calls=%fused_computation.26 | loop fusion | bytes 3145728 | tf_op jit(solution)/shard_map/squeeze | solution.py:83
  76.7 2.4 %copy.49 = bf16[8,64,768]{2,1,0:T(8,128)(2,1)} copy(bf16[8,64,768]{1,2,0:T(8,128)(2,1)} %get-tuple-element.8) | data formatting | bytes 1572864 | tf_op jit(solution)/shard_map/squeeze | solution.py:83
  79.2 12.6 %collective-permute-done.1 = bf16[8,64,768]{2,1,0:T(8,128)(2,1)} collective-permute-done((bf16[8,64,768]{2,1,0:T(8,128)(2,1)}, bf16[8,64,768]{2,1,0:T(8,128)(2,1)}, u32[]{:S(2)}, u32[]{:S(2)}) %collective-permute-start.1) | collective-permute-done | bytes 786464 | tf_op jit(solution)/shard_map/ppermute | solution.py:16
  91.8 2.5 %copy.50 = bf16[8,64,768]{1,2,0:T(8,128)(2,1)} copy(bf16[8,64,768]{2,1,0:T(8,128)(2,1)} %collective-permute-done.1) | data formatting | bytes 1572864 | tf_op jit(solution)/shard_map/ppermute | solution.py:16
  94.3 2.6 %slice_bitcast_fusion = (bf16[8,2,1,64,768]{3,4,1,0,2:T(8,128)(2,1)S(1)}, bf16[8,2,1,64,768]{3,4,1,0,2:T(8,128)(2,1)S(1)}) fusion(bf16[8,2,128,768]{2,3,1,0:T(8,128)(2,1)} %bitcast.91, bf16[8,1,64,768]{2,3,1,0:T(8,128)(2,1)S(1)} %get-tuple-element.9, bf16[8,1,64,768]{2,3,1,0:T(8,128)(2,1)} %bitcast.92), kind=kLoop, calls=%fused_computation.8 | loop fusion | flops 786432 | bytes 6291456 | tf_op jit(solution)/shard_map/stack | solution.py:85
  96.9 4.1 %pad_maximum_fusion = bf16[8,2,2,64,768]{3,4,1,0,2:T(8,128)(2,1)} fusion(bf16[8,2,1,64,768]{3,4,1,0,2:T(8,128)(2,1)S(1)} %get-tuple-element.18, bf16[8,2,1,64,768]{3,4,1,0,2:T(8,128)(2,1)S(1)} %get-tuple-element.19), kind=kLoop, calls=%fused_computation.1 | loop fusion | flops 1572864 | bytes 6291456 | tf_op jit(solution)/shard_map/stack | solution.py:85
  101.0 6.7 %copy.51 = bf16[8,2,2,64,768]{4,3,2,1,0:T(8,128)(2,1)} copy(bf16[8,2,2,64,768]{3,4,1,0,2:T(8,128)(2,1)} %pad_maximum_fusion) | data formatting | bytes 6291456 | tf_op jit(solution)/shard_map/stack | solution.py:85
  107.7 8.3 %convolution_bitcast_fusion = f32[1024,768]{0,1:T(8,128)} fusion(bf16[2048,768]{1,0:T(8,128)(2,1)} %bitcast.95, bf16[2048,1024]{1,0:T(8,128)(2,1)} %param.5), kind=kOutput, calls=%fused_computation.25 | convolution fusion | flops 3221225472 | bytes 10485760 | tf_op jit(solution)/shard_map/dot_general | solution.py:88
  116.1 7.0 %convolution_convert_fusion = bf16[2048,1024]{1,0:T(8,128)(2,1)} fusion(bf16[2048,768]{1,0:T(8,128)(2,1)} %bitcast.96, bf16[1024,768]{1,0:T(8,128)(2,1)S(1)} %copy-done), kind=kOutput, calls=%fused_computation.6 | convolution fusion | flops 3223322624 | bytes 8912896 | tf_op jit(solution)/shard_map/dot_general | solution.py:93
  123.1 61.9 %all-reduce.2.cloned.1.call-done = f32[1024,768]{0,1:T(8,128)} async-done(((f32[1024,768]{0,1:T(8,128)}), f32[1024,768]{0,1:T(8,128)}) %all-reduce.2.cloned.1.call-update) | async-done | bytes 3145744 | tf_op jit(solution)/shard_map/psum | solution.py:92
  185.0 4.2 %broadcast_multiply_fusion = f32[1024,768]{0,1:T(8,128)} fusion(f32[1024,768]{0,1:T(8,128)} %all-reduce.2.cloned.1.call-done), kind=kLoop, calls=%fused_computation.29 | loop fusion | flops 786432 | bytes 6291456 | tf_op jit(solution)/shard_map/div | solution.py:92
  189.2 3.5 %copy.52 = f32[1024,768]{1,0:T(8,128)} copy(f32[1024,768]{0,1:T(8,128)} %broadcast_multiply_fusion) | data formatting | bytes 6291456
  192.7 6.6 %reduce-scatter.2.cloned.1.call-done = bf16[512,1024]{1,0:T(8,128)(2,1)} async-done(((bf16[2048,1024]{1,0:T(8,128)(2,1)}), bf16[512,1024]{1,0:T(8,128)(2,1)}) %reduce-scatter.2.cloned.1.call-update) | async-done | bytes 1048592 | tf_op jit(solution)/shard_map/reduce_scatter | solution.py:97
  (46 shorter events, 16.8 us)
Async XLA Ops:
  8.0 1.9 copy-start
  8.0 177.0 %all-reduce.2.cloned.1.call-start = ((), (), s32[]{:S(2)}) async-start(), calls=%async_computation.2 | async-start | bytes 6291456 | tf_op jit(solution)/shard_map/psum | solution.py:92
  15.6 1.7 copy-start.5
  15.6 7.1 %copy-start.8 = (bf16[2048,256]{1,0:T(8,128)(2,1)S(1)}, bf16[2048,256]{1,0:T(8,128)(2,1)}, u32[]{:S(2)}) copy-start(bf16[2048,256]{1,0:T(8,128)(2,1)} %param.7) | copy-start | bytes 3145732
  17.2 5.5 %copy-start.10 = (f32[4,128,128]{2,1,0:T(8,128)S(1)}, f32[4,128,128]{2,1,0:T(8,128)}, u32[]{:S(2)}) copy-start(f32[4,128,128]{2,1,0:T(8,128)} %param.8) | copy-start | bytes 786436
  19.4 19.0 %collective-permute-start = (bf16[8,64,1024]{2,1,0:T(8,128)(2,1)}, bf16[8,64,1024]{2,1,0:T(8,128)(2,1)}, u32[]{:S(2)}, u32[]{:S(2)}) collective-permute-start(bf16[8,64,1024]{2,1,0:T(8,128)(2,1)} %pad_maximum_fusion.4), channel_id=1, source_target_pairs={{0,28},{4,0},{8,4},{12,8},{16,12},{20,16},{24,20},{28,24},{1,29},{... | collective-permute-start | bytes 3145736 | tf_op jit(solution)/shard_map/ppermute | solution.py:16
  30.7 7.5 %copy-start.11 = (s32[16]{0:T(128)S(1)}, s32[16]{0:T(128)}, u32[]{:S(2)}) copy-start(s32[16]{0:T(128)} %param.9) | copy-start | bytes 196
  30.7 8.6 %copy-start.9 = (bf16[8,1,64,256]{3,2,0,1:T(8,128)(2,1)S(1)}, bf16[8,1,64,256]{3,2,0,1:T(8,128)(2,1)}, u32[]{:S(2)}) copy-start(bf16[8,1,64,256]{3,2,0,1:T(8,128)(2,1)} %get-tuple-element.12) | copy-start | bytes 786436
  55.6 5.8 %copy-start.6 = (bf16[8,2,1,64,256]{3,4,1,0,2:T(8,128)(2,1)S(1)}, bf16[8,2,1,64,256]{3,4,1,0,2:T(8,128)(2,1)}, u32[]{:S(2)}) copy-start(bf16[8,2,1,64,256]{3,4,1,0,2:T(8,128)(2,1)} %copy.60) | copy-start | bytes 1572868
  61.4 4.3 %copy-start.1 = (bf16[16,64,4,3,64]{1,4,2,0,3:T(8,128)(2,1)S(1)}, bf16[16,64,4,3,64]{1,4,2,0,3:T(8,128)(2,1)}, u32[]{:S(2)}) copy-start(bf16[16,64,4,3,64]{1,4,2,0,3:T(8,128)(2,1)} %copy.39) | copy-start | bytes 4718596
  61.4 4.4 %copy-start.2 = (bf16[16,64,4,3,64]{1,4,2,0,3:T(8,128)(2,1)S(1)}, bf16[16,64,4,3,64]{1,4,2,0,3:T(8,128)(2,1)}, u32[]{:S(2)}) copy-start(bf16[16,64,4,3,64]{1,4,2,0,3:T(8,128)(2,1)} %copy.40) | copy-start | bytes 4718596
  61.4 5.6 %copy-start.4 = (f32[16,4,128,128]{2,3,1,0:T(8,128)S(1)}, f32[16,4,128,128]{2,3,1,0:T(8,128)}, u32[]{:S(2)}) copy-start(f32[16,4,128,128]{2,3,1,0:T(8,128)} %get-tuple-element.15) | copy-start | bytes 12582916
  61.4 5.8 %copy-start.7 = (bf16[8,2,64,256]{2,3,1,0:T(8,128)(2,1)S(1)}, bf16[8,2,64,256]{2,3,1,0:T(8,128)(2,1)}, u32[]{:S(2)}) copy-start(bf16[8,2,64,256]{2,3,1,0:T(8,128)(2,1)} %copy.44) | copy-start | bytes 1572868
  74.6 2.2 %copy-start.3 = (bf16[16,128,4,3,64]{1,4,3,2,0:T(8,128)(2,1)}, bf16[16,128,4,3,64]{1,4,3,2,0:T(8,128)(2,1)S(1)}, u32[]{:S(2)}) copy-start(bf16[16,128,4,3,64]{1,4,3,2,0:T(8,128)(2,1)S(1)} %copy.48) | copy-start | bytes 9437188
  79.2 12.6 %collective-permute-start.1 = (bf16[8,64,768]{2,1,0:T(8,128)(2,1)}, bf16[8,64,768]{2,1,0:T(8,128)(2,1)}, u32[]{:S(2)}, u32[]{:S(2)}) collective-permute-start(bf16[8,64,768]{2,1,0:T(8,128)(2,1)} %copy.49), channel_id=1, source_target_pairs={{0,4},{4,8},{8,12},{12,16},{16,20},{20,24},{24,28},{28,0},{1,5},{5... | collective-permute-start | bytes 2359304 | tf_op jit(solution)/shard_map/ppermute | solution.py:16
  116.0 83.3 %reduce-scatter.2.cloned.1.call-start = ((), (), s32[]{:S(2)}) async-start(), calls=%async_computation.1 | async-start | bytes 5242880 | tf_op jit(solution)/shard_map/reduce_scatter | solution.py:97
Sparse Core Ops, SparseCore 0:
  116.2 68.7 all-reduce.1
Sparse Core Ops, SparseCore 1:
  123.2 76.1 reduce-scatter.1
where the time goes:
time: 208 us; the launch traced here: 207 us
  waiting for transfers between devices  81.2 us (39%)
  local copies, waits for them, and re-layouts  55.9 us (27%)
  matrix products  35.5 us (17%)
  between operations  15.7 us (8%)
  other arithmetic  15.1 us (7%)
  starting transfers between devices  3.42 us (2%)
    psum x1, waiting for transfers between devices, shards(): weight_grad = lax.psum(local_grad, 'lon') / math.sqrt(total_tokens)  61.9 us
    concatenate x4, local copies, waits for them, and re-layouts, assemble(): return jnp.concatenate([first_part, second_part], axis=2)  24.9 us
    ppermute x2, waiting for transfers between devices, passed_along(): lax.ppermute(shard, axis, [(i, (i + by) % size) for i in range(size)])  12.6 us
    unnamed x28, local copies, waits for them, and re-layouts  9.8 us
    dot_general x1, matrix products, shards(): lax.dot_general(activations, grad_proj, (((0,), (0,)), ((), ())), preferr...  8.33 us
    dot_general x1, matrix products, shards(): lax.dot_general(grad_proj, qkv_weight, (((1,), (1,)), ((), ())), preferre...  6.99 us
    another operation x2, other arithmetic, shards(): jnp.stack([first_halves, leading], axis=2)  6.72 us
    another operation x1, local copies, waits for them, and re-layouts, shards(): jnp.stack([first_halves, leading], axis=2)  6.71 us
  transfers between devices with their start and end apart: 4, of which 3 were waited for; matrix products, arithmetic and copies ran while one was open for 15% of the time, Pallas kernels for 0%

commit v1 on v0

--- a/solution.py
+++ b/solution.py
@@ -1,19 +1,314 @@
+import functools
 import math
 
 import jax
 import jax.numpy as jnp
 from jax import lax
+from jax.experimental import pallas as pl
+from jax.experimental.pallas import tpu as pltpu
 from jax.sharding import PartitionSpec as P
 
 HEAD_DIM = 64
 WIN = 128
 WIN_ROWS = 8
 WIN_COLS = 2
+HALF = WIN // 2
+BAND = WIN_ROWS * WIN_COLS * WIN
+ROW = WIN_COLS * WIN
+VMEM_BYTES = 48 * 1024 * 1024
+
+INWARD = ((0, 1), (3, 2))
+ACROSS = ((1, 2), (2, 1))
+OUTWARD = ((1, 0), (2, 3))
+ORDER = ((3, 2, 1, 0), (3, 2, 0, 1), (0, 1, 3, 2), (0, 1, 2, 3))
 
 
 def passed_along(shard, axis, by):
     size = lax.axis_size(axis)
     return lax.ppermute(shard, axis, [(i, (i + by) % size) for i in range(size)])
+
+
+def swapped(shard, bits):
+    size = lax.axis_size("lon")
+    return lax.ppermute(shard, "lon", [(i, i ^ bits) for i in range(size)])
+
+
+def attend(proj, delta, bias_ref, counts):
+    scale = 1.0 / math.sqrt(HEAD_DIM)
+    lane = lax.broadcasted_iota(jnp.int32, (WIN, 2 * HEAD_DIM), 1)
+    low = lane < HEAD_DIM
+    key_at = lax.broadcasted_iota(jnp.int32, (2, WIN, WIN), 1)
+
+    def both(pair):
+        zero = jnp.zeros_like(pair)
+        return jnp.concatenate([jnp.where(low, pair, zero), jnp.where(low, zero, pair)], axis=0)
+
+    def rolled(x):
+        return pltpu.roll(x, HEAD_DIM, 1)
+
+    def dot(x, y, on):
+        return lax.dot_general(x, y, ((on[0], on[1]), ((), ())), preferred_element_type=jnp.float32)
+
+    pairs = proj.shape[1] // (6 * HEAD_DIM)
+    biases = [
+        jnp.stack([bias_ref[2 * p].T, bias_ref[2 * p + 1].T], axis=0) for p in range(pairs)
+    ]
+    rows = []
+    for w in range(2):
+        tiles = []
+        valid = key_at < counts[w]
+        for p in range(pairs):
+            at = [
+                proj[w * WIN : (w + 1) * WIN, p * 384 + i * 128 : p * 384 + (i + 1) * 128]
+                for i in range(3)
+            ]
+            queries = jnp.where(low, at[0], at[1]).astype(jnp.bfloat16)
+            keys = rolled(jnp.where(low, at[2], at[0])).astype(jnp.bfloat16)
+            values = jnp.where(low, at[1], at[2]).astype(jnp.bfloat16)
+            grads = delta[w * WIN : (w + 1) * WIN, p * 128 : (p + 1) * 128]
+            two_queries, two_keys, two_values, two_grads = map(both, (queries, keys, values, grads))
+            scores = dot(two_keys, queries, ((1,), (1,))).reshape(2, WIN, WIN) * scale + biases[p]
+            grad_probs = dot(two_values, grads, ((1,), (1,))).reshape(2, WIN, WIN)
+            scores = jnp.where(valid, scores, -jnp.inf)
+            weights = jnp.exp(scores - jnp.max(scores, axis=1, keepdims=True))
+            probs = weights * (1.0 / jnp.sum(weights, axis=1, keepdims=True))
+            inner = jnp.sum(probs * grad_probs, axis=1, keepdims=True)
+            grad_scores = probs * (grad_probs - inner)
+            probs_low = probs.astype(jnp.bfloat16)
+            grads_low = grad_scores.astype(jnp.bfloat16)
+            probs_side = jnp.concatenate([probs_low[0], probs_low[1]], axis=1)
+            grads_side = jnp.concatenate([grads_low[0], grads_low[1]], axis=1)
+            grad_values = dot(probs_side, two_grads, ((1,), (0,)))
+            grad_keys = rolled(dot(grads_side, two_queries, ((1,), (0,))) * scale)
+            grad_queries = dot(grads_low.reshape(2 * WIN, WIN), two_keys, ((0,), (0,))) * scale
+            tiles.append(jnp.where(low, grad_queries, grad_keys))
+            tiles.append(jnp.where(low, grad_values, grad_queries))
+            tiles.append(jnp.where(low, grad_keys, grad_values))
+        rows.append(jnp.concatenate(tiles, axis=1).astype(jnp.bfloat16))
+    return jnp.concatenate(rows, axis=0)
+
+
+def chunk_kernel(column, block_ref, counts_ref, act_ref, delta_ref, *rest):
+    if column:
+        act_far_ref, delta_far_ref, *rest = rest
+    weight_ref, bias_ref = rest[:2]
+    part_ref, grad_ref = rest[-2:]
+
+    def gathered(near_ref, far_ref):
+        pieces = []
+        for i in range(2):
+            base = i * ROW + column * WIN + HALF
+            if column:
+                pieces += [near_ref[base : base + HALF, :], far_ref[i * HALF : (i + 1) * HALF, :]]
+            else:
+                pieces += [near_ref[base : base + WIN, :]]
+        return jnp.concatenate(pieces, axis=0)
+
+    rows = gathered(act_ref, act_far_ref if column else None)
+    delta = gathered(delta_ref, delta_far_ref if column else None)
+    weight = weight_ref[...]
+    proj = jnp.dot(rows, weight, preferred_element_type=jnp.float32)
+    first = block_ref[0] * 2 * WIN_COLS + column
+    grads = attend(proj, delta, bias_ref, [counts_ref[first], counts_ref[first + WIN_COLS]])
+    grad_ref[...] = grads
+    part_ref[...] = lax.dot_general(
+        grads, weight, (((1,), (1,)), ((), ())), preferred_element_type=jnp.float32
+    ).astype(jnp.bfloat16)
+
+
+def chunk(column, block, counts, act, delta, far, weight, bias, held):
+    width, dim, delta_width = weight.shape[1], act.shape[1], delta.shape[1]
+    blocked = lambda j, block_ref, counts_ref: (block_ref[0], 0)
+    whole2 = lambda j, block_ref, counts_ref: (0, 0)
+    whole3 = lambda j, block_ref, counts_ref: (0, 0, 0)
+    operands = [act, delta]
+    specs = [pl.BlockSpec((2 * ROW, dim), blocked), pl.BlockSpec((2 * ROW, delta_width), blocked)]
+    if column:
+        operands += list(far)
+        specs += [pl.BlockSpec((WIN, dim), blocked), pl.BlockSpec((WIN, delta_width), blocked)]
+    operands += [weight, bias]
+    specs += [pl.BlockSpec(weight.shape, whole2), pl.BlockSpec(bias.shape, whole3)]
+    aliases = {}
+    if held is not None:
+        aliases = {2 + len(operands): 1}
+        operands.append(held)
+        specs.append(pl.BlockSpec(memory_space=pl.ANY))
+    tokens = 2 * WIN
+    return pl.pallas_call(
+        functools.partial(chunk_kernel, column),
+        grid_spec=pltpu.PrefetchScalarGridSpec(
+            num_scalar_prefetch=2,
+            grid=(1,),
+            in_specs=specs,
+            out_specs=[pl.BlockSpec((tokens, dim), whole2), pl.BlockSpec((tokens, width), blocked)],
+        ),
+        out_shape=[
+            jax.ShapeDtypeStruct((tokens, dim), jnp.bfloat16),
+            jax.ShapeDtypeStruct((4 * tokens, width), jnp.bfloat16),
+        ],
+        input_output_aliases=aliases,
+        compiler_params=pltpu.CompilerParams(vmem_limit_bytes=VMEM_BYTES),
+        cost_estimate=pl.CostEstimate(
+            flops=5_000_000_000, bytes_accessed=4_000_000, transcendentals=500_000
+        ),
+        name=f"chunk_{column}",
+    )(block, counts, *operands)
+
+
+def weight_kernel(core_ref, act_ref, far_ref, near_grad_ref, far_grad_ref, out_ref):
+    near, mixed = [], []
+    for r in range(WIN_ROWS):
+        near.append(act_ref[r * ROW + HALF : r * ROW + HALF + WIN, :])
+        mixed.append(act_ref[r * ROW + WIN + HALF : (r + 1) * ROW, :])
+        mixed.append(far_ref[r * HALF : (r + 1) * HALF, :])
+    over = (((0,), (0,)), ((), ()))
+    total = lax.dot_general(
+        jnp.concatenate(near, axis=0), near_grad_ref[...], over, preferred_element_type=jnp.float32
+    )
+    total += lax.dot_general(
+        jnp.concatenate(mixed, axis=0), far_grad_ref[...], over, preferred_element_type=jnp.float32
+    )
+    out_ref[...] = total.astype(out_ref.dtype)
+
+
+def weight_half(half, act, far, near_grad, far_grad, dtype):
+    dim, width = act.shape[1], near_grad.shape[1]
+    tile = 256
+    steps = dim // 2 // tile
+    column = lambda i, half_ref: (0, half_ref[0] * steps + i)
+    whole = lambda i, half_ref: (0, 0)
+    return pl.pallas_call(
+        weight_kernel,
+        grid_spec=pltpu.PrefetchScalarGridSpec(
+            num_scalar_prefetch=1,
+            grid=(steps,),
+            in_specs=[
+                pl.BlockSpec((act.shape[0], tile), column),
+                pl.BlockSpec((far.shape[0], tile), column),
+                pl.BlockSpec(near_grad.shape, whole),
+                pl.BlockSpec(far_grad.shape, whole),
+            ],
+            out_specs=pl.BlockSpec((tile, width), lambda i, half_ref: (i, 0)),
+        ),
+        out_shape=jax.ShapeDtypeStruct((dim // 2, width), dtype),
+        compiler_params=pltpu.CompilerParams(vmem_limit_bytes=VMEM_BYTES),
+        cost_estimate=pl.CostEstimate(
+            flops=2_000_000_000, bytes_accessed=8_000_000, transcendentals=0
+        ),
+        name="weight_half",
+    )(half, act, far, near_grad, far_grad)
+
+
+def split_kernel(chip_ref, mine_ref, theirs_ref, own_ref, *outs):
+    rows = own_ref.shape[0]
+    for bits in range(4):
+        at = pl.ds(pl.multiple_of((chip_ref[0] ^ bits) * rows, rows), rows)
+        total = mine_ref[at, :] + theirs_ref[at, :].astype(jnp.float32)
+        if bits:
+            outs[bits - 1][...] = total.astype(jnp.bfloat16)
+        else:
+            own_ref[...] = total
+
+
+def join_kernel(scale, chip_ref, own_ref, a_ref, b_ref, c_ref, out_ref):
+    total = own_ref[...] + a_ref[...].astype(jnp.float32)
+    total = (total + b_ref[...].astype(jnp.float32)) + c_ref[...].astype(jnp.float32)
+    out_ref[...] = (total * scale).astype(jnp.bfloat16)
+
+
+def gather_kernel(chip_ref, own_ref, a_ref, b_ref, c_ref, out_ref):
+    rows = own_ref.shape[0]
+    for bits, ref in enumerate((own_ref, a_ref, b_ref, c_ref)):
+        out_ref[pl.ds(pl.multiple_of((chip_ref[0] ^ bits) * rows, rows), rows), :] = ref[...]
+
+
+def widen_kernel(core_ref, mine_ref, theirs_ref, out_ref):
+    rows = mine_ref.shape[0]
+    for other, ref in enumerate((mine_ref, theirs_ref)):
+        at = pl.ds(pl.multiple_of((core_ref[0] ^ other) * rows, rows), rows)
+        out_ref[at, :] = ref[...].astype(jnp.float32)
+
+
+def small(kernel, out_shape, place, *operands):
+    vmem = pl.BlockSpec(memory_space=pltpu.VMEM)
+    several = isinstance(out_shape, list)
+    return pl.pallas_call(
+        kernel,
+        in_specs=[pl.BlockSpec(memory_space=pltpu.SMEM)] + [vmem] * len(operands),
+        out_specs=[vmem] * len(out_shape) if several else vmem,
+        out_shape=out_shape,
+        compiler_params=pltpu.CompilerParams(vmem_limit_bytes=VMEM_BYTES),
+    )(place, *operands)
+
+
+def summed_weight_grad(act, far, near_grad, far_grad, total_tokens):
+    dim, width = act.shape[1], near_grad.shape[1]
+    lon = lax.axis_index("lon")
+    core, chip = (lon % 2).reshape(1), (lon // 2).reshape(1)
+    outgoing = weight_half(1 - core, act, far, near_grad, far_grad, jnp.bfloat16)
+    incoming = swapped(outgoing, 1)
+    mine = weight_half(core, act, far, near_grad, far_grad, jnp.float32)
+    block = (dim // 8, width)
+    low = jax.ShapeDtypeStruct(block, jnp.bfloat16)
+    own, *sent = small(
+        split_kernel, [jax.ShapeDtypeStruct(block, jnp.float32), low, low, low], chip, mine, incoming
+    )
+    came = [swapped(part, 2 * (i + 1)) for i, part in enumerate(sent)]
+    scale = 1.0 / math.sqrt(total_tokens)
+    done = small(functools.partial(join_kernel, scale), low, chip, own, *came)
+    others = [swapped(done, 2 * (i + 1)) for i in range(3)]
+    half = jax.ShapeDtypeStruct((dim // 2, width), jnp.bfloat16)
+    gathered = small(gather_kernel, half, chip, done, *others)
+    other_half = swapped(gathered, 1)
+    return small(
+        widen_kernel, jax.ShapeDtypeStruct((dim, width), jnp.float32), core, gathered, other_half
+    )
+
+
+def add(*parts):
+    total = parts[0].astype(jnp.float32)
+    for part in parts[1:]:
+        total = total + part.astype(jnp.float32)
+    return total.astype(jnp.bfloat16)
+
+
+def line_shards(activations, qkv_weight, attn_grad, pos_bias, key_counts):
+    dim, delta_width = activations.shape[1], attn_grad.shape[1]
+    total_tokens = activations.shape[0] * lax.axis_size("lon")
+
+    def first_rows(x):
+        return x.reshape(WIN_ROWS, ROW, x.shape[1])[:, :HALF].reshape(WIN_ROWS * HALF, x.shape[1])
+
+    far = tuple(passed_along(first_rows(x), "lon", -1) for x in (activations, attn_grad))
+    order = jnp.asarray(ORDER, jnp.int32)[lax.axis_index("head")]
+    parts, held = [], []
+    for column in range(2):
+        here, grads = [], None
+        for k in range(4):
+            part, grads = chunk(
+                column, order[k : k + 1], key_counts, activations, attn_grad, far, qkv_weight, pos_bias, grads
+            )
+            here.append(part)
+        parts.append(here)
+        held.append(grads)
+
+    def hop(x, pairs):
+        return lax.ppermute(x, "head", pairs)
+
+    sums = []
+    for here in parts:
+        in_a = hop(here[0], INWARD)
+        in_b = hop(here[1], INWARD)
+        in_c = hop(here[2], INWARD)
+        over_a = hop(add(here[0], in_a), ACROSS)
+        over_b = hop(add(here[1], in_b), ACROSS)
+        out = hop(add(here[2], over_a), OUTWARD)
+        sums.append(add(here[3], in_c, over_b, out))
+    near, mixed = (x.reshape(2, WIN, dim) for x in sums)
+    back = passed_along(mixed[:, HALF:], "lon", 1)
+    input_grad = jnp.concatenate([back, near, mixed[:, :HALF]], axis=1).reshape(2 * ROW, dim)
+    weight_grad = summed_weight_grad(activations, far[0], held[0], held[1], total_tokens)
+    return (input_grad, weight_grad)
 
 
 def assemble(block_grid, far_rows):
@@ -58,16 +353,15 @@
     return jnp.stack([grad_queries, grad_keys, grad_values], axis=3).astype(jnp.bfloat16)
 
 
-def shards(activations, qkv_weight, attn_grad, pos_bias, key_counts):
+def any_shards(activations, qkv_weight, attn_grad, pos_bias, key_counts):
     heads_here = pos_bias.shape[0]
     width_all = qkv_weight.shape[1]
     delta_width = attn_grad.shape[1]
-    half_len = WIN // 2
     projected = jnp.dot(activations, qkv_weight, preferred_element_type=jnp.float32).astype(
         jnp.bfloat16
     )
-    proj_grid = projected.reshape(WIN_ROWS, WIN_COLS, 2, half_len, width_all)
-    delta_grid = attn_grad.reshape(WIN_ROWS, WIN_COLS, 2, half_len, delta_width)
+    proj_grid = projected.reshape(WIN_ROWS, WIN_COLS, 2, HALF, width_all)
+    delta_grid = attn_grad.reshape(WIN_ROWS, WIN_COLS, 2, HALF, delta_width)
     outgoing = jnp.concatenate([proj_grid[:, 0, 0], delta_grid[:, 0, 0]], axis=2)
     incoming = passed_along(outgoing, "lon", -1)
     proj_win = assemble(proj_grid, incoming[:, :, :width_all])
@@ -78,13 +372,11 @@
         pos_bias,
         key_counts,
     ).reshape(WIN_ROWS, WIN_COLS, WIN, width_all)
-    leading = gradients[:, :, :half_len]
-    trailing = gradients[:, :, half_len:]
+    leading = gradients[:, :, :HALF]
+    trailing = gradients[:, :, HALF:]
     returned = passed_along(trailing[:, WIN_COLS - 1], "lon", 1)
     first_halves = jnp.concatenate([returned[:, None], trailing[:, : WIN_COLS - 1]], axis=1)
-    grad_proj = jnp.stack([first_halves, leading], axis=2).reshape(
-        WIN_ROWS * WIN_COLS * WIN, width_all
-    )
+    grad_proj = jnp.stack([first_halves, leading], axis=2).reshape(BAND, width_all)
     local_grad = lax.dot_general(
         activations, grad_proj, (((0,), (0,)), ((), ())), preferred_element_type=jnp.float32
     )
@@ -102,8 +394,9 @@
 
 def solution(mesh):
     placed = (P("lon", None), P(None, "head"), P("lon", "head"), P("head", None, None), P("lon"))
+    on_line = mesh.shape["head"] == 4 and mesh.shape["lon"] == 8
     return jax.shard_map(
-        shards,
+        line_shards if on_line else any_shards,
         mesh=mesh,
         in_specs=placed,
         out_specs=(P(("lon", "head"), None), P(None, "head")),

time: 208 us -> 147 us (0.71)
  waiting for transfers between devices: 81.2 us -> 27.5 us
  Pallas kernels: 0 us -> 52.1 us
  local copies, waits for them, and re-layouts: 55.9 us -> 18.1 us
  starting transfers between devices: 3.42 us -> 40.5 us
  matrix products: 35.5 us -> 0 us
  between operations: 15.7 us -> 1.09 us
  other arithmetic: 15.1 us -> 6.52 us
    psum x1 -> x0, waiting for transfers between devices: 61.9 us -> none  [shards(): weight_grad = lax.psum(local_grad, 'lon') / math.sqrt(total_tokens)]
    pallas_call x0 -> x14, Pallas kernels: none -> 52.1 us  [the longest x8 41.2 us: chunk(): pl.pallas_call(functools.partial(chunk_kernel, column), grid_spec=pltpu.P...]
    ppermute x0 -> x20, starting transfers between devices: none -> 36 us  [the longest x12 28.8 us: hop(): return lax.ppermute(x, 'head', pairs)]
    dot_general x7 -> x0, matrix products: 29.8 us -> none  [the longest x1 8.33 us: shards(): lax.dot_general(activations, grad_proj, (((0,), (0,)), ((), ())), preferr...]
    ppermute x0 -> x20, waiting for transfers between devices: none -> 27.4 us  [the longest x12 21.6 us: hop(): return lax.ppermute(x, 'head', pairs)]
    concatenate x5 -> x0, local copies, waits for them, and re-layouts: 26.2 us -> none  [the longest x4 24.9 us: assemble(): return jnp.concatenate([first_part, second_part], axis=2)]
    ppermute x2 -> x3, waiting for transfers between devices: 12.6 us -> 0.01 us  [passed_along(): lax.ppermute(shard, axis, [(i, (i + by) % size) for i in range(size)])]
    another operation x2 -> x0, local copies, waits for them, and re-layouts: 7.71 us -> none  [the longest x1 6.71 us: shards(): jnp.stack([first_halves, leading], axis=2)]
  transfers between devices with their start and end apart: 4 -> 23, of which waited for: 3 -> 4; matrix products, arithmetic and copies ran while one was open for 15% -> 6% of each run, Pallas kernels for 0% -> 34%
where the time goes in v1:
time: 147 us; the launch traced here: 146 us
  Pallas kernels  52.1 us (35%)
  starting transfers between devices  40.5 us (28%)
  waiting for transfers between devices  27.5 us (19%)
  local copies, waits for them, and re-layouts  18.1 us (12%)
  other arithmetic  6.52 us (4%)
    pallas_call x8, Pallas kernels, chunk(): pl.pallas_call(functools.partial(chunk_kernel, column), grid_spec=pltpu.P...  41.2 us
    ppermute x12, starting transfers between devices, hop(): return lax.ppermute(x, 'head', pairs)  28.8 us
    ppermute x12, waiting for transfers between devices, hop(): return lax.ppermute(x, 'head', pairs)  21.6 us
    unnamed x46, local copies, waits for them, and re-layouts  13.5 us
    pallas_call x2, Pallas kernels, weight_half(): pl.pallas_call(weight_kernel, grid_spec=pltpu.PrefetchScalarGridSpec(num_...  7.49 us
    ppermute x8, starting transfers between devices, swapped(): return lax.ppermute(shard, 'lon', [(i, i ^ bits) for i in range(size)])  7.18 us
    ppermute x8, waiting for transfers between devices, swapped(): return lax.ppermute(shard, 'lon', [(i, i ^ bits) for i in range(size)])  5.81 us
    convert_element_type x8, other arithmetic, add(): return total.astype(jnp.bfloat16)  5.46 us
  transfers between devices with their start and end apart: 23, of which 4 were waited for; matrix products, arithmetic and copies ran while one was open for 6% of the time, Pallas kernels for 34%

profile of v1, /device:TPU:0, one launch (start us, length us, event | category | flops | bytes accessed | tf_op | source)
XLA Modules:
  0.0 145.8 jit_solution(12712167585413411557)
XLA Ops:
  0.6 2.3 %slice.52 = bf16[8,64,1024]{2,1,0:T(8,128)(2,1)} slice(bf16[8,256,1024]{2,1,0:T(8,128)(2,1)} %bitcast.14), slice={[0:8], [0:64], [0:1024]} | slice | bytes 2097152 | tf_op jit(solution)/shard_map/slice | solution.py:280
  3.0 3.3 %collective-permute-start = (bf16[512,1024]{1,0:T(8,128)(2,1)}, bf16[512,1024]{1,0:T(8,128)(2,1)S(1)}, u32[]{:S(2)}, u32[]{:S(2)}) collective-permute-start(bf16[512,1024]{1,0:T(8,128)(2,1)} %bitcast.2), channel_id=1, source_target_pairs={{0,28},{4,0},{8,4},{12,8},{16,12},{20,16},{24,20},{28,24},{1,29},{... | collective-permute-start | bytes 3145736 | tf_op jit(solution)/shard_map/ppermute | solution.py:28
  11.9 5.4 %chunk_0.4 = (bf16[256,1024]{1,0:T(8,128)(2,1)}, bf16[1024,768]{1,0:T(8,128)(2,1)S(1)}) custom-call(s32[1]{0:T(128)} %bitcast.7.block_ref, s32[16]{0:T(128)S(1)} %copy-done.22, bf16[2048,1024]{1,0:T(8,128)(2,1)} %act_ref.19, bf16[2048,256]{1,0:T(8,128)(2,1)S(1)} %copy-done.14, bf16[1024,768]{1,0:T(8,128)(2,1)S(1)} %copy-done.17, f32[4,128,128]{2,1,0:T(8,128)S(1)} %copy-done.19), custom_call_target="tpu_custom_call" | custom-call | flops 5000000000 | bytes 4000000 | tf_op jit(solution)/shard_map/chunk_0/pallas_call | solution.py:137
  17.4 4.3 %collective-permute-start.12 = (bf16[256,1024]{1,0:T(8,128)(2,1)}, bf16[256,1024]{1,0:T(8,128)(2,1)}, u32[]{:S(2)}, u32[]{:S(2)}) collective-permute-start(bf16[256,1024]{1,0:T(8,128)(2,1)} %get-tuple-element.35), channel_id=1, source_target_pairs={{0,1},{3,2},{4,5},{7,6},{8,9},{11,10},{12,13},{15,14},{16,17},{19,... | collective-permute-start | bytes 1572872 | tf_op jit(solution)/shard_map/ppermute | solution.py:296
  21.6 5.4 %chunk_0.5 = (bf16[256,1024]{1,0:T(8,128)(2,1)}, bf16[1024,768]{1,0:T(8,128)(2,1)S(1)}) custom-call(s32[1]{0:T(128)} %bitcast.6.block_ref, s32[16]{0:T(128)S(1)} %copy-done.22, bf16[2048,1024]{1,0:T(8,128)(2,1)} %act_ref.19, bf16[2048,256]{1,0:T(8,128)(2,1)S(1)} %copy-done.14, bf16[1024,768]{1,0:T(8,128)(2,1)S(1)} %copy-done.17, ...), custom_call_target="tpu_custom_call", output_to_operand_aliasing={{1}: (6, {})} | custom-call | flops 5000000000 | bytes 4000000 | tf_op jit(solution)/shard_map/chunk_0/pallas_call | solution.py:137
  29.6 4.5 %chunk_0.6 = (bf16[256,1024]{1,0:T(8,128)(2,1)S(1)}, bf16[1024,768]{1,0:T(8,128)(2,1)S(1)}) custom-call(s32[1]{0:T(128)} %bitcast.5.block_ref, s32[16]{0:T(128)S(1)} %copy-done.22, bf16[2048,1024]{1,0:T(8,128)(2,1)} %act_ref.19, bf16[2048,256]{1,0:T(8,128)(2,1)S(1)} %copy-done.15, bf16[1024,768]{1,0:T(8,128)(2,1)S(1)} %copy-done.18, ...), custom_call_target="tpu_custom_call", output_to_operand_aliasing={{1}: (6, {})} | custom-call | flops 5000000000 | bytes 4000000 | tf_op jit(solution)/shard_map/chunk_0/pallas_call | solution.py:137
  35.0 4.7 %chunk_0.7 = (bf16[256,1024]{1,0:T(8,128)(2,1)S(1)}, bf16[1024,768]{1,0:T(8,128)(2,1)S(1)}) custom-call(s32[1]{0:T(128)} %bitcast.block_ref, s32[16]{0:T(128)S(1)} %copy-done.22, bf16[2048,1024]{1,0:T(8,128)(2,1)} %act_ref.19, bf16[2048,256]{1,0:T(8,128)(2,1)S(1)} %copy-done.15, bf16[1024,768]{1,0:T(8,128)(2,1)S(1)} %copy-done.18, ...), custom_call_target="tpu_custom_call", output_to_operand_aliasing={{1}: (6, {})} | custom-call | flops 5000000000 | bytes 4000000 | tf_op jit(solution)/shard_map/chunk_0/pallas_call | solution.py:137
  44.3 6.0 %chunk_1.4 = (bf16[256,1024]{1,0:T(8,128)(2,1)}, bf16[1024,768]{1,0:T(8,128)(2,1)S(1)}) custom-call(s32[1]{0:T(128)} %bitcast.7.block_ref, s32[16]{0:T(128)S(1)} %copy-done.22, bf16[2048,1024]{1,0:T(8,128)(2,1)} %act_ref.19, bf16[2048,256]{1,0:T(8,128)(2,1)S(1)} %copy-done.16, bf16[512,1024]{1,0:T(8,128)(2,1)S(1)} %copy-done.1, ...), custom_call_target="tpu_custom_call" | custom-call | flops 5000000000 | bytes 4000000 | tf_op jit(solution)/shard_map/chunk_1/pallas_call | solution.py:137
  50.3 2.1 %collective-permute-start.5 = (bf16[256,1024]{1,0:T(8,128)(2,1)}, bf16[256,1024]{1,0:T(8,128)(2,1)}, u32[]{:S(2)}, u32[]{:S(2)}) collective-permute-start(bf16[256,1024]{1,0:T(8,128)(2,1)} %get-tuple-element.28), channel_id=1, source_target_pairs={{0,1},{3,2},{4,5},{7,6},{8,9},{11,10},{12,13},{15,14},{16,17},{19,... | collective-permute-start | bytes 1572872 | tf_op jit(solution)/shard_map/ppermute | solution.py:296
  53.6 5.1 %chunk_1.5 = (bf16[256,1024]{1,0:T(8,128)(2,1)S(1)}, bf16[1024,768]{1,0:T(8,128)(2,1)S(1)}) custom-call(s32[1]{0:T(128)} %bitcast.6.block_ref, s32[16]{0:T(128)S(1)} %copy-done.22, bf16[2048,1024]{1,0:T(8,128)(2,1)} %act_ref.19, bf16[2048,256]{1,0:T(8,128)(2,1)S(1)} %copy-done.16, bf16[512,1024]{1,0:T(8,128)(2,1)S(1)} %copy-done.2, ...), custom_call_target="tpu_custom_call", output_to_operand_aliasing={{1}: (8, {})} | custom-call | flops 5000000000 | bytes 4000000 | tf_op jit(solution)/shard_map/chunk_1/pallas_call | solution.py:137
  59.5 5.0 %chunk_1.6 = (bf16[256,1024]{1,0:T(8,128)(2,1)S(1)}, bf16[1024,768]{1,0:T(8,128)(2,1)S(1)}) custom-call(s32[1]{0:T(128)} %bitcast.5.block_ref, s32[16]{0:T(128)S(1)} %copy-done.22, bf16[2048,1024]{1,0:T(8,128)(2,1)} %act_ref.19, bf16[2048,256]{1,0:T(8,128)(2,1)S(1)} %copy-done.16, bf16[512,1024]{1,0:T(8,128)(2,1)S(1)} %copy-done.2, ...), custom_call_target="tpu_custom_call", output_to_operand_aliasing={{1}: (8, {})} | custom-call | flops 5000000000 | bytes 4000000 | tf_op jit(solution)/shard_map/chunk_1/pallas_call | solution.py:137
  65.3 5.1 %chunk_1.7 = (bf16[256,1024]{1,0:T(8,128)(2,1)S(1)}, bf16[1024,768]{1,0:T(8,128)(2,1)S(1)}) custom-call(s32[1]{0:T(128)} %bitcast.block_ref, s32[16]{0:T(128)S(1)} %copy-done.22, bf16[2048,1024]{1,0:T(8,128)(2,1)} %act_ref.19, bf16[2048,256]{1,0:T(8,128)(2,1)S(1)} %copy-done.16, bf16[512,1024]{1,0:T(8,128)(2,1)S(1)} %copy-done.2, ...), custom_call_target="tpu_custom_call", output_to_operand_aliasing={{1}: (8, {})} | custom-call | flops 5000000000 | bytes 4000000 | tf_op jit(solution)/shard_map/chunk_1/pallas_call | solution.py:137
  70.4 4.2 %weight_half.3 = bf16[512,768]{1,0:T(8,128)(2,1)} custom-call(s32[1]{0:T(128)S(6)} %sub.8.core_ref, bf16[2048,1024]{1,0:T(8,128)(2,1)} %act_ref.19, bf16[512,1024]{1,0:T(8,128)(2,1)S(1)} %copy-done.2, bf16[1024,768]{1,0:T(8,128)(2,1)S(1)} %get-tuple-element.36.near_grad_ref, bf16[1024,768]{1,0:T(8,128)(2,1)S(1)} %get-tuple-element.37.far_grad_ref), custom_call_target="tpu_custom_call" | custom-call | flops 2000000000 | bytes 8000000 | tf_op jit(solution)/shard_map/weight_half/pallas_call | solution.py:180
  74.7 2.1 %collective-permute-start.10 = (bf16[256,1024]{1,0:T(8,128)(2,1)}, bf16[256,1024]{1,0:T(8,128)(2,1)}, u32[]{:S(2)}, u32[]{:S(2)}) collective-permute-start(bf16[256,1024]{1,0:T(8,128)(2,1)} %get-tuple-element.34), channel_id=1, source_target_pairs={{0,1},{3,2},{4,5},{7,6},{8,9},{11,10},{12,13},{15,14},{16,17},{19,... | collective-permute-start | bytes 1572872 | tf_op jit(solution)/shard_map/ppermute | solution.py:296
  81.7 3.3 %weight_half.2.mine_ref = f32[512,768]{1,0:T(8,128)S(1)} custom-call(s32[1]{0:T(128)} %bitcast.11.core_ref, bf16[2048,1024]{1,0:T(8,128)(2,1)} %act_ref.19, bf16[512,1024]{1,0:T(8,128)(2,1)S(1)} %copy-done.3, bf16[1024,768]{1,0:T(8,128)(2,1)S(1)} %get-tuple-element.36.near_grad_ref, bf16[1024,768]{1,0:T(8,128)(2,1)S(1)} %get-tuple-element.37.far_grad_ref), custom_call_target="tpu_custom_call" | custom-call | flops 2000000000 | bytes 8000000 | tf_op jit(solution)/shard_map/weight_half/pallas_call | solution.py:180
  87.5 12.1 %collective-permute-done.3 = bf16[256,1024]{1,0:T(8,128)(2,1)S(1)} collective-permute-done((bf16[256,1024]{1,0:T(8,128)(2,1)}, bf16[256,1024]{1,0:T(8,128)(2,1)S(1)}, u32[]{:S(2)}, u32[]{:S(2)}) %collective-permute-start.3) | collective-permute-done | bytes 524320 | tf_op jit(solution)/shard_map/ppermute | solution.py:296
  101.1 7.1 %collective-permute-start.2 = (bf16[256,1024]{1,0:T(8,128)(2,1)S(1)}, bf16[256,1024]{1,0:T(8,128)(2,1)S(1)}, u32[]{:S(2)}, u32[]{:S(2)}) collective-permute-start(bf16[256,1024]{1,0:T(8,128)(2,1)S(1)} %copy-done.11), channel_id=1, source_target_pairs={{0,1},{3,2},{4,5},{7,6},{8,9},{11,10},{12,13},{15,14},{16,17},{19,... | collective-permute-start | bytes 1572872 | tf_op jit(solution)/shard_map/ppermute | solution.py:296
  113.4 1.6 %collective-permute-start.20 = (bf16[128,768]{1,0:T(8,128)(2,1)S(1)}, bf16[128,768]{1,0:T(8,128)(2,1)S(1)}, u32[]{:S(2)}, u32[]{:S(2)}) collective-permute-start(bf16[128,768]{1,0:T(8,128)(2,1)S(1)} %shard_map.78.own_ref), channel_id=1, source_target_pairs={{0,16},{4,20},{8,24},{12,28},{16,0},{20,4},{24,8},{28,12},{1,17},{... | collective-permute-start | bytes 589832 | tf_op jit(solution)/shard_map/ppermute | solution.py:33
  115.0 2.3 %collective-permute-start.21 = (bf16[128,768]{1,0:T(8,128)(2,1)S(1)}, bf16[128,768]{1,0:T(8,128)(2,1)S(1)}, u32[]{:S(2)}, u32[]{:S(2)}) collective-permute-start(bf16[128,768]{1,0:T(8,128)(2,1)S(1)} %shard_map.78.own_ref), channel_id=1, source_target_pairs={{0,24},{4,28},{8,16},{12,20},{16,8},{20,12},{24,0},{28,4},{1,25},{... | collective-permute-start | bytes 589832 | tf_op jit(solution)/shard_map/ppermute | solution.py:33
  117.6 5.8 %collective-permute-done.20.b_ref = bf16[128,768]{1,0:T(8,128)(2,1)S(1)} collective-permute-done((bf16[128,768]{1,0:T(8,128)(2,1)S(1)}, bf16[128,768]{1,0:T(8,128)(2,1)S(1)}, u32[]{:S(2)}, u32[]{:S(2)}) %collective-permute-start.20) | collective-permute-done | bytes 196640 | tf_op jit(solution)/shard_map/ppermute | solution.py:33
  123.4 6.4 %collective-permute-start.9 = (bf16[256,1024]{1,0:T(8,128)(2,1)S(1)}, bf16[256,1024]{1,0:T(8,128)(2,1)S(1)}, u32[]{:S(2)}, u32[]{:S(2)}) collective-permute-start(bf16[256,1024]{1,0:T(8,128)(2,1)S(1)} %copy-done.7), channel_id=1, source_target_pairs={{0,1},{3,2},{4,5},{7,6},{8,9},{11,10},{12,13},{15,14},{16,17},{19,... | collective-permute-start | bytes 1572872 | tf_op jit(solution)/shard_map/ppermute | solution.py:296
  132.9 4.6 %collective-permute-done.9 = bf16[256,1024]{1,0:T(8,128)(2,1)S(1)} collective-permute-done((bf16[256,1024]{1,0:T(8,128)(2,1)S(1)}, bf16[256,1024]{1,0:T(8,128)(2,1)S(1)}, u32[]{:S(2)}, u32[]{:S(2)}) %collective-permute-start.9) | collective-permute-done | bytes 524320 | tf_op jit(solution)/shard_map/ppermute | solution.py:296
  137.6 4.9 %collective-permute-done.14 = bf16[256,1024]{1,0:T(8,128)(2,1)S(1)} collective-permute-done((bf16[256,1024]{1,0:T(8,128)(2,1)S(1)}, bf16[256,1024]{1,0:T(8,128)(2,1)S(1)}, u32[]{:S(2)}, u32[]{:S(2)}) %collective-permute-start.14) | collective-permute-done | bytes 524320 | tf_op jit(solution)/shard_map/ppermute | solution.py:296
  143.9 1.9 %shard_map.80 = f32[1024,768]{1,0:T(8,128)} custom-call(s32[1]{0:T(128)} %bitcast.11.core_ref, bf16[512,768]{1,0:T(8,128)(2,1)S(1)} %shard_map.79.mine_ref, bf16[512,768]{1,0:T(8,128)(2,1)S(1)} %collective-permute-done.22.theirs_ref), custom_call_target="tpu_custom_call" | custom-call | tf_op jit(solution)/shard_map/pallas_call | solution.py:235
  (96 shorter events, 35.2 us)
Async XLA Ops:
  3.0 38.2 %collective-permute-start = (bf16[512,1024]{1,0:T(8,128)(2,1)}, bf16[512,1024]{1,0:T(8,128)(2,1)S(1)}, u32[]{:S(2)}, u32[]{:S(2)}) collective-permute-start(bf16[512,1024]{1,0:T(8,128)(2,1)} %bitcast.2), channel_id=1, source_target_pairs={{0,28},{4,0},{8,4},{12,8},{16,12},{20,16},{24,20},{28,24},{1,29},{... | collective-permute-start | bytes 3145736 | tf_op jit(solution)/shard_map/ppermute | solution.py:28
  7.3 33.2 %collective-permute-start.1 = (bf16[512,256]{1,0:T(8,128)(2,1)S(1)}, bf16[512,256]{1,0:T(8,128)(2,1)S(1)}, u32[]{:S(2)}, u32[]{:S(2)}) collective-permute-start(bf16[512,256]{1,0:T(8,128)(2,1)S(1)} %bitcast.18), channel_id=1, source_target_pairs={{0,28},{4,0},{8,4},{12,8},{16,12},{20,16},{24,20},{28,24},{1,29},{... | collective-permute-start | bytes 786440 | tf_op jit(solution)/shard_map/ppermute | solution.py:28
  17.4 62.9 %collective-permute-start.12 = (bf16[256,1024]{1,0:T(8,128)(2,1)}, bf16[256,1024]{1,0:T(8,128)(2,1)}, u32[]{:S(2)}, u32[]{:S(2)}) collective-permute-start(bf16[256,1024]{1,0:T(8,128)(2,1)} %get-tuple-element.35), channel_id=1, source_target_pairs={{0,1},{3,2},{4,5},{7,6},{8,9},{11,10},{12,13},{15,14},{16,17},{19,... | collective-permute-start | bytes 1572872 | tf_op jit(solution)/shard_map/ppermute | solution.py:296
  50.3 27.9 %collective-permute-start.5 = (bf16[256,1024]{1,0:T(8,128)(2,1)}, bf16[256,1024]{1,0:T(8,128)(2,1)}, u32[]{:S(2)}, u32[]{:S(2)}) collective-permute-start(bf16[256,1024]{1,0:T(8,128)(2,1)} %get-tuple-element.28), channel_id=1, source_target_pairs={{0,1},{3,2},{4,5},{7,6},{8,9},{11,10},{12,13},{15,14},{16,17},{19,... | collective-permute-start | bytes 1572872 | tf_op jit(solution)/shard_map/ppermute | solution.py:296
  74.7 10.4 %collective-permute-start.15 = (bf16[512,768]{1,0:T(8,128)(2,1)}, bf16[512,768]{1,0:T(8,128)(2,1)}, u32[]{:S(2)}, u32[]{:S(2)}) collective-permute-start(bf16[512,768]{1,0:T(8,128)(2,1)} %weight_half.3), channel_id=1, source_target_pairs={{0,4},{4,0},{8,12},{12,8},{16,20},{20,16},{24,28},{28,24},{1,5},{5... | collective-permute-start | bytes 2359304 | tf_op jit(solution)/shard_map/ppermute | solution.py:33
  74.7 36.1 %collective-permute-start.10 = (bf16[256,1024]{1,0:T(8,128)(2,1)}, bf16[256,1024]{1,0:T(8,128)(2,1)}, u32[]{:S(2)}, u32[]{:S(2)}) collective-permute-start(bf16[256,1024]{1,0:T(8,128)(2,1)} %get-tuple-element.34), channel_id=1, source_target_pairs={{0,1},{3,2},{4,5},{7,6},{8,9},{11,10},{12,13},{15,14},{16,17},{19,... | collective-permute-start | bytes 1572872 | tf_op jit(solution)/shard_map/ppermute | solution.py:296
  76.8 22.9 %collective-permute-start.3 = (bf16[256,1024]{1,0:T(8,128)(2,1)}, bf16[256,1024]{1,0:T(8,128)(2,1)S(1)}, u32[]{:S(2)}, u32[]{:S(2)}) collective-permute-start(bf16[256,1024]{1,0:T(8,128)(2,1)} %copy-done.12), channel_id=1, source_target_pairs={{0,1},{3,2},{4,5},{7,6},{8,9},{11,10},{12,13},{15,14},{16,17},{19,... | collective-permute-start | bytes 1572872 | tf_op jit(solution)/shard_map/ppermute | solution.py:296
  79.6 29.4 %collective-permute-start.6 = (bf16[256,1024]{1,0:T(8,128)(2,1)S(1)}, bf16[256,1024]{1,0:T(8,128)(2,1)S(1)}, u32[]{:S(2)}, u32[]{:S(2)}) collective-permute-start(bf16[256,1024]{1,0:T(8,128)(2,1)S(1)} %add_convert_fusion.6), channel_id=1, source_target_pairs={{1,2},{2,1},{5,6},{6,5},{9,10},{10,9},{13,14},{14,13},{17,18},{18,... | collective-permute-start | bytes 1572872 | tf_op jit(solution)/shard_map/ppermute | solution.py:296
  85.0 16.0 %copy-start.11 = (bf16[256,1024]{1,0:T(8,128)(2,1)S(1)}, bf16[256,1024]{1,0:T(8,128)(2,1)}, u32[]{:S(2)}) copy-start(bf16[256,1024]{1,0:T(8,128)(2,1)} %copy-done.10) | copy-start | bytes 1572868
  86.4 13.9 %collective-permute-start.16 = (bf16[128,768]{1,0:T(8,128)(2,1)S(1)}, bf16[128,768]{1,0:T(8,128)(2,1)S(1)}, u32[]{:S(2)}, u32[]{:S(2)}) collective-permute-start(bf16[128,768]{1,0:T(8,128)(2,1)S(1)} %get-tuple-element.39), channel_id=1, source_target_pairs={{0,8},{4,12},{8,0},{12,4},{16,24},{20,28},{24,16},{28,20},{1,9},{5... | collective-permute-start | bytes 589832 | tf_op jit(solution)/shard_map/ppermute | solution.py:33
  86.5 14.6 %collective-permute-start.17 = (bf16[128,768]{1,0:T(8,128)(2,1)S(1)}, bf16[128,768]{1,0:T(8,128)(2,1)S(1)}, u32[]{:S(2)}, u32[]{:S(2)}) collective-permute-start(bf16[128,768]{1,0:T(8,128)(2,1)S(1)} %get-tuple-element.40), channel_id=1, source_target_pairs={{0,16},{4,20},{8,24},{12,28},{16,0},{20,4},{24,8},{28,12},{1,17},{... | collective-permute-start | bytes 589832 | tf_op jit(solution)/shard_map/ppermute | solution.py:33
  99.6 8.6 %collective-permute-start.18 = (bf16[128,768]{1,0:T(8,128)(2,1)S(1)}, bf16[128,768]{1,0:T(8,128)(2,1)S(1)}, u32[]{:S(2)}, u32[]{:S(2)}) collective-permute-start(bf16[128,768]{1,0:T(8,128)(2,1)S(1)} %get-tuple-element.41), channel_id=1, source_target_pairs={{0,24},{4,28},{8,16},{12,20},{16,8},{20,12},{24,0},{28,4},{1,25},{... | collective-permute-start | bytes 589832 | tf_op jit(solution)/shard_map/ppermute | solution.py:33
  100.3 13.1 %collective-permute-start.13 = (bf16[256,1024]{1,0:T(8,128)(2,1)S(1)}, bf16[256,1024]{1,0:T(8,128)(2,1)S(1)}, u32[]{:S(2)}, u32[]{:S(2)}) collective-permute-start(bf16[256,1024]{1,0:T(8,128)(2,1)S(1)} %add_convert_fusion.2), channel_id=1, source_target_pairs={{1,2},{2,1},{5,6},{6,5},{9,10},{10,9},{13,14},{14,13},{17,18},{18,... | collective-permute-start | bytes 1572872 | tf_op jit(solution)/shard_map/ppermute | solution.py:296
  101.1 29.5 %collective-permute-start.2 = (bf16[256,1024]{1,0:T(8,128)(2,1)S(1)}, bf16[256,1024]{1,0:T(8,128)(2,1)S(1)}, u32[]{:S(2)}, u32[]{:S(2)}) collective-permute-start(bf16[256,1024]{1,0:T(8,128)(2,1)S(1)} %copy-done.11), channel_id=1, source_target_pairs={{0,1},{3,2},{4,5},{7,6},{8,9},{11,10},{12,13},{15,14},{16,17},{19,... | collective-permute-start | bytes 1572872 | tf_op jit(solution)/shard_map/ppermute | solution.py:296
  108.2 23.7 %collective-permute-start.4 = (bf16[256,1024]{1,0:T(8,128)(2,1)S(1)}, bf16[256,1024]{1,0:T(8,128)(2,1)S(1)}, u32[]{:S(2)}, u32[]{:S(2)}) collective-permute-start(bf16[256,1024]{1,0:T(8,128)(2,1)S(1)} %add_convert_fusion.7), channel_id=1, source_target_pairs={{1,2},{2,1},{5,6},{6,5},{9,10},{10,9},{13,14},{14,13},{17,18},{18,... | collective-permute-start | bytes 1572872 | tf_op jit(solution)/shard_map/ppermute | solution.py:296
  109.0 6.0 %collective-permute-start.19 = (bf16[128,768]{1,0:T(8,128)(2,1)S(1)}, bf16[128,768]{1,0:T(8,128)(2,1)S(1)}, u32[]{:S(2)}, u32[]{:S(2)}) collective-permute-start(bf16[128,768]{1,0:T(8,128)(2,1)S(1)} %shard_map.78.own_ref), channel_id=1, source_target_pairs={{0,8},{4,12},{8,0},{12,4},{16,24},{20,28},{24,16},{28,20},{1,9},{5... | collective-permute-start | bytes 589832 | tf_op jit(solution)/shard_map/ppermute | solution.py:33
  110.7 21.3 %collective-permute-start.7 = (bf16[256,1024]{1,0:T(8,128)(2,1)S(1)}, bf16[256,1024]{1,0:T(8,128)(2,1)S(1)}, u32[]{:S(2)}, u32[]{:S(2)}) collective-permute-start(bf16[256,1024]{1,0:T(8,128)(2,1)S(1)} %add_convert_fusion.5), channel_id=1, source_target_pairs={{1,0},{2,3},{5,4},{6,7},{9,8},{10,11},{13,12},{14,15},{17,16},{18,... | collective-permute-start | bytes 1572872 | tf_op jit(solution)/shard_map/ppermute | solution.py:296
  113.4 9.9 %collective-permute-start.20 = (bf16[128,768]{1,0:T(8,128)(2,1)S(1)}, bf16[128,768]{1,0:T(8,128)(2,1)S(1)}, u32[]{:S(2)}, u32[]{:S(2)}) collective-permute-start(bf16[128,768]{1,0:T(8,128)(2,1)S(1)} %shard_map.78.own_ref), channel_id=1, source_target_pairs={{0,16},{4,20},{8,24},{12,28},{16,0},{20,4},{24,8},{28,12},{1,17},{... | collective-permute-start | bytes 589832 | tf_op jit(solution)/shard_map/ppermute | solution.py:33
  115.0 14.8 %collective-permute-start.21 = (bf16[128,768]{1,0:T(8,128)(2,1)S(1)}, bf16[128,768]{1,0:T(8,128)(2,1)S(1)}, u32[]{:S(2)}, u32[]{:S(2)}) collective-permute-start(bf16[128,768]{1,0:T(8,128)(2,1)S(1)} %shard_map.78.own_ref), channel_id=1, source_target_pairs={{0,24},{4,28},{8,16},{12,20},{16,8},{20,12},{24,0},{28,4},{1,25},{... | collective-permute-start | bytes 589832 | tf_op jit(solution)/shard_map/ppermute | solution.py:33
  123.4 14.2 %collective-permute-start.9 = (bf16[256,1024]{1,0:T(8,128)(2,1)S(1)}, bf16[256,1024]{1,0:T(8,128)(2,1)S(1)}, u32[]{:S(2)}, u32[]{:S(2)}) collective-permute-start(bf16[256,1024]{1,0:T(8,128)(2,1)S(1)} %copy-done.7), channel_id=1, source_target_pairs={{0,1},{3,2},{4,5},{7,6},{8,9},{11,10},{12,13},{15,14},{16,17},{19,... | collective-permute-start | bytes 1572872 | tf_op jit(solution)/shard_map/ppermute | solution.py:296
  129.8 7.8 %collective-permute-start.11 = (bf16[256,1024]{1,0:T(8,128)(2,1)S(1)}, bf16[256,1024]{1,0:T(8,128)(2,1)S(1)}, u32[]{:S(2)}, u32[]{:S(2)}) collective-permute-start(bf16[256,1024]{1,0:T(8,128)(2,1)S(1)} %add_convert_fusion.3), channel_id=1, source_target_pairs={{1,2},{2,1},{5,6},{6,5},{9,10},{10,9},{13,14},{14,13},{17,18},{18,... | collective-permute-start | bytes 1572872 | tf_op jit(solution)/shard_map/ppermute | solution.py:296
  130.6 11.9 %collective-permute-start.14 = (bf16[256,1024]{1,0:T(8,128)(2,1)S(1)}, bf16[256,1024]{1,0:T(8,128)(2,1)S(1)}, u32[]{:S(2)}, u32[]{:S(2)}) collective-permute-start(bf16[256,1024]{1,0:T(8,128)(2,1)S(1)} %add_convert_fusion.1), channel_id=1, source_target_pairs={{1,0},{2,3},{5,4},{6,7},{9,8},{10,11},{13,12},{14,15},{17,16},{18,... | collective-permute-start | bytes 1572872 | tf_op jit(solution)/shard_map/ppermute | solution.py:296
  131.9 12.0 %collective-permute-start.22 = (bf16[512,768]{1,0:T(8,128)(2,1)S(1)}, bf16[512,768]{1,0:T(8,128)(2,1)S(1)}, u32[]{:S(2)}, u32[]{:S(2)}) collective-permute-start(bf16[512,768]{1,0:T(8,128)(2,1)S(1)} %shard_map.79.mine_ref), channel_id=1, source_target_pairs={{0,4},{4,0},{8,12},{12,8},{16,20},{20,16},{24,28},{28,24},{1,5},{5... | collective-permute-start | bytes 2359304 | tf_op jit(solution)/shard_map/ppermute | solution.py:33
  132.4 10.4 %collective-permute-start.8 = (bf16[2,64,1024]{2,1,0:T(8,128)(2,1)S(1)}, bf16[2,64,1024]{2,1,0:T(8,128)(2,1)S(1)}, u32[]{:S(2)}, u32[]{:S(2)}) collective-permute-start(bf16[2,64,1024]{2,1,0:T(8,128)(2,1)S(1)} %get-tuple-element.42), channel_id=1, source_target_pairs={{0,4},{4,8},{8,12},{12,16},{16,20},{20,24},{24,28},{28,0},{1,5},{5... | collective-permute-start | bytes 786440 | tf_op jit(solution)/shard_map/ppermute | solution.py:28
  (22 other events, 95.8 us)

commit v2 on v0

--- a/solution.py
+++ b/solution.py
@@ -1,19 +1,412 @@
+import functools
 import math
 
 import jax
 import jax.numpy as jnp
 from jax import lax
+from jax.experimental import pallas as pl
+from jax.experimental.pallas import tpu as pltpu
 from jax.sharding import PartitionSpec as P
 
 HEAD_DIM = 64
 WIN = 128
 WIN_ROWS = 8
 WIN_COLS = 2
+HALF = WIN // 2
+BAND = WIN_ROWS * WIN_COLS * WIN
+ROW = WIN_COLS * WIN
+VMEM_BYTES = 48 * 1024 * 1024
+
+BESIDE, ACROSS = 1, 3
+ORDER = (2, 1, 3, 0)
+SMALL_COST = pl.CostEstimate(flops=1_000_000, bytes_accessed=100_000, transcendentals=0)
 
 
 def passed_along(shard, axis, by):
     size = lax.axis_size(axis)
     return lax.ppermute(shard, axis, [(i, (i + by) % size) for i in range(size)])
+
+
+def swapped(shard, bits):
+    size = lax.axis_size("lon")
+    return lax.ppermute(shard, "lon", [(i, i ^ bits) for i in range(size)])
+
+
+def attend(proj, delta, bias_ref, counts):
+    scale = 1.0 / math.sqrt(HEAD_DIM)
+    lane = lax.broadcasted_iota(jnp.int32, (WIN, 2 * HEAD_DIM), 1)
+    low = lane < HEAD_DIM
+    key_at = lax.broadcasted_iota(jnp.int32, (2, WIN, WIN), 1)
+
+    def both(pair):
+        zero = jnp.zeros_like(pair)
+        return jnp.concatenate([jnp.where(low, pair, zero), jnp.where(low, zero, pair)], axis=0)
+
+    def rolled(x):
+        return pltpu.roll(x, HEAD_DIM, 1)
+
+    def dot(x, y, on):
+        return lax.dot_general(x, y, ((on[0], on[1]), ((), ())), preferred_element_type=jnp.float32)
+
+    pairs = proj.shape[1] // (6 * HEAD_DIM)
+    biases = [bias_ref[2 * p : 2 * p + 2] for p in range(pairs)]
+    rows = []
+    for w in range(2):
+        tiles = []
+        valid = key_at < counts[w]
+        for p in range(pairs):
+            at = [
+                proj[w * WIN : (w + 1) * WIN, p * 384 + i * 128 : p * 384 + (i + 1) * 128]
+                for i in range(3)
+            ]
+            queries = jnp.where(low, at[0], at[1]).astype(jnp.bfloat16)
+            keys = rolled(jnp.where(low, at[2], at[0])).astype(jnp.bfloat16)
+            values = jnp.where(low, at[1], at[2]).astype(jnp.bfloat16)
+            grads = delta[w * WIN : (w + 1) * WIN, p * 128 : (p + 1) * 128]
+            two_queries, two_keys, two_values, two_grads = map(both, (queries, keys, values, grads))
+            scores = dot(two_keys, queries, ((1,), (1,))).reshape(2, WIN, WIN) * scale + biases[p]
+            grad_probs = dot(two_values, grads, ((1,), (1,))).reshape(2, WIN, WIN)
+            scores = jnp.where(valid, scores, -jnp.inf)
+            weights = jnp.exp(scores - jnp.max(scores, axis=1, keepdims=True))
+            probs = weights * (1.0 / jnp.sum(weights, axis=1, keepdims=True))
+            inner = jnp.sum(probs * grad_probs, axis=1, keepdims=True)
+            grad_scores = probs * (grad_probs - inner)
+            probs_low = probs.astype(jnp.bfloat16)
+            grads_low = grad_scores.astype(jnp.bfloat16)
+            probs_side = jnp.concatenate([probs_low[0], probs_low[1]], axis=1)
+            grads_side = jnp.concatenate([grads_low[0], grads_low[1]], axis=1)
+            grad_values = dot(probs_side, two_grads, ((1,), (0,)))
+            grad_keys = rolled(dot(grads_side, two_queries, ((1,), (0,))) * scale)
+            grad_queries = dot(grads_low.reshape(2 * WIN, WIN), two_keys, ((0,), (0,))) * scale
+            tiles.append(jnp.where(low, grad_queries, grad_keys))
+            tiles.append(jnp.where(low, grad_values, grad_queries))
+            tiles.append(jnp.where(low, grad_keys, grad_values))
+        rows.append(jnp.concatenate(tiles, axis=1).astype(jnp.bfloat16))
+    return jnp.concatenate(rows, axis=0)
+
+
+def block_at(head, step):
+    bits = jnp.where(step == 3, ORDER[3], ORDER[2])
+    bits = jnp.where(step == 1, ORDER[1], bits)
+    return head ^ jnp.where(step == 0, ORDER[0], bits)
+
+
+def pack_kernel(act_ref, delta_ref, out_ref, sems):
+    dim = act_ref.shape[2]
+    copies = [
+        pltpu.make_async_copy(
+            act_ref.at[:, pl.ds(0, HALF), :], out_ref.at[:, :, pl.ds(0, dim)], sems.at[0]
+        ),
+        pltpu.make_async_copy(
+            delta_ref.at[:, pl.ds(0, HALF), :],
+            out_ref.at[:, :, pl.ds(dim, delta_ref.shape[2])],
+            sems.at[1],
+        ),
+    ]
+    for copy in copies:
+        copy.start()
+    for copy in copies:
+        copy.wait()
+
+
+def first_rows(act, delta):
+    dim, delta_width = act.shape[1], delta.shape[1]
+    anywhere = pl.BlockSpec(memory_space=pl.ANY)
+    return pl.pallas_call(
+        pack_kernel,
+        in_specs=[anywhere, anywhere],
+        out_specs=pl.BlockSpec(memory_space=pltpu.VMEM),
+        out_shape=jax.ShapeDtypeStruct((WIN_ROWS, HALF, dim + delta_width), act.dtype),
+        scratch_shapes=[pltpu.SemaphoreType.DMA((2,))],
+        name="first_rows",
+    )(act.reshape(WIN_ROWS, ROW, dim), delta.reshape(WIN_ROWS, ROW, delta_width))
+
+
+def turned_biases(bias_ref, turned_ref):
+    @pl.when(pl.program_id(0) == 0)
+    def _():
+        for h in range(bias_ref.shape[0]):
+            turned_ref[h] = bias_ref[h].T
+
+
+def counts_of(counts_ref, block, column):
+    first = block * 2 * WIN_COLS + column
+    return [counts_ref[first], counts_ref[first + WIN_COLS]]
+
+
+def part_of(grads, weight):
+    return lax.dot_general(
+        grads, weight, (((1,), (1,)), ((), ())), preferred_element_type=jnp.float32
+    ).astype(jnp.bfloat16)
+
+
+def near_kernel(
+    start, steps, head_ref, counts_ref, act_ref, delta_ref, weight_ref, bias_ref, *rest
+):
+    outs, turned_ref = rest[-2 - steps : -1], rest[-1]
+    turned_biases(bias_ref, turned_ref)
+    at = [slice(i * ROW + HALF, i * ROW + HALF + WIN) for i in range(2)]
+    rows = jnp.concatenate([act_ref[s, :] for s in at], axis=0)
+    delta = jnp.concatenate([delta_ref[s, :] for s in at], axis=0)
+    weight = weight_ref[...]
+    proj = jnp.dot(rows, weight, preferred_element_type=jnp.float32)
+    step = pl.program_id(0)
+    counts = counts_of(counts_ref, block_at(head_ref[0], step + start), 0)
+    grads = attend(proj, delta, turned_ref, counts)
+    outs[-1][...] = grads
+    part = part_of(grads, weight)
+    for i in range(steps):
+
+        @pl.when(step == i)
+        def _():
+            outs[i][...] = part
+
+
+def near_windows(start, steps, head, counts, act, delta, weight, bias, held):
+    width, dim, delta_width = weight.shape[1], act.shape[1], delta.shape[1]
+    blocked = lambda j, head_ref, counts_ref: (block_at(head_ref[0], j + start), 0)
+    whole2 = lambda j, head_ref, counts_ref: (0, 0)
+    whole3 = lambda j, head_ref, counts_ref: (0, 0, 0)
+    tokens = 2 * WIN
+    operands = [act, delta, weight, bias]
+    specs = [
+        pl.BlockSpec((2 * ROW, dim), blocked),
+        pl.BlockSpec((2 * ROW, delta_width), blocked),
+        pl.BlockSpec(weight.shape, whole2),
+        pl.BlockSpec(bias.shape, whole3),
+    ]
+    aliases = {}
+    if held is not None:
+        aliases = {2 + len(operands): steps}
+        operands.append(held)
+        specs.append(pl.BlockSpec(memory_space=pl.ANY))
+    part = jax.ShapeDtypeStruct((tokens, dim), jnp.bfloat16)
+    return pl.pallas_call(
+        functools.partial(near_kernel, start, steps),
+        grid_spec=pltpu.PrefetchScalarGridSpec(
+            num_scalar_prefetch=2,
+            grid=(steps,),
+            in_specs=specs,
+            out_specs=[pl.BlockSpec((tokens, dim), whole2)] * steps
+            + [pl.BlockSpec((tokens, width), lambda j, head_ref, counts_ref: (j + start, 0))],
+            scratch_shapes=[pltpu.VMEM(bias.shape, bias.dtype)],
+        ),
+        out_shape=[part] * steps + [jax.ShapeDtypeStruct((4 * tokens, width), jnp.bfloat16)],
+        input_output_aliases=aliases,
+        compiler_params=pltpu.CompilerParams(vmem_limit_bytes=VMEM_BYTES),
+        cost_estimate=SMALL_COST,
+        name="near_windows",
+    )(head, counts, *operands)
+
+
+def far_kernel(
+    head_ref, core_ref, counts_ref, act_ref, delta_ref, far_ref, weight_ref, bias_ref, held_ref, *rest
+):
+    outs, send_ref, keep_ref, turned_ref, total_ref = rest[:8], *rest[8:]
+    turned_biases(bias_ref, turned_ref)
+    dim, delta_width = act_ref.shape[1], delta_ref.shape[1]
+    step = pl.program_id(0)
+
+    def mixed(near_ref, low, high):
+        pieces = []
+        for i in range(2):
+            pieces.append(near_ref[(i + 1) * ROW - HALF : (i + 1) * ROW, :])
+            pieces.append(far_ref[i * HALF : (i + 1) * HALF, low:high])
+        return jnp.concatenate(pieces, axis=0)
+
+    rows = mixed(act_ref, 0, dim)
+    delta = mixed(delta_ref, dim, dim + delta_width)
+    weight = weight_ref[...]
+    proj = jnp.dot(rows, weight, preferred_element_type=jnp.float32)
+    counts = counts_of(counts_ref, block_at(head_ref[0], step), 1)
+    grads = attend(proj, delta, turned_ref, counts)
+    part = part_of(grads, weight)
+    for i in range(4):
+
+        @pl.when(step == i)
+        def _():
+            for w in range(2):
+                base = w * WIN
+                outs[2 * i][w * HALF : (w + 1) * HALF, :] = part[base + HALF : base + WIN]
+                outs[2 * i + 1][w * HALF : (w + 1) * HALF, :] = part[base : base + HALF]
+
+    near_rows = [act_ref[i * ROW + HALF : i * ROW + HALF + WIN, :] for i in range(2)]
+    all_rows = jnp.concatenate(near_rows + [rows], axis=0)
+    all_grads = jnp.concatenate([held_ref[...], grads], axis=0)
+    product = lax.dot_general(
+        all_rows, all_grads, (((0,), (0,)), ((), ())), preferred_element_type=jnp.float32
+    )
+
+    @pl.when(step == 0)
+    def _():
+        total_ref[...] = product
+
+    @pl.when(step > 0)
+    def _():
+        total_ref[...] += product
+
+    @pl.when(step == 3)
+    def _():
+        half = dim // 2
+        core = core_ref[0]
+        keep_ref[...] = total_ref[pl.ds(pl.multiple_of(core * half, half), half), :]
+        send_ref[...] = total_ref[pl.ds(pl.multiple_of((1 - core) * half, half), half), :].astype(
+            jnp.bfloat16
+        )
+
+
+def far_windows(head, core, counts, act, delta, far, weight, bias, held):
+    width, dim, delta_width = weight.shape[1], act.shape[1], delta.shape[1]
+    blocked = lambda j, head_ref, core_ref, counts_ref: (block_at(head_ref[0], j), 0)
+    whole2 = lambda j, head_ref, core_ref, counts_ref: (0, 0)
+    whole3 = lambda j, head_ref, core_ref, counts_ref: (0, 0, 0)
+    part = jax.ShapeDtypeStruct((WIN, dim), jnp.bfloat16)
+    return pl.pallas_call(
+        far_kernel,
+        grid_spec=pltpu.PrefetchScalarGridSpec(
+            num_scalar_prefetch=3,
+            grid=(4,),
+            in_specs=[
+                pl.BlockSpec((2 * ROW, dim), blocked),
+                pl.BlockSpec((2 * ROW, delta_width), blocked),
+                pl.BlockSpec((WIN, dim + delta_width), blocked),
+                pl.BlockSpec(weight.shape, whole2),
+                pl.BlockSpec(bias.shape, whole3),
+                pl.BlockSpec((2 * WIN, width), lambda j, head_ref, core_ref, counts_ref: (j, 0)),
+            ],
+            out_specs=[pl.BlockSpec((WIN, dim), whole2)] * 8
+            + [pl.BlockSpec((dim // 2, width), whole2)] * 2,
+            scratch_shapes=[
+                pltpu.VMEM(bias.shape, bias.dtype),
+                pltpu.VMEM((dim, width), jnp.float32),
+            ],
+        ),
+        out_shape=[part] * 8
+        + [
+            jax.ShapeDtypeStruct((dim // 2, width), jnp.bfloat16),
+            jax.ShapeDtypeStruct((dim // 2, width), jnp.float32),
+        ],
+        compiler_params=pltpu.CompilerParams(vmem_limit_bytes=VMEM_BYTES),
+        cost_estimate=SMALL_COST,
+        name="far_windows",
+    )(head, core, counts, act, delta, far, weight, bias, held)
+
+
+def split_kernel(chip_ref, mine_ref, theirs_ref, own_ref, *outs):
+    rows = own_ref.shape[0]
+    for bits in range(4):
+        at = pl.ds(pl.multiple_of((chip_ref[0] ^ bits) * rows, rows), rows)
+        total = mine_ref[at, :] + theirs_ref[at, :].astype(jnp.float32)
+        if bits:
+            outs[bits - 1][...] = total.astype(jnp.bfloat16)
+        else:
+            own_ref[...] = total
+
+
+def join_kernel(scale, chip_ref, own_ref, a_ref, b_ref, c_ref, out_ref):
+    total = own_ref[...] + a_ref[...].astype(jnp.float32)
+    total = (total + b_ref[...].astype(jnp.float32)) + c_ref[...].astype(jnp.float32)
+    out_ref[...] = (total * scale).astype(jnp.bfloat16)
+
+
+def gather_kernel(chip_ref, own_ref, a_ref, b_ref, c_ref, out_ref):
+    rows = own_ref.shape[0]
+    for bits, ref in enumerate((own_ref, a_ref, b_ref, c_ref)):
+        out_ref[pl.ds(pl.multiple_of((chip_ref[0] ^ bits) * rows, rows), rows), :] = ref[...]
+
+
+def widen_kernel(core_ref, mine_ref, theirs_ref, out_ref):
+    rows = mine_ref.shape[0]
+    for other, ref in enumerate((mine_ref, theirs_ref)):
+        at = pl.ds(pl.multiple_of((core_ref[0] ^ other) * rows, rows), rows)
+        out_ref[at, :] = ref[...].astype(jnp.float32)
+
+
+def small(kernel, out_shape, place, *operands):
+    vmem = pl.BlockSpec(memory_space=pltpu.VMEM)
+    several = isinstance(out_shape, list)
+    return pl.pallas_call(
+        kernel,
+        in_specs=[pl.BlockSpec(memory_space=pltpu.SMEM)] + [vmem] * len(operands),
+        out_specs=[vmem] * len(out_shape) if several else vmem,
+        out_shape=out_shape,
+        compiler_params=pltpu.CompilerParams(vmem_limit_bytes=VMEM_BYTES),
+    )(place, *operands)
+
+
+def after(x, *others):
+    return lax.optimization_barrier((x, *others))[0]
+
+
+def add(*parts):
+    total = parts[0].astype(jnp.float32)
+    for part in parts[1:]:
+        total = total + part.astype(jnp.float32)
+    return total.astype(jnp.bfloat16)
+
+
+def line_shards(activations, qkv_weight, attn_grad, pos_bias, key_counts):
+    dim, width = qkv_weight.shape
+    total_tokens = activations.shape[0] * lax.axis_size("lon")
+    head = lax.axis_index("head").reshape(1)
+    lon = lax.axis_index("lon")
+    core, chip = (lon % 2).reshape(1), (lon // 2).reshape(1)
+
+    arrived = []
+
+    def hop(x, bits):
+        x = x if len(arrived) < 2 else after(x, arrived[-2])
+        pairs = [(i, i ^ bits) for i in range(lax.axis_size("head"))]
+        arrived.append(lax.ppermute(x, "head", pairs))
+        return arrived[-1]
+
+    far = passed_along(first_rows(activations, attn_grad), "lon", -1)
+    here = (activations, attn_grad, qkv_weight, pos_bias)
+    first, held = near_windows(0, 1, head, key_counts, *here, None)
+    in_near = [hop(first, BESIDE)]
+    *near, held = near_windows(1, 3, head, key_counts, *here, held)
+    in_near.append(hop(near[0], BESIDE))
+    in_near.append(hop(add(near[1], in_near[0]), ACROSS))
+    far = after(far, in_near[0]).reshape(WIN_ROWS * HALF, far.shape[2])
+    *parts, outgoing, mine = far_windows(
+        head, core, key_counts, activations, attn_grad, far, qkv_weight, pos_bias, held
+    )
+    nexts, this = parts[0::2], parts[1::2]
+    in_next, in_this = [hop(nexts[0], BESIDE)], [hop(this[0], BESIDE)]
+    in_next.append(hop(add(nexts[2], in_next[0]), ACROSS))
+    in_next.append(hop(nexts[1], BESIDE))
+    in_this.append(hop(add(this[2], in_this[0]), ACROSS))
+    in_this.append(hop(this[1], BESIDE))
+    near_sum = add(near[2], *in_near[1:])
+    back = passed_along(add(nexts[3], *in_next[1:]), "lon", 1)
+    this_sum = add(this[3], *in_this[1:])
+    input_grad = jnp.concatenate(
+        [x.reshape(2, -1, dim) for x in (back, near_sum, this_sum)], axis=1
+    ).reshape(2 * ROW, dim)
+
+    incoming = swapped(outgoing, 1)
+    block = (dim // 8, width)
+    low = jax.ShapeDtypeStruct(block, jnp.bfloat16)
+    own, *sent = small(
+        split_kernel,
+        [jax.ShapeDtypeStruct(block, jnp.float32), low, low, low],
+        after(chip, *in_near[1:]),
+        mine,
+        incoming,
+    )
+    came = [swapped(part, 2 * (i + 1)) for i, part in enumerate(sent)]
+    scale = 1.0 / math.sqrt(total_tokens)
+    done = small(
+        functools.partial(join_kernel, scale), low, after(chip, in_next[0], in_this[0]), own, *came
+    )
+    others = [swapped(done, 2 * (i + 1)) for i in range(3)]
+    half = jax.ShapeDtypeStruct((dim // 2, width), jnp.bfloat16)
+    gathered = small(gather_kernel, half, after(chip, *in_next[1:], in_this[1]), done, *others)
+    other_half = swapped(gathered, 1)
+    weight_grad = small(
+        widen_kernel, jax.ShapeDtypeStruct((dim, width), jnp.float32), core, gathered, other_half
+    )
+    return (input_grad, weight_grad)
 
 
 def assemble(block_grid, far_rows):
@@ -58,16 +451,15 @@
     return jnp.stack([grad_queries, grad_keys, grad_values], axis=3).astype(jnp.bfloat16)
 
 
-def shards(activations, qkv_weight, attn_grad, pos_bias, key_counts):
+def any_shards(activations, qkv_weight, attn_grad, pos_bias, key_counts):
     heads_here = pos_bias.shape[0]
     width_all = qkv_weight.shape[1]
     delta_width = attn_grad.shape[1]
-    half_len = WIN // 2
     projected = jnp.dot(activations, qkv_weight, preferred_element_type=jnp.float32).astype(
         jnp.bfloat16
     )
-    proj_grid = projected.reshape(WIN_ROWS, WIN_COLS, 2, half_len, width_all)
-    delta_grid = attn_grad.reshape(WIN_ROWS, WIN_COLS, 2, half_len, delta_width)
+    proj_grid = projected.reshape(WIN_ROWS, WIN_COLS, 2, HALF, width_all)
+    delta_grid = attn_grad.reshape(WIN_ROWS, WIN_COLS, 2, HALF, delta_width)
     outgoing = jnp.concatenate([proj_grid[:, 0, 0], delta_grid[:, 0, 0]], axis=2)
     incoming = passed_along(outgoing, "lon", -1)
     proj_win = assemble(proj_grid, incoming[:, :, :width_all])
@@ -78,13 +470,11 @@
         pos_bias,
         key_counts,
     ).reshape(WIN_ROWS, WIN_COLS, WIN, width_all)
-    leading = gradients[:, :, :half_len]
-    trailing = gradients[:, :, half_len:]
+    leading = gradients[:, :, :HALF]
+    trailing = gradients[:, :, HALF:]
     returned = passed_along(trailing[:, WIN_COLS - 1], "lon", 1)
     first_halves = jnp.concatenate([returned[:, None], trailing[:, : WIN_COLS - 1]], axis=1)
-    grad_proj = jnp.stack([first_halves, leading], axis=2).reshape(
-        WIN_ROWS * WIN_COLS * WIN, width_all
-    )
+    grad_proj = jnp.stack([first_halves, leading], axis=2).reshape(BAND, width_all)
     local_grad = lax.dot_general(
         activations, grad_proj, (((0,), (0,)), ((), ())), preferred_element_type=jnp.float32
     )
@@ -102,8 +492,9 @@
 
 def solution(mesh):
     placed = (P("lon", None), P(None, "head"), P("lon", "head"), P("head", None, None), P("lon"))
+    on_line = mesh.shape["head"] == 4 and mesh.shape["lon"] == 8
     return jax.shard_map(
-        shards,
+        line_shards if on_line else any_shards,
         mesh=mesh,
         in_specs=placed,
         out_specs=(P(("lon", "head"), None), P(None, "head")),

time: 208 us -> 102 us (0.49)
  local copies, waits for them, and re-layouts: 55.9 us -> 3.36 us
  waiting for transfers between devices: 81.2 us -> 30.7 us
  Pallas kernels: 0 us -> 37.6 us
  matrix products: 35.5 us -> 0 us
  starting transfers between devices: 3.42 us -> 22.3 us
  between operations: 15.7 us -> 0.79 us
  other arithmetic: 15.1 us -> 6.57 us
    psum x1 -> x0, waiting for transfers between devices: 61.9 us -> none  [shards(): weight_grad = lax.psum(local_grad, 'lon') / math.sqrt(total_tokens)]
    pallas_call x0 -> x8, Pallas kernels: none -> 37.6 us  [the longest x1 18.6 us: far_windows(): pl.pallas_call(far_kernel, grid_spec=pltpu.PrefetchScalarGridSpec(num_sca...]
    dot_general x7 -> x0, matrix products: 29.8 us -> none  [the longest x1 8.33 us: shards(): lax.dot_general(activations, grad_proj, (((0,), (0,)), ((), ())), preferr...]
    concatenate x5 -> x0, local copies, waits for them, and re-layouts: 26.2 us -> none  [the longest x4 24.9 us: assemble(): return jnp.concatenate([first_part, second_part], axis=2)]
    ppermute x0 -> x17, waiting for transfers between devices: none -> 26.1 us  [the longest x9 15.4 us: hop(): arrived.append(lax.ppermute(x, 'head', pairs))]
    ppermute x0 -> x17, starting transfers between devices: none -> 18.4 us  [the longest x9 11.2 us: hop(): arrived.append(lax.ppermute(x, 'head', pairs))]
    ppermute x2, waiting for transfers between devices: 12.6 us -> 4.59 us  [passed_along(): lax.ppermute(shard, axis, [(i, (i + by) % size) for i in range(size)])]
    another operation x2 -> x0, local copies, waits for them, and re-layouts: 7.71 us -> none  [the longest x1 6.71 us: shards(): jnp.stack([first_halves, leading], axis=2)]
  transfers between devices with their start and end apart: 4 -> 19, of which waited for: 3 -> 9; matrix products, arithmetic and copies ran while one was open for 15% -> 6% of each run, Pallas kernels for 0% -> 33%
where the time goes in v2:
time: 102 us; the launch traced here: 101 us
  Pallas kernels  37.6 us (37%)
  waiting for transfers between devices  30.7 us (30%)
  starting transfers between devices  22.3 us (22%)
  other arithmetic  6.57 us (6%)
  local copies, waits for them, and re-layouts  3.36 us (3%)
    pallas_call x1, Pallas kernels, far_windows(): pl.pallas_call(far_kernel, grid_spec=pltpu.PrefetchScalarGridSpec(num_sca...  18.6 us
    ppermute x9, waiting for transfers between devices, hop(): arrived.append(lax.ppermute(x, 'head', pairs))  15.4 us
    pallas_call x2, Pallas kernels, near_windows(): pl.pallas_call(functools.partial(near_kernel, start, steps), grid_spec=pl...  14.3 us
    ppermute x9, starting transfers between devices, hop(): arrived.append(lax.ppermute(x, 'head', pairs))  11.2 us
    ppermute x8, waiting for transfers between devices, swapped(): return lax.ppermute(shard, 'lon', [(i, i ^ bits) for i in range(size)])  10.7 us
    ppermute x8, starting transfers between devices, swapped(): return lax.ppermute(shard, 'lon', [(i, i ^ bits) for i in range(size)])  7.18 us
    convert_element_type x6, other arithmetic, add(): return total.astype(jnp.bfloat16)  5.53 us
    ppermute x2, waiting for transfers between devices, passed_along(): lax.ppermute(shard, axis, [(i, (i + by) % size) for i in range(size)])  4.59 us
  transfers between devices with their start and end apart: 19, of which 9 were waited for; matrix products, arithmetic and copies ran while one was open for 6% of the time, Pallas kernels for 33%

profile of v2, /device:TPU:0, one launch (start us, length us, event | category | flops | bytes accessed | tf_op | source)
XLA Modules:
  0.0 101.4 jit_solution(6022646604295818589)
XLA Ops:
  0.7 2.5 %first_rows.1 = bf16[8,64,1280]{2,1,0:T(8,128)(2,1)} custom-call(bf16[8,256,1024]{2,1,0:T(8,128)(2,1)} %bitcast.11, bf16[8,256,256]{2,1,0:T(8,128)(2,1)} %bitcast.10), custom_call_target="tpu_custom_call" | custom-call | tf_op jit(solution)/shard_map/first_rows/pallas_call | solution.py:115
  3.2 3.4 %collective-permute-start = (bf16[8,64,1280]{2,1,0:T(8,128)(2,1)}, bf16[8,64,1280]{2,1,0:T(8,128)(2,1)}, u32[]{:S(2)}, u32[]{:S(2)}) collective-permute-start(bf16[8,64,1280]{2,1,0:T(8,128)(2,1)} %first_rows.1), channel_id=1, source_target_pairs={{0,28},{4,0},{8,4},{12,8},{16,12},{20,16},{24,20},{28,24},{1,29},{... | collective-permute-start | bytes 3932168 | tf_op jit(solution)/shard_map/ppermute | solution.py:27
  6.6 4.8 %near_windows.2 = (bf16[256,1024]{1,0:T(8,128)(2,1)}, bf16[1024,768]{1,0:T(8,128)(2,1)S(1)}) custom-call(s32[1]{0:T(128)} %bitcast.head_ref, s32[16]{0:T(128)S(1)} %copy-done.7, bf16[2048,1024]{1,0:T(8,128)(2,1)} %act_ref.5, bf16[2048,256]{1,0:T(8,128)(2,1)S(1)} %copy-done, bf16[1024,768]{1,0:T(8,128)(2,1)S(1)} %copy-done.1, f32[4,128,128]{2,1,0:T(8,128)S(1)} %copy-done.3), custom_call_target="tpu_custom_call" | custom-call | flops 1000000 | bytes 100000 | tf_op jit(solution)/shard_map/near_windows/pallas_call | solution.py:184
  11.4 1.6 %collective-permute-start.1 = (bf16[256,1024]{1,0:T(8,128)(2,1)}, bf16[256,1024]{1,0:T(8,128)(2,1)}, u32[]{:S(2)}, u32[]{:S(2)}) collective-permute-start(bf16[256,1024]{1,0:T(8,128)(2,1)} %get-tuple-element.33), channel_id=1, source_target_pairs={{0,1},{1,0},{2,3},{3,2},{4,5},{5,4},{6,7},{7,6},{8,9},{9,8},{10,11... | collective-permute-start | bytes 1572872 | tf_op jit(solution)/shard_map/ppermute | solution.py:360
  13.0 9.6 %near_windows.3 = (bf16[256,1024]{1,0:T(8,128)(2,1)}, bf16[256,1024]{1,0:T(8,128)(2,1)S(1)}, bf16[256,1024]{1,0:T(8,128)(2,1)S(1)}, bf16[1024,768]{1,0:T(8,128)(2,1)S(1)}) custom-call(s32[1]{0:T(128)} %bitcast.head_ref, s32[16]{0:T(128)S(1)} %copy-done.7, bf16[2048,1024]{1,0:T(8,128)(2,1)} %act_ref.5, ...), custom_call_target="tpu_custom_call", output_to_operand_aliasing={{3}: (6, {})} | custom-call | flops 1000000 | bytes 100000 | tf_op jit(solution)/shard_map/near_windows/pallas_call | solution.py:184
  22.5 1.1 %copy-done.2 = bf16[1024,768]{1,0:T(8,128)(2,1)} copy-done((bf16[1024,768]{1,0:T(8,128)(2,1)}, bf16[1024,768]{1,0:T(8,128)(2,1)S(1)}, u32[]{:S(2)}) %copy-start.2) | copy-done | bytes 1572888
  24.9 2.0 %add_convert_fusion.1 = bf16[256,1024]{1,0:T(8,128)(2,1)} fusion(bf16[256,1024]{1,0:T(8,128)(2,1)} %collective-permute-done.1, bf16[256,1024]{1,0:T(8,128)(2,1)S(1)} %get-tuple-element.45), kind=kLoop, calls=%fused_computation.2 | loop fusion | flops 1048576 | bytes 1572864 | tf_op jit(solution)/shard_map/convert_element_type | solution.py:345
  26.9 3.6 %collective-permute-start.5 = (bf16[256,1024]{1,0:T(8,128)(2,1)}, bf16[256,1024]{1,0:T(8,128)(2,1)}, u32[]{:S(2)}, u32[]{:S(2)}) collective-permute-start(bf16[256,1024]{1,0:T(8,128)(2,1)} %add_convert_fusion.1), channel_id=1, source_target_pairs={{0,3},{1,2},{2,1},{3,0},{4,7},{5,6},{6,5},{7,4},{8,11},{9,10},{10,... | collective-permute-start | bytes 1572872 | tf_op jit(solution)/shard_map/ppermute | solution.py:360
  30.6 18.6 %far_windows.1 = (bf16[128,1024]{1,0:T(8,128)(2,1)S(1)}, bf16[128,1024]{1,0:T(8,128)(2,1)}, bf16[128,1024]{1,0:T(8,128)(2,1)S(1)}, bf16[128,1024]{1,0:T(8,128)(2...) custom-call(s32[1]{0:T(128)} %bitcast.head_ref, ...), custom_call_target="tpu_custom_call" | custom-call | flops 1000000 | bytes 100000 | tf_op jit(solution)/shard_map/far_windows/pallas_call | solution.py:264
  50.3 1.6 %collective-permute-start.6 = (bf16[128,1024]{1,0:T(8,128)(2,1)}, bf16[128,1024]{1,0:T(8,128)(2,1)S(1)}, u32[]{:S(2)}, u32[]{:S(2)}) collective-permute-start(bf16[128,1024]{1,0:T(8,128)(2,1)} %get-tuple-element.47), channel_id=1, source_target_pairs={{0,1},{1,0},{2,3},{3,2},{4,5},{5,4},{6,7},{7,6},{8,9},{9,8},{10,11... | collective-permute-start | bytes 786440 | tf_op jit(solution)/shard_map/ppermute | solution.py:360
  52.0 6.4 %collective-permute-done.3 = bf16[128,1024]{1,0:T(8,128)(2,1)S(1)} collective-permute-done((bf16[128,1024]{1,0:T(8,128)(2,1)S(1)}, bf16[128,1024]{1,0:T(8,128)(2,1)S(1)}, u32[]{:S(2)}, u32[]{:S(2)}) %collective-permute-start.3) | collective-permute-done | bytes 262176 | tf_op jit(solution)/shard_map/ppermute | solution.py:360
  59.1 1.6 %collective-permute-start.4 = (bf16[128,1024]{1,0:T(8,128)(2,1)}, bf16[128,1024]{1,0:T(8,128)(2,1)}, u32[]{:S(2)}, u32[]{:S(2)}) collective-permute-start(bf16[128,1024]{1,0:T(8,128)(2,1)} %add_convert_fusion.5), channel_id=1, source_target_pairs={{0,3},{1,2},{2,1},{3,0},{4,7},{5,6},{6,5},{7,4},{8,11},{9,10},{10,... | collective-permute-start | bytes 786440 | tf_op jit(solution)/shard_map/ppermute | solution.py:360
  60.7 7.9 %collective-permute-done.6 = bf16[128,1024]{1,0:T(8,128)(2,1)S(1)} collective-permute-done((bf16[128,1024]{1,0:T(8,128)(2,1)}, bf16[128,1024]{1,0:T(8,128)(2,1)S(1)}, u32[]{:S(2)}, u32[]{:S(2)}) %collective-permute-start.6) | collective-permute-done | bytes 262176 | tf_op jit(solution)/shard_map/ppermute | solution.py:360
  68.6 1.4 %copy-done.4 = f32[512,768]{1,0:T(8,128)S(1)} copy-done((f32[512,768]{1,0:T(8,128)S(1)}, f32[512,768]{1,0:T(8,128)}, u32[]{:S(2)}) %copy-start.4) | copy-done | bytes 1572888
  71.0 1.5 %collective-permute-start.13 = (bf16[128,768]{1,0:T(8,128)(2,1)S(1)}, bf16[128,768]{1,0:T(8,128)(2,1)S(1)}, u32[]{:S(2)}, u32[]{:S(2)}) collective-permute-start(bf16[128,768]{1,0:T(8,128)(2,1)S(1)} %get-tuple-element.62), channel_id=1, source_target_pairs={{0,16},{4,20},{8,24},{12,28},{16,0},{20,4},{24,8},{28,12},{1,17},{... | collective-permute-start | bytes 589832 | tf_op jit(solution)/shard_map/ppermute | solution.py:32
  72.5 1.2 %collective-permute-start.14 = (bf16[128,768]{1,0:T(8,128)(2,1)S(1)}, bf16[128,768]{1,0:T(8,128)(2,1)S(1)}, u32[]{:S(2)}, u32[]{:S(2)}) collective-permute-start(bf16[128,768]{1,0:T(8,128)(2,1)S(1)} %get-tuple-element.63), channel_id=1, source_target_pairs={{0,24},{4,28},{8,16},{12,20},{16,8},{20,12},{24,0},{28,4},{1,25},{... | collective-permute-start | bytes 589832 | tf_op jit(solution)/shard_map/ppermute | solution.py:32
  73.9 2.0 %collective-permute-done.12.a_ref = bf16[128,768]{1,0:T(8,128)(2,1)S(1)} collective-permute-done((bf16[128,768]{1,0:T(8,128)(2,1)S(1)}, bf16[128,768]{1,0:T(8,128)(2,1)S(1)}, u32[]{:S(2)}, u32[]{:S(2)}) %collective-permute-start.12) | collective-permute-done | bytes 196640 | tf_op jit(solution)/shard_map/ppermute | solution.py:32
  75.9 5.5 %collective-permute-done.13.b_ref = bf16[128,768]{1,0:T(8,128)(2,1)S(1)} collective-permute-done((bf16[128,768]{1,0:T(8,128)(2,1)S(1)}, bf16[128,768]{1,0:T(8,128)(2,1)S(1)}, u32[]{:S(2)}, u32[]{:S(2)}) %collective-permute-start.13) | collective-permute-done | bytes 196640 | tf_op jit(solution)/shard_map/ppermute | solution.py:32
  81.5 1.6 %collective-permute-start.17 = (bf16[128,768]{1,0:T(8,128)(2,1)S(1)}, bf16[128,768]{1,0:T(8,128)(2,1)S(1)}, u32[]{:S(2)}, u32[]{:S(2)}) collective-permute-start(bf16[128,768]{1,0:T(8,128)(2,1)S(1)} %shard_map.69.own_ref), channel_id=1, source_target_pairs={{0,24},{4,28},{8,16},{12,20},{16,8},{20,12},{24,0},{28,4},{1,25},{... | collective-permute-start | bytes 589832 | tf_op jit(solution)/shard_map/ppermute | solution.py:32
  85.1 2.2 %collective-permute-start.10 = (bf16[128,1024]{1,0:T(8,128)(2,1)S(1)}, bf16[128,1024]{1,0:T(8,128)(2,1)S(1)}, u32[]{:S(2)}, u32[]{:S(2)}) collective-permute-start(bf16[128,1024]{1,0:T(8,128)(2,1)S(1)} %get-tuple-element.54), channel_id=1, source_target_pairs={{0,1},{1,0},{2,3},{3,2},{4,5},{5,4},{6,7},{7,6},{8,9},{9,8},{10,11... | collective-permute-start | bytes 786440 | tf_op jit(solution)/shard_map/ppermute | solution.py:360
  88.2 2.0 %collective-permute-done.16.b_ref = bf16[128,768]{1,0:T(8,128)(2,1)S(1)} collective-permute-done((bf16[128,768]{1,0:T(8,128)(2,1)S(1)}, bf16[128,768]{1,0:T(8,128)(2,1)S(1)}, u32[]{:S(2)}, u32[]{:S(2)}) %collective-permute-start.16) | collective-permute-done | bytes 196640 | tf_op jit(solution)/shard_map/ppermute | solution.py:32
  92.3 1.5 %add_convert_fusion = bf16[256,1024]{1,0:T(8,128)(2,1)S(1)} fusion(bf16[256,1024]{1,0:T(8,128)(2,1)} %collective-permute-done.5, bf16[256,1024]{1,0:T(8,128)(2,1)} %collective-permute-done.2, bf16[256,1024]{1,0:T(8,128)(2,1)S(1)} %copy-done.6), kind=kLoop, calls=%fused_computation.1 | loop fusion | flops 1572864 | bytes 2097152 | tf_op jit(solution)/shard_map/convert_element_type | solution.py:345
  93.9 4.6 %collective-permute-done.8 = bf16[128,1024]{1,0:T(8,128)(2,1)S(1)} collective-permute-done((bf16[128,1024]{1,0:T(8,128)(2,1)S(1)}, bf16[128,1024]{1,0:T(8,128)(2,1)S(1)}, u32[]{:S(2)}, u32[]{:S(2)}) %collective-permute-start.8) | collective-permute-done | bytes 262176 | tf_op jit(solution)/shard_map/ppermute | solution.py:27
  99.5 1.9 %shard_map.71 = f32[1024,768]{1,0:T(8,128)} custom-call(s32[1]{0:T(128)} %bitcast.1.core_ref, bf16[512,768]{1,0:T(8,128)(2,1)S(1)} %shard_map.70.mine_ref, bf16[512,768]{1,0:T(8,128)(2,1)S(1)} %collective-permute-done.18.theirs_ref), custom_call_target="tpu_custom_call" | custom-call | tf_op jit(solution)/shard_map/pallas_call | solution.py:328
  (45 shorter events, 10.5 us)
Async XLA Ops:
  0.6 6.0 %copy-start = (bf16[2048,256]{1,0:T(8,128)(2,1)S(1)}, bf16[2048,256]{1,0:T(8,128)(2,1)}, u32[]{:S(2)}) copy-start(bf16[2048,256]{1,0:T(8,128)(2,1)} %delta_ref.5) | copy-start | bytes 3145732
  0.6 6.0 %copy-start.1 = (bf16[1024,768]{1,0:T(8,128)(2,1)S(1)}, bf16[1024,768]{1,0:T(8,128)(2,1)}, u32[]{:S(2)}) copy-start(bf16[1024,768]{1,0:T(8,128)(2,1)} %weight_ref.5) | copy-start | bytes 4718596
  0.7 6.0 %copy-start.3 = (f32[4,128,128]{2,1,0:T(8,128)S(1)}, f32[4,128,128]{2,1,0:T(8,128)}, u32[]{:S(2)}) copy-start(f32[4,128,128]{2,1,0:T(8,128)} %bias_ref.5) | copy-start | bytes 786436
  0.7 5.9 %copy-start.7 = (s32[16]{0:T(128)S(1)}, s32[16]{0:T(128)}, u32[]{:S(2)}) copy-start(s32[16]{0:T(128)} %counts_ref.5) | copy-start | bytes 196
  3.2 27.3 %collective-permute-start = (bf16[8,64,1280]{2,1,0:T(8,128)(2,1)}, bf16[8,64,1280]{2,1,0:T(8,128)(2,1)}, u32[]{:S(2)}, u32[]{:S(2)}) collective-permute-start(bf16[8,64,1280]{2,1,0:T(8,128)(2,1)} %first_rows.1), channel_id=1, source_target_pairs={{0,28},{4,0},{8,4},{12,8},{16,12},{20,16},{24,20},{28,24},{1,29},{... | collective-permute-start | bytes 3932168 | tf_op jit(solution)/shard_map/ppermute | solution.py:27
  11.4 13.5 %collective-permute-start.1 = (bf16[256,1024]{1,0:T(8,128)(2,1)}, bf16[256,1024]{1,0:T(8,128)(2,1)}, u32[]{:S(2)}, u32[]{:S(2)}) collective-permute-start(bf16[256,1024]{1,0:T(8,128)(2,1)} %get-tuple-element.33), channel_id=1, source_target_pairs={{0,1},{1,0},{2,3},{3,2},{4,5},{5,4},{6,7},{7,6},{8,9},{9,8},{10,11... | collective-permute-start | bytes 1572872 | tf_op jit(solution)/shard_map/ppermute | solution.py:360
  24.5 24.7 %collective-permute-start.2 = (bf16[256,1024]{1,0:T(8,128)(2,1)}, bf16[256,1024]{1,0:T(8,128)(2,1)}, u32[]{:S(2)}, u32[]{:S(2)}) collective-permute-start(bf16[256,1024]{1,0:T(8,128)(2,1)} %get-tuple-element.40), channel_id=1, source_target_pairs={{0,1},{1,0},{2,3},{3,2},{4,5},{5,4},{6,7},{7,6},{8,9},{9,8},{10,11... | collective-permute-start | bytes 1572872 | tf_op jit(solution)/shard_map/ppermute | solution.py:360
  26.9 23.4 %collective-permute-start.5 = (bf16[256,1024]{1,0:T(8,128)(2,1)}, bf16[256,1024]{1,0:T(8,128)(2,1)}, u32[]{:S(2)}, u32[]{:S(2)}) collective-permute-start(bf16[256,1024]{1,0:T(8,128)(2,1)} %add_convert_fusion.1), channel_id=1, source_target_pairs={{0,3},{1,2},{2,1},{3,0},{4,7},{5,6},{6,5},{7,4},{8,11},{9,10},{10,... | collective-permute-start | bytes 1572872 | tf_op jit(solution)/shard_map/ppermute | solution.py:360
  49.2 19.5 %collective-permute-start.11 = (bf16[512,768]{1,0:T(8,128)(2,1)S(1)}, bf16[512,768]{1,0:T(8,128)(2,1)S(1)}, u32[]{:S(2)}, u32[]{:S(2)}) collective-permute-start(bf16[512,768]{1,0:T(8,128)(2,1)S(1)} %get-tuple-element.59), channel_id=1, source_target_pairs={{0,4},{4,0},{8,12},{12,8},{16,20},{20,16},{24,28},{28,24},{1,5},{5... | collective-permute-start | bytes 2359304 | tf_op jit(solution)/shard_map/ppermute | solution.py:32
  49.2 9.2 %collective-permute-start.3 = (bf16[128,1024]{1,0:T(8,128)(2,1)S(1)}, bf16[128,1024]{1,0:T(8,128)(2,1)S(1)}, u32[]{:S(2)}, u32[]{:S(2)}) collective-permute-start(bf16[128,1024]{1,0:T(8,128)(2,1)S(1)} %get-tuple-element.41), channel_id=1, source_target_pairs={{0,1},{1,0},{2,3},{3,2},{4,5},{5,4},{6,7},{7,6},{8,9},{9,8},{10,11... | collective-permute-start | bytes 786440 | tf_op jit(solution)/shard_map/ppermute | solution.py:360
  50.3 18.3 %collective-permute-start.6 = (bf16[128,1024]{1,0:T(8,128)(2,1)}, bf16[128,1024]{1,0:T(8,128)(2,1)S(1)}, u32[]{:S(2)}, u32[]{:S(2)}) collective-permute-start(bf16[128,1024]{1,0:T(8,128)(2,1)} %get-tuple-element.47), channel_id=1, source_target_pairs={{0,1},{1,0},{2,3},{3,2},{4,5},{5,4},{6,7},{7,6},{8,9},{9,8},{10,11... | collective-permute-start | bytes 786440 | tf_op jit(solution)/shard_map/ppermute | solution.py:360
  59.1 14.7 %collective-permute-start.4 = (bf16[128,1024]{1,0:T(8,128)(2,1)}, bf16[128,1024]{1,0:T(8,128)(2,1)}, u32[]{:S(2)}, u32[]{:S(2)}) collective-permute-start(bf16[128,1024]{1,0:T(8,128)(2,1)} %add_convert_fusion.5), channel_id=1, source_target_pairs={{0,3},{1,2},{2,1},{3,0},{4,7},{5,6},{6,5},{7,4},{8,11},{9,10},{10,... | collective-permute-start | bytes 786440 | tf_op jit(solution)/shard_map/ppermute | solution.py:360
  68.6 16.4 %collective-permute-start.7 = (bf16[128,1024]{1,0:T(8,128)(2,1)S(1)}, bf16[128,1024]{1,0:T(8,128)(2,1)S(1)}, u32[]{:S(2)}, u32[]{:S(2)}) collective-permute-start(bf16[128,1024]{1,0:T(8,128)(2,1)S(1)} %get-tuple-element.48), channel_id=1, source_target_pairs={{0,1},{1,0},{2,3},{3,2},{4,5},{5,4},{6,7},{7,6},{8,9},{9,8},{10,11... | collective-permute-start | bytes 786440 | tf_op jit(solution)/shard_map/ppermute | solution.py:360
  70.2 5.7 %collective-permute-start.12 = (bf16[128,768]{1,0:T(8,128)(2,1)S(1)}, bf16[128,768]{1,0:T(8,128)(2,1)S(1)}, u32[]{:S(2)}, u32[]{:S(2)}) collective-permute-start(bf16[128,768]{1,0:T(8,128)(2,1)S(1)} %get-tuple-element.61), channel_id=1, source_target_pairs={{0,8},{4,12},{8,0},{12,4},{16,24},{20,28},{24,16},{28,20},{1,9},{5... | collective-permute-start | bytes 589832 | tf_op jit(solution)/shard_map/ppermute | solution.py:32
  71.0 10.4 %collective-permute-start.13 = (bf16[128,768]{1,0:T(8,128)(2,1)S(1)}, bf16[128,768]{1,0:T(8,128)(2,1)S(1)}, u32[]{:S(2)}, u32[]{:S(2)}) collective-permute-start(bf16[128,768]{1,0:T(8,128)(2,1)S(1)} %get-tuple-element.62), channel_id=1, source_target_pairs={{0,16},{4,20},{8,24},{12,28},{16,0},{20,4},{24,8},{28,12},{1,17},{... | collective-permute-start | bytes 589832 | tf_op jit(solution)/shard_map/ppermute | solution.py:32
  72.5 8.9 %collective-permute-start.14 = (bf16[128,768]{1,0:T(8,128)(2,1)S(1)}, bf16[128,768]{1,0:T(8,128)(2,1)S(1)}, u32[]{:S(2)}, u32[]{:S(2)}) collective-permute-start(bf16[128,768]{1,0:T(8,128)(2,1)S(1)} %get-tuple-element.63), channel_id=1, source_target_pairs={{0,24},{4,28},{8,16},{12,20},{16,8},{20,12},{24,0},{28,4},{1,25},{... | collective-permute-start | bytes 589832 | tf_op jit(solution)/shard_map/ppermute | solution.py:32
  73.8 18.5 %copy-start.6 = (bf16[256,1024]{1,0:T(8,128)(2,1)S(1)}, bf16[256,1024]{1,0:T(8,128)(2,1)}, u32[]{:S(2)}) copy-start(bf16[256,1024]{1,0:T(8,128)(2,1)} %copy-done.5) | copy-start | bytes 1572868
  73.8 13.4 %collective-permute-start.9 = (bf16[128,1024]{1,0:T(8,128)(2,1)S(1)}, bf16[128,1024]{1,0:T(8,128)(2,1)S(1)}, u32[]{:S(2)}, u32[]{:S(2)}) collective-permute-start(bf16[128,1024]{1,0:T(8,128)(2,1)S(1)} %add_convert_fusion.3), channel_id=1, source_target_pairs={{0,3},{1,2},{2,1},{3,0},{4,7},{5,6},{6,5},{7,4},{8,11},{9,10},{10,... | collective-permute-start | bytes 786440 | tf_op jit(solution)/shard_map/ppermute | solution.py:360
  81.5 6.7 %collective-permute-start.17 = (bf16[128,768]{1,0:T(8,128)(2,1)S(1)}, bf16[128,768]{1,0:T(8,128)(2,1)S(1)}, u32[]{:S(2)}, u32[]{:S(2)}) collective-permute-start(bf16[128,768]{1,0:T(8,128)(2,1)S(1)} %shard_map.69.own_ref), channel_id=1, source_target_pairs={{0,24},{4,28},{8,16},{12,20},{16,8},{20,12},{24,0},{28,4},{1,25},{... | collective-permute-start | bytes 589832 | tf_op jit(solution)/shard_map/ppermute | solution.py:32
  83.1 7.2 %collective-permute-start.16 = (bf16[128,768]{1,0:T(8,128)(2,1)S(1)}, bf16[128,768]{1,0:T(8,128)(2,1)S(1)}, u32[]{:S(2)}, u32[]{:S(2)}) collective-permute-start(bf16[128,768]{1,0:T(8,128)(2,1)S(1)} %shard_map.69.own_ref), channel_id=1, source_target_pairs={{0,16},{4,20},{8,24},{12,28},{16,0},{20,4},{24,8},{28,12},{1,17},{... | collective-permute-start | bytes 589832 | tf_op jit(solution)/shard_map/ppermute | solution.py:32
  84.1 6.4 %collective-permute-start.15 = (bf16[128,768]{1,0:T(8,128)(2,1)S(1)}, bf16[128,768]{1,0:T(8,128)(2,1)S(1)}, u32[]{:S(2)}, u32[]{:S(2)}) collective-permute-start(bf16[128,768]{1,0:T(8,128)(2,1)S(1)} %shard_map.69.own_ref), channel_id=1, source_target_pairs={{0,8},{4,12},{8,0},{12,4},{16,24},{20,28},{24,16},{28,20},{1,9},{5... | collective-permute-start | bytes 589832 | tf_op jit(solution)/shard_map/ppermute | solution.py:32
  85.1 8.7 %collective-permute-start.10 = (bf16[128,1024]{1,0:T(8,128)(2,1)S(1)}, bf16[128,1024]{1,0:T(8,128)(2,1)S(1)}, u32[]{:S(2)}, u32[]{:S(2)}) collective-permute-start(bf16[128,1024]{1,0:T(8,128)(2,1)S(1)} %get-tuple-element.54), channel_id=1, source_target_pairs={{0,1},{1,0},{2,3},{3,2},{4,5},{5,4},{6,7},{7,6},{8,9},{9,8},{10,11... | collective-permute-start | bytes 786440 | tf_op jit(solution)/shard_map/ppermute | solution.py:360
  90.6 9.0 %collective-permute-start.18 = (bf16[512,768]{1,0:T(8,128)(2,1)S(1)}, bf16[512,768]{1,0:T(8,128)(2,1)S(1)}, u32[]{:S(2)}, u32[]{:S(2)}) collective-permute-start(bf16[512,768]{1,0:T(8,128)(2,1)S(1)} %shard_map.70.mine_ref), channel_id=1, source_target_pairs={{0,4},{4,0},{8,12},{12,8},{16,20},{20,16},{24,28},{28,24},{1,5},{5... | collective-permute-start | bytes 2359304 | tf_op jit(solution)/shard_map/ppermute | solution.py:32
  91.7 6.7 %collective-permute-start.8 = (bf16[128,1024]{1,0:T(8,128)(2,1)S(1)}, bf16[128,1024]{1,0:T(8,128)(2,1)S(1)}, u32[]{:S(2)}, u32[]{:S(2)}) collective-permute-start(bf16[128,1024]{1,0:T(8,128)(2,1)S(1)} %add_convert_fusion.4), channel_id=1, source_target_pairs={{0,4},{4,8},{8,12},{12,16},{16,20},{20,24},{24,28},{28,0},{1,5},{5... | collective-permute-start | bytes 786440 | tf_op jit(solution)/shard_map/ppermute | solution.py:27
  (3 other events, 3.3 us)

commit v3 on v2

--- a/solution.py
+++ b/solution.py
@@ -16,10 +16,12 @@
 BAND = WIN_ROWS * WIN_COLS * WIN
 ROW = WIN_COLS * WIN
 VMEM_BYTES = 48 * 1024 * 1024
-
-BESIDE, ACROSS = 1, 3
-ORDER = (2, 1, 3, 0)
-SMALL_COST = pl.CostEstimate(flops=1_000_000, bytes_accessed=100_000, transcendentals=0)
+LARGE_VMEM_BYTES = 58 * 1024 * 1024
+SMALL_VMEM_BYTES = 12 * 1024 * 1024
+
+BESIDE, ACROSS = 1, 2
+ORDER = (3, 1, 2, 0)
+COST = pl.CostEstimate(flops=1_000_000, bytes_accessed=100_000, transcendentals=0)
 
 
 def passed_along(shard, axis, by):
@@ -34,9 +36,8 @@
 
 def attend(proj, delta, bias_ref, counts):
     scale = 1.0 / math.sqrt(HEAD_DIM)
-    lane = lax.broadcasted_iota(jnp.int32, (WIN, 2 * HEAD_DIM), 1)
-    low = lane < HEAD_DIM
-    key_at = lax.broadcasted_iota(jnp.int32, (2, WIN, WIN), 1)
+    low = lax.broadcasted_iota(jnp.int32, (WIN, 2 * HEAD_DIM), 1) < HEAD_DIM
+    key_at = lax.broadcasted_iota(jnp.int32, (WIN, WIN), 0)
 
     def both(pair):
         zero = jnp.zeros_like(pair)
@@ -46,43 +47,50 @@
         return pltpu.roll(x, HEAD_DIM, 1)
 
     def dot(x, y, on):
-        return lax.dot_general(x, y, ((on[0], on[1]), ((), ())), preferred_element_type=jnp.float32)
+        return lax.dot_general(x, y, (on, ((), ())), preferred_element_type=jnp.float32)
 
     pairs = proj.shape[1] // (6 * HEAD_DIM)
-    biases = [bias_ref[2 * p : 2 * p + 2] for p in range(pairs)]
-    rows = []
-    for w in range(2):
-        tiles = []
-        valid = key_at < counts[w]
-        for p in range(pairs):
-            at = [
-                proj[w * WIN : (w + 1) * WIN, p * 384 + i * 128 : p * 384 + (i + 1) * 128]
-                for i in range(3)
+    units = [(w, p) for w in range(2) for p in range(pairs)]
+    scored, softened, tiles = [], [], []
+    for w, p in units:
+        rows = slice(w * WIN, (w + 1) * WIN)
+        at = [proj[rows, (3 * p + i) * WIN : (3 * p + i + 1) * WIN] for i in range(3)]
+        queries = jnp.where(low, at[0], at[1]).astype(jnp.bfloat16)
+        keys = rolled(jnp.where(low, at[2], at[0])).astype(jnp.bfloat16)
+        values = jnp.where(low, at[1], at[2]).astype(jnp.bfloat16)
+        grads = delta[rows, p * WIN : (p + 1) * WIN]
+        two_keys = both(keys)
+        scores = dot(two_keys, queries, ((1,), (1,)))
+        grad_probs = dot(both(values), grads, ((1,), (1,)))
+        scored.append((queries, two_keys, grads, scores, grad_probs))
+    for (w, p), (queries, two_keys, grads, scores, grad_probs) in zip(units, scored):
+        probs_low, grads_low = [], []
+        for h in range(2):
+            head = slice(h * WIN, (h + 1) * WIN)
+            biased = scores[head] * scale + bias_ref[2 * p + h]
+            biased = jnp.where(key_at < counts[w], biased, -jnp.inf)
+            weights = jnp.exp(biased - jnp.max(biased, axis=0, keepdims=True))
+            probs = weights * (1.0 / jnp.sum(weights, axis=0, keepdims=True))
+            inner = jnp.sum(probs * grad_probs[head], axis=0, keepdims=True)
+            probs_low.append(probs.astype(jnp.bfloat16))
+            grads_low.append((probs * (grad_probs[head] - inner)).astype(jnp.bfloat16))
+        softened.append((queries, two_keys, grads, probs_low, grads_low))
+    for queries, two_keys, grads, probs_low, grads_low in softened:
+        grad_values = dot(jnp.concatenate(probs_low, axis=1), both(grads), ((1,), (0,)))
+        grad_keys = dot(jnp.concatenate(grads_low, axis=1), both(queries), ((1,), (0,)))
+        grad_queries = dot(jnp.concatenate(grads_low, axis=0), two_keys, ((0,), (0,))) * scale
+        grad_keys = rolled(grad_keys * scale)
+        tiles.append(
+            [
+                jnp.where(low, grad_queries, grad_keys).astype(jnp.bfloat16),
+                jnp.where(low, grad_values, grad_queries).astype(jnp.bfloat16),
+                jnp.where(low, grad_keys, grad_values).astype(jnp.bfloat16),
             ]
-            queries = jnp.where(low, at[0], at[1]).astype(jnp.bfloat16)
-            keys = rolled(jnp.where(low, at[2], at[0])).astype(jnp.bfloat16)
-            values = jnp.where(low, at[1], at[2]).astype(jnp.bfloat16)
-            grads = delta[w * WIN : (w + 1) * WIN, p * 128 : (p + 1) * 128]
-            two_queries, two_keys, two_values, two_grads = map(both, (queries, keys, values, grads))
-            scores = dot(two_keys, queries, ((1,), (1,))).reshape(2, WIN, WIN) * scale + biases[p]
-            grad_probs = dot(two_values, grads, ((1,), (1,))).reshape(2, WIN, WIN)
-            scores = jnp.where(valid, scores, -jnp.inf)
-            weights = jnp.exp(scores - jnp.max(scores, axis=1, keepdims=True))
-            probs = weights * (1.0 / jnp.sum(weights, axis=1, keepdims=True))
-            inner = jnp.sum(probs * grad_probs, axis=1, keepdims=True)
-            grad_scores = probs * (grad_probs - inner)
-            probs_low = probs.astype(jnp.bfloat16)
-            grads_low = grad_scores.astype(jnp.bfloat16)
-            probs_side = jnp.concatenate([probs_low[0], probs_low[1]], axis=1)
-            grads_side = jnp.concatenate([grads_low[0], grads_low[1]], axis=1)
-            grad_values = dot(probs_side, two_grads, ((1,), (0,)))
-            grad_keys = rolled(dot(grads_side, two_queries, ((1,), (0,))) * scale)
-            grad_queries = dot(grads_low.reshape(2 * WIN, WIN), two_keys, ((0,), (0,))) * scale
-            tiles.append(jnp.where(low, grad_queries, grad_keys))
-            tiles.append(jnp.where(low, grad_values, grad_queries))
-            tiles.append(jnp.where(low, grad_keys, grad_values))
-        rows.append(jnp.concatenate(tiles, axis=1).astype(jnp.bfloat16))
-    return jnp.concatenate(rows, axis=0)
+        )
+    return jnp.concatenate(
+        [jnp.concatenate(sum(tiles[w * pairs : (w + 1) * pairs], []), axis=1) for w in range(2)],
+        axis=0,
+    )
 
 
 def block_at(head, step):
@@ -143,7 +151,8 @@
 def near_kernel(
     start, steps, head_ref, counts_ref, act_ref, delta_ref, weight_ref, bias_ref, *rest
 ):
-    outs, turned_ref = rest[-2 - steps : -1], rest[-1]
+    *outs, held_ref = rest[-5 - steps : -4]
+    turned_ref, parts_ref, grads_ref, sems = rest[-4:]
     turned_biases(bias_ref, turned_ref)
     at = [slice(i * ROW + HALF, i * ROW + HALF + WIN) for i in range(2)]
     rows = jnp.concatenate([act_ref[s, :] for s in at], axis=0)
@@ -153,13 +162,29 @@
     step = pl.program_id(0)
     counts = counts_of(counts_ref, block_at(head_ref[0], step + start), 0)
     grads = attend(proj, delta, turned_ref, counts)
-    outs[-1][...] = grads
-    part = part_of(grads, weight)
+    grads_ref[step] = grads
+    parts_ref[step] = part_of(grads, weight)
+    tokens = 2 * WIN
+    copies = [
+        [
+            pltpu.make_async_copy(parts_ref.at[i], outs[i], sems.at[0, i]),
+            pltpu.make_async_copy(
+                grads_ref.at[i], held_ref.at[pl.ds((start + i) * tokens, tokens), :], sems.at[1, i]
+            ),
+        ]
+        for i in range(steps)
+    ]
     for i in range(steps):
 
         @pl.when(step == i)
         def _():
-            outs[i][...] = part
+            for copy in copies[i]:
+                copy.start()
+
+    @pl.when(step == steps - 1)
+    def _():
+        for copy in sum(copies, []):
+            copy.wait()
 
 
 def near_windows(start, steps, head, counts, act, delta, weight, bias, held):
@@ -187,14 +212,18 @@
             num_scalar_prefetch=2,
             grid=(steps,),
             in_specs=specs,
-            out_specs=[pl.BlockSpec((tokens, dim), whole2)] * steps
-            + [pl.BlockSpec((tokens, width), lambda j, head_ref, counts_ref: (j + start, 0))],
-            scratch_shapes=[pltpu.VMEM(bias.shape, bias.dtype)],
+            out_specs=[pl.BlockSpec(memory_space=pl.ANY)] * (steps + 1),
+            scratch_shapes=[
+                pltpu.VMEM(bias.shape, bias.dtype),
+                pltpu.VMEM((steps, tokens, dim), jnp.bfloat16),
+                pltpu.VMEM((steps, tokens, width), jnp.bfloat16),
+                pltpu.SemaphoreType.DMA((2, steps)),
+            ],
         ),
         out_shape=[part] * steps + [jax.ShapeDtypeStruct((4 * tokens, width), jnp.bfloat16)],
         input_output_aliases=aliases,
-        compiler_params=pltpu.CompilerParams(vmem_limit_bytes=VMEM_BYTES),
-        cost_estimate=SMALL_COST,
+        compiler_params=pltpu.CompilerParams(vmem_limit_bytes=VMEM_BYTES if start == 0 else LARGE_VMEM_BYTES),
+        cost_estimate=COST,
         name="near_windows",
     )(head, counts, *operands)
 
@@ -202,7 +231,7 @@
 def far_kernel(
     head_ref, core_ref, counts_ref, act_ref, delta_ref, far_ref, weight_ref, bias_ref, held_ref, *rest
 ):
-    outs, send_ref, keep_ref, turned_ref, total_ref = rest[:8], *rest[8:]
+    outs, send_ref, keep_ref, turned_ref, total_ref, parts_ref, sems = rest[:7], *rest[7:]
     turned_biases(bias_ref, turned_ref)
     dim, delta_width = act_ref.shape[1], delta_ref.shape[1]
     step = pl.program_id(0)
@@ -221,29 +250,36 @@
     counts = counts_of(counts_ref, block_at(head_ref[0], step), 1)
     grads = attend(proj, delta, turned_ref, counts)
     part = part_of(grads, weight)
+    parts_ref[step, :HALF] = part[HALF:WIN]
+    parts_ref[step, HALF:WIN] = part[WIN + HALF :]
+    parts_ref[step, WIN : WIN + HALF] = part[:HALF]
+    parts_ref[step, WIN + HALF :] = part[WIN : WIN + HALF]
+    halves = [pl.ds(0, WIN), pl.ds(WIN, WIN)]
+    copies = [[pltpu.make_async_copy(parts_ref.at[0], outs[0], sems.at[0, 0])]]
+    copies += [
+        [
+            pltpu.make_async_copy(parts_ref.at[i, halves[j], :], outs[2 * i - 1 + j], sems.at[i, j])
+            for j in range(2)
+        ]
+        for i in range(1, 4)
+    ]
     for i in range(4):
 
         @pl.when(step == i)
         def _():
-            for w in range(2):
-                base = w * WIN
-                outs[2 * i][w * HALF : (w + 1) * HALF, :] = part[base + HALF : base + WIN]
-                outs[2 * i + 1][w * HALF : (w + 1) * HALF, :] = part[base : base + HALF]
+            for copy in copies[i]:
+                copy.start()
 
     near_rows = [act_ref[i * ROW + HALF : i * ROW + HALF + WIN, :] for i in range(2)]
     all_rows = jnp.concatenate(near_rows + [rows], axis=0)
     all_grads = jnp.concatenate([held_ref[...], grads], axis=0)
-    product = lax.dot_general(
-        all_rows, all_grads, (((0,), (0,)), ((), ())), preferred_element_type=jnp.float32
-    )
-
     @pl.when(step == 0)
     def _():
-        total_ref[...] = product
-
-    @pl.when(step > 0)
-    def _():
-        total_ref[...] += product
+        total_ref[...] = jnp.zeros_like(total_ref)
+
+    total_ref[...] += lax.dot_general(
+        all_rows, all_grads, (((0,), (0,)), ((), ())), preferred_element_type=jnp.float32
+    )
 
     @pl.when(step == 3)
     def _():
@@ -253,6 +289,8 @@
         send_ref[...] = total_ref[pl.ds(pl.multiple_of((1 - core) * half, half), half), :].astype(
             jnp.bfloat16
         )
+        for copy in sum(copies, []):
+            copy.wait()
 
 
 def far_windows(head, core, counts, act, delta, far, weight, bias, held):
@@ -260,7 +298,10 @@
     blocked = lambda j, head_ref, core_ref, counts_ref: (block_at(head_ref[0], j), 0)
     whole2 = lambda j, head_ref, core_ref, counts_ref: (0, 0)
     whole3 = lambda j, head_ref, core_ref, counts_ref: (0, 0, 0)
-    part = jax.ShapeDtypeStruct((WIN, dim), jnp.bfloat16)
+    parts = [
+        jax.ShapeDtypeStruct((tokens, dim), jnp.bfloat16)
+        for tokens in (2 * WIN, WIN, WIN, WIN, WIN, WIN, WIN)
+    ]
     return pl.pallas_call(
         far_kernel,
         grid_spec=pltpu.PrefetchScalarGridSpec(
@@ -274,20 +315,19 @@
                 pl.BlockSpec(bias.shape, whole3),
                 pl.BlockSpec((2 * WIN, width), lambda j, head_ref, core_ref, counts_ref: (j, 0)),
             ],
-            out_specs=[pl.BlockSpec((WIN, dim), whole2)] * 8
+            out_specs=[pl.BlockSpec(memory_space=pl.ANY)] * 7
             + [pl.BlockSpec((dim // 2, width), whole2)] * 2,
             scratch_shapes=[
                 pltpu.VMEM(bias.shape, bias.dtype),
                 pltpu.VMEM((dim, width), jnp.float32),
+                pltpu.VMEM((4, 2 * WIN, dim), jnp.bfloat16),
+                pltpu.SemaphoreType.DMA((4, 2)),
             ],
         ),
-        out_shape=[part] * 8
-        + [
-            jax.ShapeDtypeStruct((dim // 2, width), jnp.bfloat16),
-            jax.ShapeDtypeStruct((dim // 2, width), jnp.float32),
-        ],
-        compiler_params=pltpu.CompilerParams(vmem_limit_bytes=VMEM_BYTES),
-        cost_estimate=SMALL_COST,
+        out_shape=parts
+        + [jax.ShapeDtypeStruct((dim // 2, width), dtype) for dtype in (jnp.bfloat16, jnp.float32)],
+        compiler_params=pltpu.CompilerParams(vmem_limit_bytes=LARGE_VMEM_BYTES),
+        cost_estimate=COST,
         name="far_windows",
     )(head, core, counts, act, delta, far, weight, bias, held)
 
@@ -330,7 +370,8 @@
         in_specs=[pl.BlockSpec(memory_space=pltpu.SMEM)] + [vmem] * len(operands),
         out_specs=[vmem] * len(out_shape) if several else vmem,
         out_shape=out_shape,
-        compiler_params=pltpu.CompilerParams(vmem_limit_bytes=VMEM_BYTES),
+        compiler_params=pltpu.CompilerParams(vmem_limit_bytes=SMALL_VMEM_BYTES),
+        cost_estimate=COST,
     )(place, *operands)
 
 
@@ -352,13 +393,8 @@
     lon = lax.axis_index("lon")
     core, chip = (lon % 2).reshape(1), (lon // 2).reshape(1)
 
-    arrived = []
-
     def hop(x, bits):
-        x = x if len(arrived) < 2 else after(x, arrived[-2])
-        pairs = [(i, i ^ bits) for i in range(lax.axis_size("head"))]
-        arrived.append(lax.ppermute(x, "head", pairs))
-        return arrived[-1]
+        return lax.ppermute(x, "head", [(i, i ^ bits) for i in range(lax.axis_size("head"))])
 
     far = passed_along(first_rows(activations, attn_grad), "lon", -1)
     here = (activations, attn_grad, qkv_weight, pos_bias)
@@ -366,46 +402,49 @@
     in_near = [hop(first, BESIDE)]
     *near, held = near_windows(1, 3, head, key_counts, *here, held)
     in_near.append(hop(near[0], BESIDE))
-    in_near.append(hop(add(near[1], in_near[0]), ACROSS))
-    far = after(far, in_near[0]).reshape(WIN_ROWS * HALF, far.shape[2])
+    in_near.append(hop(after(add(near[1], in_near[0]), far), ACROSS))
+    far = far.reshape(WIN_ROWS * HALF, far.shape[2])
     *parts, outgoing, mine = far_windows(
         head, core, key_counts, activations, attn_grad, far, qkv_weight, pos_bias, held
     )
-    nexts, this = parts[0::2], parts[1::2]
-    in_next, in_this = [hop(nexts[0], BESIDE)], [hop(this[0], BESIDE)]
-    in_next.append(hop(add(nexts[2], in_next[0]), ACROSS))
-    in_next.append(hop(nexts[1], BESIDE))
-    in_this.append(hop(add(this[2], in_this[0]), ACROSS))
-    in_this.append(hop(this[1], BESIDE))
+    incoming = swapped(outgoing, 1)
+    both_a, next_b, this_b, next_c, this_c, next_d, this_d = parts
+    in_both, more_next = hop(both_a, BESIDE), hop(next_b, BESIDE)
     near_sum = add(near[2], *in_near[1:])
-    back = passed_along(add(nexts[3], *in_next[1:]), "lon", 1)
-    this_sum = add(this[3], *in_this[1:])
-    input_grad = jnp.concatenate(
-        [x.reshape(2, -1, dim) for x in (back, near_sum, this_sum)], axis=1
-    ).reshape(2 * ROW, dim)
-
-    incoming = swapped(outgoing, 1)
+
     block = (dim // 8, width)
     low = jax.ShapeDtypeStruct(block, jnp.bfloat16)
     own, *sent = small(
         split_kernel,
         [jax.ShapeDtypeStruct(block, jnp.float32), low, low, low],
-        after(chip, *in_near[1:]),
+        after(chip, near_sum),
         mine,
         incoming,
     )
     came = [swapped(part, 2 * (i + 1)) for i, part in enumerate(sent)]
+
+    in_both = after(in_both, own, *came)
+    out_next, out_this = add(next_c, in_both[:WIN]), add(this_c, in_both[WIN:])
+    more_this = hop(after(this_b, out_next), BESIDE)
+    over_next, over_this = hop(out_next, ACROSS), hop(out_this, ACROSS)
+
     scale = 1.0 / math.sqrt(total_tokens)
-    done = small(
-        functools.partial(join_kernel, scale), low, after(chip, in_next[0], in_this[0]), own, *came
-    )
+    done = small(functools.partial(join_kernel, scale), low, after(chip, out_this), own, *came)
     others = [swapped(done, 2 * (i + 1)) for i in range(3)]
+
+    next_sum = add(next_d, more_next, over_next)
+    back = passed_along(next_sum, "lon", 1)
     half = jax.ShapeDtypeStruct((dim // 2, width), jnp.bfloat16)
-    gathered = small(gather_kernel, half, after(chip, *in_next[1:], in_this[1]), done, *others)
+    gathered = small(gather_kernel, half, chip, done, *others)
     other_half = swapped(gathered, 1)
     weight_grad = small(
         widen_kernel, jax.ShapeDtypeStruct((dim, width), jnp.float32), core, gathered, other_half
     )
+    this_sum = add(this_d, more_this, over_this)
+    input_grad = jnp.concatenate(
+        [x.reshape(2, -1, dim) for x in (back, near_sum, this_sum)], axis=1
+    ).reshape(2 * ROW, dim)
+
     return (input_grad, weight_grad)
 
 

time: 102 us -> 95.7 us (0.938)
  starting transfers between devices: 22.3 us -> 28 us
  Pallas kernels: 37.6 us -> 33.9 us
  waiting for transfers between devices: 30.7 us -> 27.2 us
  other arithmetic: 6.57 us -> 4.39 us
  local copies, waits for them, and re-layouts: 3.36 us -> 1.19 us
    ppermute x9 -> x8, waiting for transfers between devices: 15.4 us -> 21.3 us  [hop(): lax.ppermute(x, 'head', [(i, i ^ bits) for i in range(lax.axis_size('head...]
    ppermute x8, waiting for transfers between devices: 10.7 us -> 5.55 us  [swapped(): return lax.ppermute(shard, 'lon', [(i, i ^ bits) for i in range(size)])]
    ppermute x9 -> x8, starting transfers between devices: 11.2 us -> 15.6 us  [hop(): lax.ppermute(x, 'head', [(i, i ^ bits) for i in range(lax.axis_size('head...]
    ppermute x2, waiting for transfers between devices: 4.59 us -> 0.37 us  [passed_along(): lax.ppermute(shard, axis, [(i, (i + by) % size) for i in range(size)])]
    pallas_call x1, Pallas kernels: 18.6 us -> 16.3 us  [far_windows(): pl.pallas_call(far_kernel, grid_spec=pltpu.PrefetchScalarGridSpec(num_sca...]
    convert_element_type x6 -> x5, other arithmetic: 5.53 us -> 3.35 us  [add(): return total.astype(jnp.bfloat16)]
    unnamed x16 -> x24, local copies, waits for them, and re-layouts: 3.36 us -> 1.19 us
    ppermute x8, starting transfers between devices: 7.18 us -> 8.93 us  [swapped(): return lax.ppermute(shard, 'lon', [(i, i ^ bits) for i in range(size)])]
  transfers between devices with their start and end apart: 19 -> 18, of which waited for: 9 -> 9; matrix products, arithmetic and copies ran while one was open for 6% -> 4% of each run, Pallas kernels for 33% -> 31%
where the time goes in v3:
time: 95.7 us; the launch traced here: 95.5 us
  Pallas kernels  33.9 us (35%)
  starting transfers between devices  28 us (29%)
  waiting for transfers between devices  27.2 us (28%)
  other arithmetic  4.39 us (5%)
  local copies, waits for them, and re-layouts  1.19 us (1%)
    ppermute x8, waiting for transfers between devices, hop(): lax.ppermute(x, 'head', [(i, i ^ bits) for i in range(lax.axis_size('head...  21.3 us
    pallas_call x1, Pallas kernels, far_windows(): pl.pallas_call(far_kernel, grid_spec=pltpu.PrefetchScalarGridSpec(num_sca...  16.3 us
    ppermute x8, starting transfers between devices, hop(): lax.ppermute(x, 'head', [(i, i ^ bits) for i in range(lax.axis_size('head...  15.6 us
    pallas_call x2, Pallas kernels, near_windows(): pl.pallas_call(functools.partial(near_kernel, start, steps), grid_spec=pl...  12.9 us
    ppermute x8, starting transfers between devices, swapped(): return lax.ppermute(shard, 'lon', [(i, i ^ bits) for i in range(size)])  8.93 us
    ppermute x8, waiting for transfers between devices, swapped(): return lax.ppermute(shard, 'lon', [(i, i ^ bits) for i in range(size)])  5.55 us
    ppermute x2, starting transfers between devices, passed_along(): lax.ppermute(shard, axis, [(i, (i + by) % size) for i in range(size)])  3.44 us
    convert_element_type x5, other arithmetic, add(): return total.astype(jnp.bfloat16)  3.35 us
  transfers between devices with their start and end apart: 18, of which 9 were waited for; matrix products, arithmetic and copies ran while one was open for 4% of the time, Pallas kernels for 31%

profile of v3, /device:TPU:0, one launch (start us, length us, event | category | flops | bytes accessed | tf_op | source)
XLA Modules:
  0.0 95.5 jit_solution(6456925232037034246)
XLA Ops:
  0.7 2.5 %first_rows.1 = bf16[8,64,1280]{2,1,0:T(8,128)(2,1)} custom-call(bf16[8,256,1024]{2,1,0:T(8,128)(2,1)} %bitcast.11, bf16[8,256,256]{2,1,0:T(8,128)(2,1)} %bitcast.10), custom_call_target="tpu_custom_call" | custom-call | tf_op jit(solution)/shard_map/first_rows/pallas_call | solution.py:123
  3.2 3.4 %collective-permute-start = (bf16[8,64,1280]{2,1,0:T(8,128)(2,1)}, bf16[8,64,1280]{2,1,0:T(8,128)(2,1)}, u32[]{:S(2)}, u32[]{:S(2)}) collective-permute-start(bf16[8,64,1280]{2,1,0:T(8,128)(2,1)} %first_rows.1), channel_id=1, source_target_pairs={{0,28},{4,0},{8,4},{12,8},{16,12},{20,16},{24,20},{28,24},{1,29},{... | collective-permute-start | bytes 3932168 | tf_op jit(solution)/shard_map/ppermute | solution.py:29
  6.6 3.8 %near_windows.2 = (bf16[256,1024]{1,0:T(8,128)(2,1)S(1)}, bf16[1024,768]{1,0:T(8,128)(2,1)S(1)}) custom-call(s32[1]{0:T(128)} %bitcast.head_ref, s32[16]{0:T(128)S(1)} %copy-done.5, bf16[2048,1024]{1,0:T(8,128)(2,1)} %act_ref.5, bf16[2048,256]{1,0:T(8,128)(2,1)S(1)} %copy-done, bf16[1024,768]{1,0:T(8,128)(2,1)S(1)} %copy-done.1, f32[4,128,128]{2,1,0:T(8,128)S(1)} %copy-done.3), custom_call_target="tpu_custom_call" | custom-call | flops 1000000 | bytes 100000 | tf_op jit(solution)/shard_map/near_windows/pallas_call | solution.py:209
  11.6 1.6 %collective-permute-start.4 = (bf16[256,1024]{1,0:T(8,128)(2,1)S(1)}, bf16[256,1024]{1,0:T(8,128)(2,1)S(1)}, u32[]{:S(2)}, u32[]{:S(2)}) collective-permute-start(bf16[256,1024]{1,0:T(8,128)(2,1)S(1)} %get-tuple-element.35), channel_id=1, source_target_pairs={{0,1},{1,0},{2,3},{3,2},{4,5},{5,4},{6,7},{7,6},{8,9},{9,8},{10,11... | collective-permute-start | bytes 1572872 | tf_op jit(solution)/shard_map/ppermute | solution.py:397
  13.1 9.1 %near_windows.3 = (bf16[256,1024]{1,0:T(8,128)(2,1)}, bf16[256,1024]{1,0:T(8,128)(2,1)}, bf16[256,1024]{1,0:T(8,128)(2,1)}, bf16[1024,768]{1,0:T(8,128)(2,1)}) custom-call(s32[1]{0:T(128)} %bitcast.head_ref, s32[16]{0:T(128)} %counts_ref.5, bf16[2048,1024]{1,0:T(8,128)(2,1)} %act_ref.5, ...), custom_call_target="tpu_custom_call", output_to_operand_aliasing={{3}: (6, {})} | custom-call | flops 1000000 | bytes 100000 | tf_op jit(solution)/shard_map/near_windows/pallas_call | solution.py:209
  22.7 2.2 %collective-permute-done.4 = bf16[256,1024]{1,0:T(8,128)(2,1)S(1)} collective-permute-done((bf16[256,1024]{1,0:T(8,128)(2,1)S(1)}, bf16[256,1024]{1,0:T(8,128)(2,1)S(1)}, u32[]{:S(2)}, u32[]{:S(2)}) %collective-permute-start.4) | collective-permute-done | bytes 524320 | tf_op jit(solution)/shard_map/ppermute | solution.py:397
  26.2 2.5 %collective-permute-start.5 = (bf16[256,1024]{1,0:T(8,128)(2,1)S(1)}, bf16[256,1024]{1,0:T(8,128)(2,1)}, u32[]{:S(2)}, u32[]{:S(2)}) collective-permute-start(bf16[256,1024]{1,0:T(8,128)(2,1)S(1)} %add_convert_fusion.1), channel_id=1, source_target_pairs={{0,2},{1,3},{2,0},{3,1},{4,6},{5,7},{6,4},{7,5},{8,10},{9,11},{10,... | collective-permute-start | bytes 1572872 | tf_op jit(solution)/shard_map/ppermute | solution.py:397
  28.7 16.3 %far_windows.1 = (bf16[256,1024]{1,0:T(8,128)(2,1)}, bf16[128,1024]{1,0:T(8,128)(2,1)}, bf16[128,1024]{1,0:T(8,128)(2,1)}, bf16[128,1024]{1,0:T(8,128)(2,1)}, bf...) custom-call(s32[1]{0:T(128)} %bitcast.head_ref, ...), custom_call_target="tpu_custom_call" | custom-call | flops 1000000 | bytes 100000 | tf_op jit(solution)/shard_map/far_windows/pallas_call | solution.py:305
  45.1 2.6 %collective-permute-start.2 = (bf16[256,1024]{1,0:T(8,128)(2,1)}, bf16[256,1024]{1,0:T(8,128)(2,1)S(1)}, u32[]{:S(2)}, u32[]{:S(2)}) collective-permute-start(bf16[256,1024]{1,0:T(8,128)(2,1)} %get-tuple-element.31), channel_id=1, source_target_pairs={{0,1},{1,0},{2,3},{3,2},{4,5},{5,4},{6,7},{7,6},{8,9},{9,8},{10,11... | collective-permute-start | bytes 1572872 | tf_op jit(solution)/shard_map/ppermute | solution.py:397
  47.6 1.4 %collective-permute-done.5 = bf16[256,1024]{1,0:T(8,128)(2,1)} collective-permute-done((bf16[256,1024]{1,0:T(8,128)(2,1)S(1)}, bf16[256,1024]{1,0:T(8,128)(2,1)}, u32[]{:S(2)}, u32[]{:S(2)}) %collective-permute-start.5) | collective-permute-done | bytes 524320 | tf_op jit(solution)/shard_map/ppermute | solution.py:397
  49.1 1.7 %add_convert_fusion = bf16[256,1024]{1,0:T(8,128)(2,1)S(1)} fusion(bf16[256,1024]{1,0:T(8,128)(2,1)} %collective-permute-done.5, bf16[256,1024]{1,0:T(8,128)(2,1)} %collective-permute-done.3, bf16[256,1024]{1,0:T(8,128)(2,1)} %get-tuple-element.32), kind=kLoop, calls=%fused_computation.1 | loop fusion | flops 1572864 | bytes 2097152 | tf_op jit(solution)/shard_map/convert_element_type | solution.py:386
  51.0 3.7 %collective-permute-start.7 = (bf16[128,768]{1,0:T(8,128)(2,1)S(1)}, bf16[128,768]{1,0:T(8,128)(2,1)S(1)}, u32[]{:S(2)}, u32[]{:S(2)}) collective-permute-start(bf16[128,768]{1,0:T(8,128)(2,1)S(1)} %get-tuple-element.41), channel_id=1, source_target_pairs={{0,8},{4,12},{8,0},{12,4},{16,24},{20,28},{24,16},{28,20},{1,9},{5... | collective-permute-start | bytes 589832 | tf_op jit(solution)/shard_map/ppermute | solution.py:34
  54.7 1.5 %collective-permute-start.8 = (bf16[128,768]{1,0:T(8,128)(2,1)S(1)}, bf16[128,768]{1,0:T(8,128)(2,1)S(1)}, u32[]{:S(2)}, u32[]{:S(2)}) collective-permute-start(bf16[128,768]{1,0:T(8,128)(2,1)S(1)} %get-tuple-element.42), channel_id=1, source_target_pairs={{0,16},{4,20},{8,24},{12,28},{16,0},{20,4},{24,8},{28,12},{1,17},{... | collective-permute-start | bytes 589832 | tf_op jit(solution)/shard_map/ppermute | solution.py:34
  56.2 4.2 %collective-permute-done.2 = bf16[256,1024]{1,0:T(8,128)(2,1)S(1)} collective-permute-done((bf16[256,1024]{1,0:T(8,128)(2,1)}, bf16[256,1024]{1,0:T(8,128)(2,1)S(1)}, u32[]{:S(2)}, u32[]{:S(2)}) %collective-permute-start.2) | collective-permute-done | bytes 524320 | tf_op jit(solution)/shard_map/ppermute | solution.py:397
  60.4 3.7 %collective-permute-done.8.b_ref = bf16[128,768]{1,0:T(8,128)(2,1)S(1)} collective-permute-done((bf16[128,768]{1,0:T(8,128)(2,1)S(1)}, bf16[128,768]{1,0:T(8,128)(2,1)S(1)}, u32[]{:S(2)}, u32[]{:S(2)}) %collective-permute-start.8) | collective-permute-done | bytes 196640 | tf_op jit(solution)/shard_map/ppermute | solution.py:34
  65.4 1.4 %collective-permute-start.15 = (bf16[128,768]{1,0:T(8,128)(2,1)S(1)}, bf16[128,768]{1,0:T(8,128)(2,1)S(1)}, u32[]{:S(2)}, u32[]{:S(2)}) collective-permute-start(bf16[128,768]{1,0:T(8,128)(2,1)S(1)} %shard_map.69.own_ref), channel_id=1, source_target_pairs={{0,16},{4,20},{8,24},{12,28},{16,0},{20,4},{24,8},{28,12},{1,17},{... | collective-permute-start | bytes 589832 | tf_op jit(solution)/shard_map/ppermute | solution.py:34
  68.7 3.5 %collective-permute-start.10 = (bf16[128,1024]{1,0:T(8,128)(2,1)S(1)}, bf16[128,1024]{1,0:T(8,128)(2,1)S(1)}, u32[]{:S(2)}, u32[]{:S(2)}) collective-permute-start(bf16[128,1024]{1,0:T(8,128)(2,1)S(1)} %get-tuple-element.50), channel_id=1, source_target_pairs={{0,2},{1,3},{2,0},{3,1},{4,6},{5,7},{6,4},{7,5},{8,10},{9,11},{10,... | collective-permute-start | bytes 786440 | tf_op jit(solution)/shard_map/ppermute | solution.py:397
  72.2 1.8 %collective-permute-done.15.b_ref = bf16[128,768]{1,0:T(8,128)(2,1)S(1)} collective-permute-done((bf16[128,768]{1,0:T(8,128)(2,1)S(1)}, bf16[128,768]{1,0:T(8,128)(2,1)S(1)}, u32[]{:S(2)}, u32[]{:S(2)}) %collective-permute-start.15) | collective-permute-done | bytes 196640 | tf_op jit(solution)/shard_map/ppermute | solution.py:34
  74.1 1.7 %collective-permute-start.13 = (bf16[128,1024]{1,0:T(8,128)(2,1)S(1)}, bf16[128,1024]{1,0:T(8,128)(2,1)S(1)}, u32[]{:S(2)}, u32[]{:S(2)}) collective-permute-start(bf16[128,1024]{1,0:T(8,128)(2,1)S(1)} %get-tuple-element.51), channel_id=1, source_target_pairs={{0,2},{1,3},{2,0},{3,1},{4,6},{5,7},{6,4},{7,5},{8,10},{9,11},{10,... | collective-permute-start | bytes 786440 | tf_op jit(solution)/shard_map/ppermute | solution.py:397
  75.8 2.6 %collective-permute-start.12 = (bf16[128,1024]{1,0:T(8,128)(2,1)S(1)}, bf16[128,1024]{1,0:T(8,128)(2,1)S(1)}, u32[]{:S(2)}, u32[]{:S(2)}) collective-permute-start(bf16[128,1024]{1,0:T(8,128)(2,1)S(1)} %copy-done.10), channel_id=1, source_target_pairs={{0,1},{1,0},{2,3},{3,2},{4,5},{5,4},{6,7},{7,6},{8,9},{9,8},{10,11... | collective-permute-start | bytes 786440 | tf_op jit(solution)/shard_map/ppermute | solution.py:397
  78.4 7.3 %collective-permute-done.10 = bf16[128,1024]{1,0:T(8,128)(2,1)S(1)} collective-permute-done((bf16[128,1024]{1,0:T(8,128)(2,1)S(1)}, bf16[128,1024]{1,0:T(8,128)(2,1)S(1)}, u32[]{:S(2)}, u32[]{:S(2)}) %collective-permute-start.10) | collective-permute-done | bytes 262176 | tf_op jit(solution)/shard_map/ppermute | solution.py:397
  85.9 2.6 %collective-permute-done.12 = bf16[128,1024]{1,0:T(8,128)(2,1)S(1)} collective-permute-done((bf16[128,1024]{1,0:T(8,128)(2,1)S(1)}, bf16[128,1024]{1,0:T(8,128)(2,1)S(1)}, u32[]{:S(2)}, u32[]{:S(2)}) %collective-permute-start.12) | collective-permute-done | bytes 262176 | tf_op jit(solution)/shard_map/ppermute | solution.py:397
  88.5 3.6 %collective-permute-done.13 = bf16[128,1024]{1,0:T(8,128)(2,1)S(1)} collective-permute-done((bf16[128,1024]{1,0:T(8,128)(2,1)S(1)}, bf16[128,1024]{1,0:T(8,128)(2,1)S(1)}, u32[]{:S(2)}, u32[]{:S(2)}) %collective-permute-start.13) | collective-permute-done | bytes 262176 | tf_op jit(solution)/shard_map/ppermute | solution.py:397
  93.6 1.9 %shard_map.71 = f32[1024,768]{1,0:T(8,128)} custom-call(s32[1]{0:T(128)} %bitcast.1.core_ref, bf16[512,768]{1,0:T(8,128)(2,1)S(1)} %shard_map.70.mine_ref, bf16[512,768]{1,0:T(8,128)(2,1)S(1)} %collective-permute-done.17.theirs_ref), custom_call_target="tpu_custom_call" | custom-call | flops 1000000 | bytes 100000 | tf_op jit(solution)/shard_map/pallas_call | solution.py:368
  (50 shorter events, 8.2 us)
Async XLA Ops:
  3.2 23.0 %collective-permute-start = (bf16[8,64,1280]{2,1,0:T(8,128)(2,1)}, bf16[8,64,1280]{2,1,0:T(8,128)(2,1)}, u32[]{:S(2)}, u32[]{:S(2)}) collective-permute-start(bf16[8,64,1280]{2,1,0:T(8,128)(2,1)} %first_rows.1), channel_id=1, source_target_pairs={{0,28},{4,0},{8,4},{12,8},{16,12},{20,16},{24,20},{28,24},{1,29},{... | collective-permute-start | bytes 3932168 | tf_op jit(solution)/shard_map/ppermute | solution.py:29
  11.6 13.4 %collective-permute-start.4 = (bf16[256,1024]{1,0:T(8,128)(2,1)S(1)}, bf16[256,1024]{1,0:T(8,128)(2,1)S(1)}, u32[]{:S(2)}, u32[]{:S(2)}) collective-permute-start(bf16[256,1024]{1,0:T(8,128)(2,1)S(1)} %get-tuple-element.35), channel_id=1, source_target_pairs={{0,1},{1,0},{2,3},{3,2},{4,5},{5,4},{6,7},{7,6},{8,9},{9,8},{10,11... | collective-permute-start | bytes 1572872 | tf_op jit(solution)/shard_map/ppermute | solution.py:397
  22.2 25.4 %collective-permute-start.3 = (bf16[256,1024]{1,0:T(8,128)(2,1)}, bf16[256,1024]{1,0:T(8,128)(2,1)}, u32[]{:S(2)}, u32[]{:S(2)}) collective-permute-start(bf16[256,1024]{1,0:T(8,128)(2,1)} %get-tuple-element.33), channel_id=1, source_target_pairs={{0,1},{1,0},{2,3},{3,2},{4,5},{5,4},{6,7},{7,6},{8,9},{9,8},{10,11... | collective-permute-start | bytes 1572872 | tf_op jit(solution)/shard_map/ppermute | solution.py:397
  26.2 22.9 %collective-permute-start.5 = (bf16[256,1024]{1,0:T(8,128)(2,1)S(1)}, bf16[256,1024]{1,0:T(8,128)(2,1)}, u32[]{:S(2)}, u32[]{:S(2)}) collective-permute-start(bf16[256,1024]{1,0:T(8,128)(2,1)S(1)} %add_convert_fusion.1), channel_id=1, source_target_pairs={{0,2},{1,3},{2,0},{3,1},{4,6},{5,7},{6,4},{7,5},{8,10},{9,11},{10,... | collective-permute-start | bytes 1572872 | tf_op jit(solution)/shard_map/ppermute | solution.py:397
  45.0 5.8 %collective-permute-start.6 = (bf16[512,768]{1,0:T(8,128)(2,1)}, bf16[512,768]{1,0:T(8,128)(2,1)S(1)}, u32[]{:S(2)}, u32[]{:S(2)}) collective-permute-start(bf16[512,768]{1,0:T(8,128)(2,1)} %get-tuple-element.39), channel_id=1, source_target_pairs={{0,4},{4,0},{8,12},{12,8},{16,20},{20,16},{24,28},{28,24},{1,5},{5... | collective-permute-start | bytes 2359304 | tf_op jit(solution)/shard_map/ppermute | solution.py:34
  45.1 15.3 %collective-permute-start.2 = (bf16[256,1024]{1,0:T(8,128)(2,1)}, bf16[256,1024]{1,0:T(8,128)(2,1)S(1)}, u32[]{:S(2)}, u32[]{:S(2)}) collective-permute-start(bf16[256,1024]{1,0:T(8,128)(2,1)} %get-tuple-element.31), channel_id=1, source_target_pairs={{0,1},{1,0},{2,3},{3,2},{4,5},{5,4},{6,7},{7,6},{8,9},{9,8},{10,11... | collective-permute-start | bytes 1572872 | tf_op jit(solution)/shard_map/ppermute | solution.py:397
  49.1 15.0 %copy-start.8 = (bf16[128,1024]{1,0:T(8,128)(2,1)S(1)}, bf16[128,1024]{1,0:T(8,128)(2,1)}, u32[]{:S(2)}) copy-start(bf16[128,1024]{1,0:T(8,128)(2,1)} %get-tuple-element.30) | copy-start | bytes 786436
  49.1 15.0 %copy-start.9 = (bf16[128,1024]{1,0:T(8,128)(2,1)S(1)}, bf16[128,1024]{1,0:T(8,128)(2,1)}, u32[]{:S(2)}) copy-start(bf16[128,1024]{1,0:T(8,128)(2,1)} %get-tuple-element.48) | copy-start | bytes 786436
  50.8 17.2 %copy-start.11 = (bf16[128,1024]{1,0:T(8,128)(2,1)S(1)}, bf16[128,1024]{1,0:T(8,128)(2,1)}, u32[]{:S(2)}) copy-start(bf16[128,1024]{1,0:T(8,128)(2,1)} %get-tuple-element.29) | copy-start | bytes 786436
  51.0 9.4 %collective-permute-start.7 = (bf16[128,768]{1,0:T(8,128)(2,1)S(1)}, bf16[128,768]{1,0:T(8,128)(2,1)S(1)}, u32[]{:S(2)}, u32[]{:S(2)}) collective-permute-start(bf16[128,768]{1,0:T(8,128)(2,1)S(1)} %get-tuple-element.41), channel_id=1, source_target_pairs={{0,8},{4,12},{8,0},{12,4},{16,24},{20,28},{24,16},{28,20},{1,9},{5... | collective-permute-start | bytes 589832 | tf_op jit(solution)/shard_map/ppermute | solution.py:34
  54.7 9.5 %collective-permute-start.8 = (bf16[128,768]{1,0:T(8,128)(2,1)S(1)}, bf16[128,768]{1,0:T(8,128)(2,1)S(1)}, u32[]{:S(2)}, u32[]{:S(2)}) collective-permute-start(bf16[128,768]{1,0:T(8,128)(2,1)S(1)} %get-tuple-element.42), channel_id=1, source_target_pairs={{0,16},{4,20},{8,24},{12,28},{16,0},{20,4},{24,8},{28,12},{1,17},{... | collective-permute-start | bytes 589832 | tf_op jit(solution)/shard_map/ppermute | solution.py:34
  56.2 7.9 %collective-permute-start.9 = (bf16[128,768]{1,0:T(8,128)(2,1)S(1)}, bf16[128,768]{1,0:T(8,128)(2,1)S(1)}, u32[]{:S(2)}, u32[]{:S(2)}) collective-permute-start(bf16[128,768]{1,0:T(8,128)(2,1)S(1)} %get-tuple-element.43), channel_id=1, source_target_pairs={{0,24},{4,28},{8,16},{12,20},{16,8},{20,12},{24,0},{28,4},{1,25},{... | collective-permute-start | bytes 589832 | tf_op jit(solution)/shard_map/ppermute | solution.py:34
  64.1 11.7 %copy-start.10 = (bf16[128,1024]{1,0:T(8,128)(2,1)S(1)}, bf16[128,1024]{1,0:T(8,128)(2,1)}, u32[]{:S(2)}) copy-start(bf16[128,1024]{1,0:T(8,128)(2,1)} %get-tuple-element.47) | copy-start | bytes 786436
  64.1 21.6 %copy-start.7 = (bf16[128,1024]{1,0:T(8,128)(2,1)S(1)}, bf16[128,1024]{1,0:T(8,128)(2,1)}, u32[]{:S(2)}) copy-start(bf16[128,1024]{1,0:T(8,128)(2,1)} %get-tuple-element.28) | copy-start | bytes 786436
  64.3 27.7 %copy-start.6 = (bf16[128,1024]{1,0:T(8,128)(2,1)S(1)}, bf16[128,1024]{1,0:T(8,128)(2,1)}, u32[]{:S(2)}) copy-start(bf16[128,1024]{1,0:T(8,128)(2,1)} %get-tuple-element.45) | copy-start | bytes 786436
  64.5 7.8 %collective-permute-start.16 = (bf16[128,768]{1,0:T(8,128)(2,1)S(1)}, bf16[128,768]{1,0:T(8,128)(2,1)S(1)}, u32[]{:S(2)}, u32[]{:S(2)}) collective-permute-start(bf16[128,768]{1,0:T(8,128)(2,1)S(1)} %shard_map.69.own_ref), channel_id=1, source_target_pairs={{0,24},{4,28},{8,16},{12,20},{16,8},{20,12},{24,0},{28,4},{1,25},{... | collective-permute-start | bytes 589832 | tf_op jit(solution)/shard_map/ppermute | solution.py:34
  65.4 8.6 %collective-permute-start.15 = (bf16[128,768]{1,0:T(8,128)(2,1)S(1)}, bf16[128,768]{1,0:T(8,128)(2,1)S(1)}, u32[]{:S(2)}, u32[]{:S(2)}) collective-permute-start(bf16[128,768]{1,0:T(8,128)(2,1)S(1)} %shard_map.69.own_ref), channel_id=1, source_target_pairs={{0,16},{4,20},{8,24},{12,28},{16,0},{20,4},{24,8},{28,12},{1,17},{... | collective-permute-start | bytes 589832 | tf_op jit(solution)/shard_map/ppermute | solution.py:34
  66.7 7.3 %collective-permute-start.14 = (bf16[128,768]{1,0:T(8,128)(2,1)S(1)}, bf16[128,768]{1,0:T(8,128)(2,1)S(1)}, u32[]{:S(2)}, u32[]{:S(2)}) collective-permute-start(bf16[128,768]{1,0:T(8,128)(2,1)S(1)} %shard_map.69.own_ref), channel_id=1, source_target_pairs={{0,8},{4,12},{8,0},{12,4},{16,24},{20,28},{24,16},{28,20},{1,9},{5... | collective-permute-start | bytes 589832 | tf_op jit(solution)/shard_map/ppermute | solution.py:34
  68.0 10.4 %collective-permute-start.1 = (bf16[128,1024]{1,0:T(8,128)(2,1)S(1)}, bf16[128,1024]{1,0:T(8,128)(2,1)S(1)}, u32[]{:S(2)}, u32[]{:S(2)}) collective-permute-start(bf16[128,1024]{1,0:T(8,128)(2,1)S(1)} %copy-done.11), channel_id=1, source_target_pairs={{0,1},{1,0},{2,3},{3,2},{4,5},{5,4},{6,7},{7,6},{8,9},{9,8},{10,11... | collective-permute-start | bytes 786440 | tf_op jit(solution)/shard_map/ppermute | solution.py:397
  68.7 17.0 %collective-permute-start.10 = (bf16[128,1024]{1,0:T(8,128)(2,1)S(1)}, bf16[128,1024]{1,0:T(8,128)(2,1)S(1)}, u32[]{:S(2)}, u32[]{:S(2)}) collective-permute-start(bf16[128,1024]{1,0:T(8,128)(2,1)S(1)} %get-tuple-element.50), channel_id=1, source_target_pairs={{0,2},{1,3},{2,0},{3,1},{4,6},{5,7},{6,4},{7,5},{8,10},{9,11},{10,... | collective-permute-start | bytes 786440 | tf_op jit(solution)/shard_map/ppermute | solution.py:397
  74.1 19.6 %collective-permute-start.17 = (bf16[512,768]{1,0:T(8,128)(2,1)S(1)}, bf16[512,768]{1,0:T(8,128)(2,1)S(1)}, u32[]{:S(2)}, u32[]{:S(2)}) collective-permute-start(bf16[512,768]{1,0:T(8,128)(2,1)S(1)} %shard_map.70.mine_ref), channel_id=1, source_target_pairs={{0,4},{4,0},{8,12},{12,8},{16,20},{20,16},{24,28},{28,24},{1,5},{5... | collective-permute-start | bytes 2359304 | tf_op jit(solution)/shard_map/ppermute | solution.py:34
  74.1 17.9 %collective-permute-start.13 = (bf16[128,1024]{1,0:T(8,128)(2,1)S(1)}, bf16[128,1024]{1,0:T(8,128)(2,1)S(1)}, u32[]{:S(2)}, u32[]{:S(2)}) collective-permute-start(bf16[128,1024]{1,0:T(8,128)(2,1)S(1)} %get-tuple-element.51), channel_id=1, source_target_pairs={{0,2},{1,3},{2,0},{3,1},{4,6},{5,7},{6,4},{7,5},{8,10},{9,11},{10,... | collective-permute-start | bytes 786440 | tf_op jit(solution)/shard_map/ppermute | solution.py:397
  75.8 12.7 %collective-permute-start.12 = (bf16[128,1024]{1,0:T(8,128)(2,1)S(1)}, bf16[128,1024]{1,0:T(8,128)(2,1)S(1)}, u32[]{:S(2)}, u32[]{:S(2)}) collective-permute-start(bf16[128,1024]{1,0:T(8,128)(2,1)S(1)} %copy-done.10), channel_id=1, source_target_pairs={{0,1},{1,0},{2,3},{3,2},{4,5},{5,4},{6,7},{7,6},{8,9},{9,8},{10,11... | collective-permute-start | bytes 786440 | tf_op jit(solution)/shard_map/ppermute | solution.py:397
  85.8 6.7 %collective-permute-start.11 = (bf16[128,1024]{1,0:T(8,128)(2,1)S(1)}, bf16[128,1024]{1,0:T(8,128)(2,1)S(1)}, u32[]{:S(2)}, u32[]{:S(2)}) collective-permute-start(bf16[128,1024]{1,0:T(8,128)(2,1)S(1)} %add_convert_fusion.4), channel_id=1, source_target_pairs={{0,4},{4,8},{8,12},{12,16},{16,20},{20,24},{24,28},{28,0},{1,5},{5... | collective-permute-start | bytes 786440 | tf_op jit(solution)/shard_map/ppermute | solution.py:29
  (6 other events, 30.7 us)

commit v4 on v3

--- a/solution.py
+++ b/solution.py
@@ -15,8 +15,9 @@
 HALF = WIN // 2
 BAND = WIN_ROWS * WIN_COLS * WIN
 ROW = WIN_COLS * WIN
-VMEM_BYTES = 48 * 1024 * 1024
-LARGE_VMEM_BYTES = 58 * 1024 * 1024
+NEAR_VMEM_BYTES = 48 * 1024 * 1024
+LARGE_VMEM_BYTES = 56 * 1024 * 1024
+HELD_ROWS = 12 * 1024
 SMALL_VMEM_BYTES = 12 * 1024 * 1024
 
 BESIDE, ACROSS = 1, 2
@@ -131,10 +132,8 @@
 
 
 def turned_biases(bias_ref, turned_ref):
-    @pl.when(pl.program_id(0) == 0)
-    def _():
-        for h in range(bias_ref.shape[0]):
-            turned_ref[h] = bias_ref[h].T
+    for h in range(bias_ref.shape[0]):
+        turned_ref[h] = bias_ref[h].T
 
 
 def counts_of(counts_ref, block, column):
@@ -148,188 +147,201 @@
     ).astype(jnp.bfloat16)
 
 
-def near_kernel(
-    start, steps, head_ref, counts_ref, act_ref, delta_ref, weight_ref, bias_ref, *rest
-):
-    *outs, held_ref = rest[-5 - steps : -4]
-    turned_ref, parts_ref, grads_ref, sems = rest[-4:]
+def near_kernel(start, steps, head_ref, counts_ref, weight_ref, bias_ref, delta_ref, act_ref, *rest):
+    *outs, held_ref = rest[-6 - steps : -5]
+    turned_ref, rows_ref, parts_ref, grads_ref, sems = rest[-5:]
+    tokens = 2 * WIN
+
+    def fetch(k):
+        block = block_at(head_ref[0], start + k)
+        return pltpu.make_async_copy(
+            act_ref.at[pl.ds(2 * block, 2), pl.ds(HALF, WIN), :], rows_ref.at[k], sems.at[2, k]
+        )
+
+    def put(k):
+        held_rows = held_ref.at[pl.ds((start + k) * tokens, tokens), :]
+        return [
+            pltpu.make_async_copy(parts_ref.at[k], outs[k], sems.at[0, k]),
+            pltpu.make_async_copy(grads_ref.at[k], held_rows, sems.at[1, k]),
+        ]
+
+    fetch(0).start()
     turned_biases(bias_ref, turned_ref)
-    at = [slice(i * ROW + HALF, i * ROW + HALF + WIN) for i in range(2)]
-    rows = jnp.concatenate([act_ref[s, :] for s in at], axis=0)
-    delta = jnp.concatenate([delta_ref[s, :] for s in at], axis=0)
-    weight = weight_ref[...]
-    proj = jnp.dot(rows, weight, preferred_element_type=jnp.float32)
-    step = pl.program_id(0)
-    counts = counts_of(counts_ref, block_at(head_ref[0], step + start), 0)
-    grads = attend(proj, delta, turned_ref, counts)
-    grads_ref[step] = grads
-    parts_ref[step] = part_of(grads, weight)
+    for k in range(steps):
+        block = block_at(head_ref[0], start + k)
+        base = pl.multiple_of(block * 2 * ROW, 2 * ROW)
+        delta = [delta_ref[pl.ds(base + i * ROW + HALF, WIN), :] for i in range(2)]
+        fetch(k).wait()
+        if k + 1 < steps:
+            fetch(k + 1).start()
+        weight = weight_ref[...]
+        rows = rows_ref[k].reshape(tokens, weight.shape[0])
+        proj = jnp.dot(rows, weight, preferred_element_type=jnp.float32)
+        counts = counts_of(counts_ref, block, 0)
+        grads = attend(proj, jnp.concatenate(delta, axis=0), turned_ref, counts)
+        grads_ref[k] = grads
+        parts_ref[k] = part_of(grads, weight)
+        for copy in put(k):
+            copy.start()
+    for k in range(steps):
+        for copy in put(k):
+            copy.wait()
+
+
+VMEM = pl.BlockSpec(memory_space=pltpu.VMEM)
+SMEM = pl.BlockSpec(memory_space=pltpu.SMEM)
+ANYWHERE = pl.BlockSpec(memory_space=pl.ANY)
+
+
+def near_windows(start, steps, head, counts, act, delta, weight, bias, held):
+    width, dim = weight.shape[1], act.shape[1]
     tokens = 2 * WIN
-    copies = [
-        [
-            pltpu.make_async_copy(parts_ref.at[i], outs[i], sems.at[0, i]),
-            pltpu.make_async_copy(
-                grads_ref.at[i], held_ref.at[pl.ds((start + i) * tokens, tokens), :], sems.at[1, i]
-            ),
-        ]
-        for i in range(steps)
-    ]
-    for i in range(steps):
-
-        @pl.when(step == i)
-        def _():
-            for copy in copies[i]:
-                copy.start()
-
-    @pl.when(step == steps - 1)
-    def _():
-        for copy in sum(copies, []):
-            copy.wait()
-
-
-def near_windows(start, steps, head, counts, act, delta, weight, bias, held):
-    width, dim, delta_width = weight.shape[1], act.shape[1], delta.shape[1]
-    blocked = lambda j, head_ref, counts_ref: (block_at(head_ref[0], j + start), 0)
-    whole2 = lambda j, head_ref, counts_ref: (0, 0)
-    whole3 = lambda j, head_ref, counts_ref: (0, 0, 0)
-    tokens = 2 * WIN
-    operands = [act, delta, weight, bias]
-    specs = [
-        pl.BlockSpec((2 * ROW, dim), blocked),
-        pl.BlockSpec((2 * ROW, delta_width), blocked),
-        pl.BlockSpec(weight.shape, whole2),
-        pl.BlockSpec(bias.shape, whole3),
-    ]
+    operands = [head, counts, weight, bias, delta, act.reshape(WIN_ROWS, ROW, dim)]
+    specs = [SMEM, SMEM, VMEM, VMEM, VMEM, ANYWHERE]
     aliases = {}
     if held is not None:
-        aliases = {2 + len(operands): steps}
+        aliases = {len(operands): steps}
         operands.append(held)
-        specs.append(pl.BlockSpec(memory_space=pl.ANY))
+        specs.append(ANYWHERE)
     part = jax.ShapeDtypeStruct((tokens, dim), jnp.bfloat16)
     return pl.pallas_call(
         functools.partial(near_kernel, start, steps),
-        grid_spec=pltpu.PrefetchScalarGridSpec(
-            num_scalar_prefetch=2,
-            grid=(steps,),
-            in_specs=specs,
-            out_specs=[pl.BlockSpec(memory_space=pl.ANY)] * (steps + 1),
-            scratch_shapes=[
-                pltpu.VMEM(bias.shape, bias.dtype),
-                pltpu.VMEM((steps, tokens, dim), jnp.bfloat16),
-                pltpu.VMEM((steps, tokens, width), jnp.bfloat16),
-                pltpu.SemaphoreType.DMA((2, steps)),
-            ],
-        ),
-        out_shape=[part] * steps + [jax.ShapeDtypeStruct((4 * tokens, width), jnp.bfloat16)],
+        in_specs=specs,
+        out_specs=[ANYWHERE] * (steps + 1),
+        scratch_shapes=[
+            pltpu.VMEM(bias.shape, bias.dtype),
+            pltpu.VMEM((steps, 2, WIN, dim), jnp.bfloat16),
+            pltpu.VMEM((steps, tokens, dim), jnp.bfloat16),
+            pltpu.VMEM((steps, tokens, width), jnp.bfloat16),
+            pltpu.SemaphoreType.DMA((3, steps)),
+        ],
+        out_shape=[part] * steps + [jax.ShapeDtypeStruct((HELD_ROWS, width), jnp.bfloat16)],
         input_output_aliases=aliases,
-        compiler_params=pltpu.CompilerParams(vmem_limit_bytes=VMEM_BYTES if start == 0 else LARGE_VMEM_BYTES),
+        compiler_params=pltpu.CompilerParams(vmem_limit_bytes=NEAR_VMEM_BYTES),
         cost_estimate=COST,
         name="near_windows",
-    )(head, counts, *operands)
+    )(*operands)
 
 
 def far_kernel(
-    head_ref, core_ref, counts_ref, act_ref, delta_ref, far_ref, weight_ref, bias_ref, held_ref, *rest
+    head_ref, core_ref, counts_ref, weight_ref, bias_ref, delta_ref, act_ref, far_ref, held_ref, *rest
 ):
-    outs, send_ref, keep_ref, turned_ref, total_ref, parts_ref, sems = rest[:7], *rest[7:]
-    turned_biases(bias_ref, turned_ref)
-    dim, delta_width = act_ref.shape[1], delta_ref.shape[1]
-    step = pl.program_id(0)
-
-    def mixed(near_ref, low, high):
-        pieces = []
-        for i in range(2):
-            pieces.append(near_ref[(i + 1) * ROW - HALF : (i + 1) * ROW, :])
-            pieces.append(far_ref[i * HALF : (i + 1) * HALF, low:high])
-        return jnp.concatenate(pieces, axis=0)
-
-    rows = mixed(act_ref, 0, dim)
-    delta = mixed(delta_ref, dim, dim + delta_width)
-    weight = weight_ref[...]
-    proj = jnp.dot(rows, weight, preferred_element_type=jnp.float32)
-    counts = counts_of(counts_ref, block_at(head_ref[0], step), 1)
-    grads = attend(proj, delta, turned_ref, counts)
-    part = part_of(grads, weight)
-    parts_ref[step, :HALF] = part[HALF:WIN]
-    parts_ref[step, HALF:WIN] = part[WIN + HALF :]
-    parts_ref[step, WIN : WIN + HALF] = part[:HALF]
-    parts_ref[step, WIN + HALF :] = part[WIN : WIN + HALF]
+    outs, send_ref, keep_ref, *scratch = rest[:7], *rest[7:]
+    turned_ref, total_ref, rows_ref, grads_ref, halo_ref, parts_ref, in_sems, out_sems = scratch
+    dim, delta_width = act_ref.shape[2], delta_ref.shape[1]
+
+    def fetch(k):
+        block = block_at(head_ref[0], k)
+        copies = [
+            (
+                act_ref.at[pl.ds(2 * block, 2), pl.ds(HALF, ROW - HALF), :],
+                rows_ref.at[k, :, pl.ds(0, ROW - HALF), :],
+            ),
+            (
+                far_ref.at[pl.ds(2 * block, 2), :, pl.ds(0, dim)],
+                rows_ref.at[k, :, pl.ds(ROW - HALF, HALF), :],
+            ),
+            (far_ref.at[pl.ds(2 * block, 2), :, pl.ds(dim, delta_width)], halo_ref.at[k]),
+            (held_ref.at[pl.ds(2 * k, 2), :, :], grads_ref.at[k, :, pl.ds(0, WIN), :]),
+        ]
+        return [
+            pltpu.make_async_copy(source, target, in_sems.at[k, i])
+            for i, (source, target) in enumerate(copies)
+        ]
+
     halves = [pl.ds(0, WIN), pl.ds(WIN, WIN)]
-    copies = [[pltpu.make_async_copy(parts_ref.at[0], outs[0], sems.at[0, 0])]]
-    copies += [
+    put = [[pltpu.make_async_copy(parts_ref.at[0], outs[0], out_sems.at[0, 0])]]
+    put += [
         [
-            pltpu.make_async_copy(parts_ref.at[i, halves[j], :], outs[2 * i - 1 + j], sems.at[i, j])
+            pltpu.make_async_copy(parts_ref.at[k, halves[j], :], outs[2 * k - 1 + j], out_sems.at[k, j])
             for j in range(2)
         ]
-        for i in range(1, 4)
+        for k in range(1, 4)
     ]
-    for i in range(4):
-
-        @pl.when(step == i)
-        def _():
-            for copy in copies[i]:
+    for copy in fetch(0):
+        copy.start()
+    turned_biases(bias_ref, turned_ref)
+    for k in range(4):
+        block = block_at(head_ref[0], k)
+        base = pl.multiple_of(block * 2 * ROW, 2 * ROW)
+        for copy in fetch(k):
+            copy.wait()
+        if k < 3:
+            for copy in fetch(k + 1):
                 copy.start()
-
-    near_rows = [act_ref[i * ROW + HALF : i * ROW + HALF + WIN, :] for i in range(2)]
-    all_rows = jnp.concatenate(near_rows + [rows], axis=0)
-    all_grads = jnp.concatenate([held_ref[...], grads], axis=0)
-    @pl.when(step == 0)
-    def _():
-        total_ref[...] = jnp.zeros_like(total_ref)
-
-    total_ref[...] += lax.dot_general(
-        all_rows, all_grads, (((0,), (0,)), ((), ())), preferred_element_type=jnp.float32
-    )
-
-    @pl.when(step == 3)
-    def _():
-        half = dim // 2
-        core = core_ref[0]
-        keep_ref[...] = total_ref[pl.ds(pl.multiple_of(core * half, half), half), :]
-        send_ref[...] = total_ref[pl.ds(pl.multiple_of((1 - core) * half, half), half), :].astype(
-            jnp.bfloat16
+        delta = []
+        for i in range(2):
+            delta += [delta_ref[pl.ds(base + (i + 1) * ROW - HALF, HALF), :], halo_ref[k, i]]
+        weight = weight_ref[...]
+        rows = rows_ref[k, :, WIN:, :].reshape(2 * WIN, dim)
+        proj = jnp.dot(rows, weight, preferred_element_type=jnp.float32)
+        counts = counts_of(counts_ref, block, 1)
+        grads = attend(proj, jnp.concatenate(delta, axis=0), turned_ref, counts)
+        grads_ref[k, 0, WIN:, :] = grads[:WIN]
+        grads_ref[k, 1, WIN:, :] = grads[WIN:]
+        part = part_of(grads, weight)
+        parts_ref[k, :HALF] = part[HALF:WIN]
+        parts_ref[k, HALF:WIN] = part[WIN + HALF :]
+        parts_ref[k, WIN : WIN + HALF] = part[:HALF]
+        parts_ref[k, WIN + HALF :] = part[WIN : WIN + HALF]
+        for copy in put[k]:
+            copy.start()
+        product = lax.dot_general(
+            rows_ref[k].reshape(2 * ROW, dim),
+            grads_ref[k].reshape(2 * ROW, weight.shape[1]),
+            (((0,), (0,)), ((), ())),
+            preferred_element_type=jnp.float32,
         )
-        for copy in sum(copies, []):
-            copy.wait()
+        if k:
+            total_ref[...] += product
+        else:
+            total_ref[...] = product
+    half = dim // 2
+    core = core_ref[0]
+    send_ref[...] = total_ref[pl.ds(pl.multiple_of((1 - core) * half, half), half), :].astype(
+        jnp.bfloat16
+    )
+    keep_ref[...] = total_ref[pl.ds(pl.multiple_of(core * half, half), half), :]
+    for copy in sum(put, []):
+        copy.wait()
 
 
 def far_windows(head, core, counts, act, delta, far, weight, bias, held):
     width, dim, delta_width = weight.shape[1], act.shape[1], delta.shape[1]
-    blocked = lambda j, head_ref, core_ref, counts_ref: (block_at(head_ref[0], j), 0)
-    whole2 = lambda j, head_ref, core_ref, counts_ref: (0, 0)
-    whole3 = lambda j, head_ref, core_ref, counts_ref: (0, 0, 0)
     parts = [
         jax.ShapeDtypeStruct((tokens, dim), jnp.bfloat16)
         for tokens in (2 * WIN, WIN, WIN, WIN, WIN, WIN, WIN)
     ]
     return pl.pallas_call(
         far_kernel,
-        grid_spec=pltpu.PrefetchScalarGridSpec(
-            num_scalar_prefetch=3,
-            grid=(4,),
-            in_specs=[
-                pl.BlockSpec((2 * ROW, dim), blocked),
-                pl.BlockSpec((2 * ROW, delta_width), blocked),
-                pl.BlockSpec((WIN, dim + delta_width), blocked),
-                pl.BlockSpec(weight.shape, whole2),
-                pl.BlockSpec(bias.shape, whole3),
-                pl.BlockSpec((2 * WIN, width), lambda j, head_ref, core_ref, counts_ref: (j, 0)),
-            ],
-            out_specs=[pl.BlockSpec(memory_space=pl.ANY)] * 7
-            + [pl.BlockSpec((dim // 2, width), whole2)] * 2,
-            scratch_shapes=[
-                pltpu.VMEM(bias.shape, bias.dtype),
-                pltpu.VMEM((dim, width), jnp.float32),
-                pltpu.VMEM((4, 2 * WIN, dim), jnp.bfloat16),
-                pltpu.SemaphoreType.DMA((4, 2)),
-            ],
-        ),
+        in_specs=[SMEM] * 3 + [VMEM] * 3 + [ANYWHERE] * 3,
+        out_specs=[ANYWHERE] * 7 + [VMEM] * 2,
+        scratch_shapes=[
+            pltpu.VMEM(bias.shape, bias.dtype),
+            pltpu.VMEM((dim, width), jnp.float32),
+            pltpu.VMEM((4, 2, ROW, dim), jnp.bfloat16),
+            pltpu.VMEM((4, 2, ROW, width), jnp.bfloat16),
+            pltpu.VMEM((4, 2, HALF, delta_width), jnp.bfloat16),
+            pltpu.VMEM((4, 2 * WIN, dim), jnp.bfloat16),
+            pltpu.SemaphoreType.DMA((4, 4)),
+            pltpu.SemaphoreType.DMA((4, 2)),
+        ],
         out_shape=parts
         + [jax.ShapeDtypeStruct((dim // 2, width), dtype) for dtype in (jnp.bfloat16, jnp.float32)],
         compiler_params=pltpu.CompilerParams(vmem_limit_bytes=LARGE_VMEM_BYTES),
         cost_estimate=COST,
         name="far_windows",
-    )(head, core, counts, act, delta, far, weight, bias, held)
+    )(
+        head,
+        core,
+        counts,
+        weight,
+        bias,
+        delta,
+        act.reshape(WIN_ROWS, ROW, dim),
+        far.reshape(WIN_ROWS, HALF, dim + delta_width),
+        held.reshape(-1, WIN, width),
+    )
 
 
 def split_kernel(chip_ref, mine_ref, theirs_ref, own_ref, *outs):
@@ -401,8 +413,9 @@
     first, held = near_windows(0, 1, head, key_counts, *here, None)
     in_near = [hop(first, BESIDE)]
     *near, held = near_windows(1, 3, head, key_counts, *here, held)
-    in_near.append(hop(near[0], BESIDE))
-    in_near.append(hop(after(add(near[1], in_near[0]), far), ACROSS))
+    out_near = add(near[1], after(in_near[0], far))
+    in_near.append(hop(after(near[0], out_near), BESIDE))
+    in_near.append(hop(out_near, ACROSS))
     far = far.reshape(WIN_ROWS * HALF, far.shape[2])
     *parts, outgoing, mine = far_windows(
         head, core, key_counts, activations, attn_grad, far, qkv_weight, pos_bias, held
@@ -432,7 +445,7 @@
     done = small(functools.partial(join_kernel, scale), low, after(chip, out_this), own, *came)
     others = [swapped(done, 2 * (i + 1)) for i in range(3)]
 
-    next_sum = add(next_d, more_next, over_next)
+    next_sum = last_sum(10_000_000_000, next_d, more_next, over_next)
     back = passed_along(next_sum, "lon", 1)
     half = jax.ShapeDtypeStruct((dim // 2, width), jnp.bfloat16)
     gathered = small(gather_kernel, half, chip, done, *others)
@@ -440,12 +453,31 @@
     weight_grad = small(
         widen_kernel, jax.ShapeDtypeStruct((dim, width), jnp.float32), core, gathered, other_half
     )
-    this_sum = add(this_d, more_this, over_this)
+    this_sum = last_sum(10_000_000_000, this_d, more_this, over_this)
     input_grad = jnp.concatenate(
-        [x.reshape(2, -1, dim) for x in (back, near_sum, this_sum)], axis=1
+        [x.reshape(2, -1, dim) for x in (after(back, weight_grad), near_sum, this_sum)], axis=1
     ).reshape(2 * ROW, dim)
 
     return (input_grad, weight_grad)
+
+
+def sum_kernel(*refs):
+    total = refs[0][...].astype(jnp.float32)
+    for ref in refs[1:-1]:
+        total = total + ref[...].astype(jnp.float32)
+    refs[-1][...] = total.astype(refs[-1].dtype)
+
+
+def last_sum(flops, *parts):
+    return pl.pallas_call(
+        sum_kernel,
+        in_specs=[VMEM] * len(parts),
+        out_specs=VMEM,
+        out_shape=jax.ShapeDtypeStruct(parts[0].shape, parts[0].dtype),
+        compiler_params=pltpu.CompilerParams(vmem_limit_bytes=SMALL_VMEM_BYTES),
+        cost_estimate=pl.CostEstimate(flops=flops, bytes_accessed=1_000_000, transcendentals=0),
+        name="last_sum",
+    )(*parts)
 
 
 def assemble(block_grid, far_rows):

time: 95.7 us -> 91.7 us (0.958)
  waiting for transfers between devices: 27.2 us -> 24.6 us
  local copies, waits for them, and re-layouts: 1.19 us -> 0.05 us
    ppermute x8, waiting for transfers between devices: 21.3 us -> 16.9 us  [hop(): lax.ppermute(x, 'head', [(i, i ^ bits) for i in range(lax.axis_size('head...]
    ppermute x2, waiting for transfers between devices: 0.37 us -> 1.51 us  [passed_along(): lax.ppermute(shard, axis, [(i, (i + by) % size) for i in range(size)])]
    unnamed x24 -> x22, local copies, waits for them, and re-layouts: 1.19 us -> 0.05 us
    pallas_call x3 -> x5, Pallas kernels: 29.2 us -> 28.8 us  [the longest x1 16.4 us: far_windows(): pl.pallas_call(far_kernel, in_specs=[SMEM] * 3 + [VMEM] * 3 + [ANYWHERE]...]
    convert_element_type x5 -> x3, other arithmetic: 3.35 us -> 2.99 us  [add(): return total.astype(jnp.bfloat16)]
  transfers between devices with their start and end apart: 18 -> 18, of which waited for: 9 -> 10; matrix products, arithmetic and copies ran while one was open for 4% -> 3% of each run, Pallas kernels for 31% -> 34%
where the time goes in v4:
time: 91.7 us; the launch traced here: 91.4 us
  Pallas kernels  33.5 us (37%)
  starting transfers between devices  28.4 us (31%)
  waiting for transfers between devices  24.6 us (27%)
  other arithmetic  4.03 us (4%)
    ppermute x8, waiting for transfers between devices, hop(): lax.ppermute(x, 'head', [(i, i ^ bits) for i in range(lax.axis_size('head...  16.9 us
    ppermute x8, starting transfers between devices, hop(): lax.ppermute(x, 'head', [(i, i ^ bits) for i in range(lax.axis_size('head...  16.5 us
    pallas_call x1, Pallas kernels, far_windows(): pl.pallas_call(far_kernel, in_specs=[SMEM] * 3 + [VMEM] * 3 + [ANYWHERE]...  16.4 us
    pallas_call x2, Pallas kernels, near_windows(): pl.pallas_call(functools.partial(near_kernel, start, steps), in_specs=spe...  12.3 us
    ppermute x8, starting transfers between devices, swapped(): return lax.ppermute(shard, 'lon', [(i, i ^ bits) for i in range(size)])  8.39 us
    ppermute x8, waiting for transfers between devices, swapped(): return lax.ppermute(shard, 'lon', [(i, i ^ bits) for i in range(size)])  6.18 us
    ppermute x2, starting transfers between devices, passed_along(): lax.ppermute(shard, axis, [(i, (i + by) % size) for i in range(size)])  3.44 us
    convert_element_type x3, other arithmetic, add(): return total.astype(jnp.bfloat16)  2.99 us
  transfers between devices with their start and end apart: 18, of which 10 were waited for; matrix products, arithmetic and copies ran while one was open for 3% of the time, Pallas kernels for 34%

profile of v4, /device:TPU:0, one launch (start us, length us, event | category | flops | bytes accessed | tf_op | source)
XLA Modules:
  0.0 91.4 jit_solution(14826674140100146002)
XLA Ops:
  0.7 2.5 %first_rows.1 = bf16[8,64,1280]{2,1,0:T(8,128)(2,1)} custom-call(bf16[8,256,1024]{2,1,0:T(8,128)(2,1)} %bitcast.13, bf16[8,256,256]{2,1,0:T(8,128)(2,1)} %bitcast.10), custom_call_target="tpu_custom_call" | custom-call | tf_op jit(solution)/shard_map/first_rows/pallas_call | solution.py:124
  3.2 3.4 %collective-permute-start = (bf16[8,64,1280]{2,1,0:T(8,128)(2,1)}, bf16[8,64,1280]{2,1,0:T(8,128)(2,1)}, u32[]{:S(2)}, u32[]{:S(2)}) collective-permute-start(bf16[8,64,1280]{2,1,0:T(8,128)(2,1)} %first_rows.1), channel_id=1, source_target_pairs={{0,28},{4,0},{8,4},{12,8},{16,12},{20,16},{24,20},{28,24},{1,29},{... | collective-permute-start | bytes 3932168 | tf_op jit(solution)/shard_map/ppermute | solution.py:30
  6.6 4.2 %near_windows.2 = (bf16[256,1024]{1,0:T(8,128)(2,1)S(1)}, bf16[12288,768]{1,0:T(8,128)(2,1)}) custom-call(s32[1]{0:T(128)} %bitcast.head_ref, s32[16]{0:T(128)S(1)} %copy-done.4, bf16[1024,768]{1,0:T(8,128)(2,1)S(1)} %copy-done.1, f32[4,128,128]{2,1,0:T(8,128)S(1)} %copy-done.2, bf16[2048,256]{1,0:T(8,128)(2,1)S(1)} %copy-done, bf16[8,256,1024]{2,1,0:T(8,128)(2,1)} %bitcast.14), custom_call_target="tpu_custom_call" | custom-call | flops 1000000 | bytes 100000 | tf_op jit(solution)/shard_map/near_windows/pallas_call | solution.py:207
  10.8 1.6 %collective-permute-start.3 = (bf16[256,1024]{1,0:T(8,128)(2,1)S(1)}, bf16[256,1024]{1,0:T(8,128)(2,1)S(1)}, u32[]{:S(2)}, u32[]{:S(2)}) collective-permute-start(bf16[256,1024]{1,0:T(8,128)(2,1)S(1)} %get-tuple-element.37), channel_id=1, source_target_pairs={{0,1},{1,0},{2,3},{3,2},{4,5},{5,4},{6,7},{7,6},{8,9},{9,8},{10,11... | collective-permute-start | bytes 1572872 | tf_op jit(solution)/shard_map/ppermute | solution.py:409
  12.4 8.1 %near_windows.3 = (bf16[256,1024]{1,0:T(8,128)(2,1)}, bf16[256,1024]{1,0:T(8,128)(2,1)S(1)}, bf16[256,1024]{1,0:T(8,128)(2,1)S(1)}, bf16[12288,768]{1,0:T(8,128)(2,1)}) custom-call(s32[1]{0:T(128)} %bitcast.head_ref, s32[16]{0:T(128)S(1)} %copy-done.4, bf16[1024,768]{1,0:T(8,128)(2,1)S(1)} %copy-done.1, ...), custom_call_target="tpu_custom_call", output_to_operand_aliasing={{3}: (6, {})} | custom-call | flops 1000000 | bytes 100000 | tf_op jit(solution)/shard_map/near_windows/pallas_call | solution.py:207
  20.5 2.6 %collective-permute-done.3 = bf16[256,1024]{1,0:T(8,128)(2,1)S(1)} collective-permute-done((bf16[256,1024]{1,0:T(8,128)(2,1)S(1)}, bf16[256,1024]{1,0:T(8,128)(2,1)S(1)}, u32[]{:S(2)}, u32[]{:S(2)}) %collective-permute-start.3) | collective-permute-done | bytes 524320 | tf_op jit(solution)/shard_map/ppermute | solution.py:409
  23.3 1.8 %collective-permute-start.4 = (bf16[256,1024]{1,0:T(8,128)(2,1)}, bf16[256,1024]{1,0:T(8,128)(2,1)}, u32[]{:S(2)}, u32[]{:S(2)}) collective-permute-start(bf16[256,1024]{1,0:T(8,128)(2,1)} %get-tuple-element.39), channel_id=1, source_target_pairs={{0,1},{1,0},{2,3},{3,2},{4,5},{5,4},{6,7},{7,6},{8,9},{9,8},{10,11... | collective-permute-start | bytes 1572872 | tf_op jit(solution)/shard_map/ppermute | solution.py:409
  25.1 2.6 %collective-permute-start.5 = (bf16[256,1024]{1,0:T(8,128)(2,1)S(1)}, bf16[256,1024]{1,0:T(8,128)(2,1)}, u32[]{:S(2)}, u32[]{:S(2)}) collective-permute-start(bf16[256,1024]{1,0:T(8,128)(2,1)S(1)} %add_convert_fusion.1), channel_id=1, source_target_pairs={{0,2},{1,3},{2,0},{3,1},{4,6},{5,7},{6,4},{7,5},{8,10},{9,11},{10,... | collective-permute-start | bytes 1572872 | tf_op jit(solution)/shard_map/ppermute | solution.py:409
  27.7 16.4 %far_windows.1 = (bf16[256,1024]{1,0:T(8,128)(2,1)}, bf16[128,1024]{1,0:T(8,128)(2,1)}, bf16[128,1024]{1,0:T(8,128)(2,1)}, bf16[128,1024]{1,0:T(8,128)(2,1)}, bf...) custom-call(s32[1]{0:T(128)} %bitcast.head_ref, ...), custom_call_target="tpu_custom_call" | custom-call | flops 1000000 | bytes 100000 | tf_op jit(solution)/shard_map/far_windows/pallas_call | solution.py:315
  44.7 3.1 %collective-permute-done.4 = bf16[256,1024]{1,0:T(8,128)(2,1)} collective-permute-done((bf16[256,1024]{1,0:T(8,128)(2,1)}, bf16[256,1024]{1,0:T(8,128)(2,1)}, u32[]{:S(2)}, u32[]{:S(2)}) %collective-permute-start.4) | collective-permute-done | bytes 524320 | tf_op jit(solution)/shard_map/ppermute | solution.py:409
  48.0 1.5 %add_convert_fusion = bf16[256,1024]{1,0:T(8,128)(2,1)S(1)} fusion(bf16[256,1024]{1,0:T(8,128)(2,1)} %collective-permute-done.5, bf16[256,1024]{1,0:T(8,128)(2,1)} %collective-permute-done.4, bf16[256,1024]{1,0:T(8,128)(2,1)S(1)} %get-tuple-element.34), kind=kLoop, calls=%fused_computation.1 | loop fusion | flops 1572864 | bytes 2097152 | tf_op jit(solution)/shard_map/convert_element_type | solution.py:398
  49.7 3.2 %collective-permute-start.7 = (bf16[128,768]{1,0:T(8,128)(2,1)S(1)}, bf16[128,768]{1,0:T(8,128)(2,1)S(1)}, u32[]{:S(2)}, u32[]{:S(2)}) collective-permute-start(bf16[128,768]{1,0:T(8,128)(2,1)S(1)} %get-tuple-element.44), channel_id=1, source_target_pairs={{0,8},{4,12},{8,0},{12,4},{16,24},{20,28},{24,16},{28,20},{1,9},{5... | collective-permute-start | bytes 589832 | tf_op jit(solution)/shard_map/ppermute | solution.py:35
  52.9 1.5 %collective-permute-start.8 = (bf16[128,768]{1,0:T(8,128)(2,1)S(1)}, bf16[128,768]{1,0:T(8,128)(2,1)S(1)}, u32[]{:S(2)}, u32[]{:S(2)}) collective-permute-start(bf16[128,768]{1,0:T(8,128)(2,1)S(1)} %get-tuple-element.45), channel_id=1, source_target_pairs={{0,16},{4,20},{8,24},{12,28},{16,0},{20,4},{24,8},{28,12},{1,17},{... | collective-permute-start | bytes 589832 | tf_op jit(solution)/shard_map/ppermute | solution.py:35
  54.4 3.4 %collective-permute-start.1 = (bf16[128,1024]{1,0:T(8,128)(2,1)S(1)}, bf16[128,1024]{1,0:T(8,128)(2,1)S(1)}, u32[]{:S(2)}, u32[]{:S(2)}) collective-permute-start(bf16[128,1024]{1,0:T(8,128)(2,1)S(1)} %copy-done.10), channel_id=1, source_target_pairs={{0,1},{1,0},{2,3},{3,2},{4,5},{5,4},{6,7},{7,6},{8,9},{9,8},{10,11... | collective-permute-start | bytes 786440 | tf_op jit(solution)/shard_map/ppermute | solution.py:409
  57.8 1.5 %collective-permute-done.2 = bf16[256,1024]{1,0:T(8,128)(2,1)} collective-permute-done((bf16[256,1024]{1,0:T(8,128)(2,1)}, bf16[256,1024]{1,0:T(8,128)(2,1)}, u32[]{:S(2)}, u32[]{:S(2)}) %collective-permute-start.2) | collective-permute-done | bytes 524320 | tf_op jit(solution)/shard_map/ppermute | solution.py:409
  59.3 2.7 %collective-permute-done.8.b_ref = bf16[128,768]{1,0:T(8,128)(2,1)S(1)} collective-permute-done((bf16[128,768]{1,0:T(8,128)(2,1)S(1)}, bf16[128,768]{1,0:T(8,128)(2,1)S(1)}, u32[]{:S(2)}, u32[]{:S(2)}) %collective-permute-start.8) | collective-permute-done | bytes 196640 | tf_op jit(solution)/shard_map/ppermute | solution.py:35
  63.3 2.6 %collective-permute-start.10 = (bf16[128,1024]{1,0:T(8,128)(2,1)S(1)}, bf16[128,1024]{1,0:T(8,128)(2,1)S(1)}, u32[]{:S(2)}, u32[]{:S(2)}) collective-permute-start(bf16[128,1024]{1,0:T(8,128)(2,1)S(1)} %get-tuple-element.55), channel_id=1, source_target_pairs={{0,2},{1,3},{2,0},{3,1},{4,6},{5,7},{6,4},{7,5},{8,10},{9,11},{10,... | collective-permute-start | bytes 786440 | tf_op jit(solution)/shard_map/ppermute | solution.py:409
  66.8 1.5 %collective-permute-start.13 = (bf16[128,768]{1,0:T(8,128)(2,1)S(1)}, bf16[128,768]{1,0:T(8,128)(2,1)S(1)}, u32[]{:S(2)}, u32[]{:S(2)}) collective-permute-start(bf16[128,768]{1,0:T(8,128)(2,1)S(1)} %shard_map.69.own_ref), channel_id=1, source_target_pairs={{0,16},{4,20},{8,24},{12,28},{16,0},{20,4},{24,8},{28,12},{1,17},{... | collective-permute-start | bytes 589832 | tf_op jit(solution)/shard_map/ppermute | solution.py:35
  69.6 2.2 %collective-permute-done.12.a_ref = bf16[128,768]{1,0:T(8,128)(2,1)S(1)} collective-permute-done((bf16[128,768]{1,0:T(8,128)(2,1)S(1)}, bf16[128,768]{1,0:T(8,128)(2,1)S(1)}, u32[]{:S(2)}, u32[]{:S(2)}) %collective-permute-start.12) | collective-permute-done | bytes 196640 | tf_op jit(solution)/shard_map/ppermute | solution.py:35
  73.8 3.2 %collective-permute-start.16 = (bf16[128,1024]{1,0:T(8,128)(2,1)S(1)}, bf16[128,1024]{1,0:T(8,128)(2,1)S(1)}, u32[]{:S(2)}, u32[]{:S(2)}) collective-permute-start(bf16[128,1024]{1,0:T(8,128)(2,1)S(1)} %copy-done.9), channel_id=1, source_target_pairs={{0,1},{1,0},{2,3},{3,2},{4,5},{5,4},{6,7},{7,6},{8,9},{9,8},{10,11... | collective-permute-start | bytes 786440 | tf_op jit(solution)/shard_map/ppermute | solution.py:409
  77.1 6.3 %collective-permute-done.10.refs_2_ = bf16[128,1024]{1,0:T(8,128)(2,1)S(1)} collective-permute-done((bf16[128,1024]{1,0:T(8,128)(2,1)S(1)}, bf16[128,1024]{1,0:T(8,128)(2,1)S(1)}, u32[]{:S(2)}, u32[]{:S(2)}) %collective-permute-start.10) | collective-permute-done | bytes 262176 | tf_op jit(solution)/shard_map/ppermute | solution.py:409
  83.6 3.2 %collective-permute-done.16.refs_1_ = bf16[128,1024]{1,0:T(8,128)(2,1)S(1)} collective-permute-done((bf16[128,1024]{1,0:T(8,128)(2,1)S(1)}, bf16[128,1024]{1,0:T(8,128)(2,1)S(1)}, u32[]{:S(2)}, u32[]{:S(2)}) %collective-permute-start.16) | collective-permute-done | bytes 262176 | tf_op jit(solution)/shard_map/ppermute | solution.py:409
  86.9 1.9 %shard_map.71 = f32[1024,768]{1,0:T(8,128)} custom-call(s32[1]{0:T(128)} %bitcast.1.core_ref, bf16[512,768]{1,0:T(8,128)(2,1)S(1)} %shard_map.70.mine_ref, bf16[512,768]{1,0:T(8,128)(2,1)S(1)} %collective-permute-done.15.theirs_ref), custom_call_target="tpu_custom_call" | custom-call | flops 1000000 | bytes 100000 | tf_op jit(solution)/shard_map/pallas_call | solution.py:380
  88.8 1.5 %collective-permute-done.11 = bf16[128,1024]{1,0:T(8,128)(2,1)S(1)} collective-permute-done((bf16[128,1024]{1,0:T(8,128)(2,1)S(1)}, bf16[128,1024]{1,0:T(8,128)(2,1)S(1)}, u32[]{:S(2)}, u32[]{:S(2)}) %collective-permute-start.11) | collective-permute-done | bytes 262176 | tf_op jit(solution)/shard_map/ppermute | solution.py:30
  (48 shorter events, 8.1 us)
Async XLA Ops:
  0.6 5.9 %copy-start = (bf16[2048,256]{1,0:T(8,128)(2,1)S(1)}, bf16[2048,256]{1,0:T(8,128)(2,1)}, u32[]{:S(2)}) copy-start(bf16[2048,256]{1,0:T(8,128)(2,1)} %delta_ref.5) | copy-start | bytes 3145732
  3.2 20.0 %collective-permute-start = (bf16[8,64,1280]{2,1,0:T(8,128)(2,1)}, bf16[8,64,1280]{2,1,0:T(8,128)(2,1)}, u32[]{:S(2)}, u32[]{:S(2)}) collective-permute-start(bf16[8,64,1280]{2,1,0:T(8,128)(2,1)} %first_rows.1), channel_id=1, source_target_pairs={{0,28},{4,0},{8,4},{12,8},{16,12},{20,16},{24,20},{28,24},{1,29},{... | collective-permute-start | bytes 3932168 | tf_op jit(solution)/shard_map/ppermute | solution.py:30
  10.8 12.4 %collective-permute-start.3 = (bf16[256,1024]{1,0:T(8,128)(2,1)S(1)}, bf16[256,1024]{1,0:T(8,128)(2,1)S(1)}, u32[]{:S(2)}, u32[]{:S(2)}) collective-permute-start(bf16[256,1024]{1,0:T(8,128)(2,1)S(1)} %get-tuple-element.37), channel_id=1, source_target_pairs={{0,1},{1,0},{2,3},{3,2},{4,5},{5,4},{6,7},{7,6},{8,9},{9,8},{10,11... | collective-permute-start | bytes 1572872 | tf_op jit(solution)/shard_map/ppermute | solution.py:409
  23.3 24.4 %collective-permute-start.4 = (bf16[256,1024]{1,0:T(8,128)(2,1)}, bf16[256,1024]{1,0:T(8,128)(2,1)}, u32[]{:S(2)}, u32[]{:S(2)}) collective-permute-start(bf16[256,1024]{1,0:T(8,128)(2,1)} %get-tuple-element.39), channel_id=1, source_target_pairs={{0,1},{1,0},{2,3},{3,2},{4,5},{5,4},{6,7},{7,6},{8,9},{9,8},{10,11... | collective-permute-start | bytes 1572872 | tf_op jit(solution)/shard_map/ppermute | solution.py:409
  25.1 22.8 %collective-permute-start.5 = (bf16[256,1024]{1,0:T(8,128)(2,1)S(1)}, bf16[256,1024]{1,0:T(8,128)(2,1)}, u32[]{:S(2)}, u32[]{:S(2)}) collective-permute-start(bf16[256,1024]{1,0:T(8,128)(2,1)S(1)} %add_convert_fusion.1), channel_id=1, source_target_pairs={{0,2},{1,3},{2,0},{3,1},{4,6},{5,7},{6,4},{7,5},{8,10},{9,11},{10,... | collective-permute-start | bytes 1572872 | tf_op jit(solution)/shard_map/ppermute | solution.py:409
  44.1 5.4 %collective-permute-start.6 = (bf16[512,768]{1,0:T(8,128)(2,1)}, bf16[512,768]{1,0:T(8,128)(2,1)S(1)}, u32[]{:S(2)}, u32[]{:S(2)}) collective-permute-start(bf16[512,768]{1,0:T(8,128)(2,1)} %get-tuple-element.42), channel_id=1, source_target_pairs={{0,4},{4,0},{8,12},{12,8},{16,20},{20,16},{24,28},{28,24},{1,5},{5... | collective-permute-start | bytes 2359304 | tf_op jit(solution)/shard_map/ppermute | solution.py:35
  44.2 15.1 %collective-permute-start.2 = (bf16[256,1024]{1,0:T(8,128)(2,1)}, bf16[256,1024]{1,0:T(8,128)(2,1)}, u32[]{:S(2)}, u32[]{:S(2)}) collective-permute-start(bf16[256,1024]{1,0:T(8,128)(2,1)} %get-tuple-element.33), channel_id=1, source_target_pairs={{0,1},{1,0},{2,3},{3,2},{4,5},{5,4},{6,7},{7,6},{8,9},{9,8},{10,11... | collective-permute-start | bytes 1572872 | tf_op jit(solution)/shard_map/ppermute | solution.py:409
  48.0 6.4 %copy-start.10 = (bf16[128,1024]{1,0:T(8,128)(2,1)S(1)}, bf16[128,1024]{1,0:T(8,128)(2,1)}, u32[]{:S(2)}) copy-start(bf16[128,1024]{1,0:T(8,128)(2,1)} %get-tuple-element.31) | copy-start | bytes 786436
  48.0 14.0 %copy-start.7 = (bf16[128,1024]{1,0:T(8,128)(2,1)S(1)}, bf16[128,1024]{1,0:T(8,128)(2,1)}, u32[]{:S(2)}) copy-start(bf16[128,1024]{1,0:T(8,128)(2,1)} %get-tuple-element.32) | copy-start | bytes 786436
  48.0 14.0 %copy-start.8 = (bf16[128,1024]{1,0:T(8,128)(2,1)S(1)}, bf16[128,1024]{1,0:T(8,128)(2,1)}, u32[]{:S(2)}) copy-start(bf16[128,1024]{1,0:T(8,128)(2,1)} %get-tuple-element.48) | copy-start | bytes 786436
  49.6 24.2 %copy-start.9 = (bf16[128,1024]{1,0:T(8,128)(2,1)S(1)}, bf16[128,1024]{1,0:T(8,128)(2,1)}, u32[]{:S(2)}) copy-start(bf16[128,1024]{1,0:T(8,128)(2,1)} %get-tuple-element.53) | copy-start | bytes 786436
  49.7 9.6 %collective-permute-start.7 = (bf16[128,768]{1,0:T(8,128)(2,1)S(1)}, bf16[128,768]{1,0:T(8,128)(2,1)S(1)}, u32[]{:S(2)}, u32[]{:S(2)}) collective-permute-start(bf16[128,768]{1,0:T(8,128)(2,1)S(1)} %get-tuple-element.44), channel_id=1, source_target_pairs={{0,8},{4,12},{8,0},{12,4},{16,24},{20,28},{24,16},{28,20},{1,9},{5... | collective-permute-start | bytes 589832 | tf_op jit(solution)/shard_map/ppermute | solution.py:35
  52.9 9.1 %collective-permute-start.8 = (bf16[128,768]{1,0:T(8,128)(2,1)S(1)}, bf16[128,768]{1,0:T(8,128)(2,1)S(1)}, u32[]{:S(2)}, u32[]{:S(2)}) collective-permute-start(bf16[128,768]{1,0:T(8,128)(2,1)S(1)} %get-tuple-element.45), channel_id=1, source_target_pairs={{0,16},{4,20},{8,24},{12,28},{16,0},{20,4},{24,8},{28,12},{1,17},{... | collective-permute-start | bytes 589832 | tf_op jit(solution)/shard_map/ppermute | solution.py:35
  54.4 7.6 %collective-permute-start.9 = (bf16[128,768]{1,0:T(8,128)(2,1)S(1)}, bf16[128,768]{1,0:T(8,128)(2,1)S(1)}, u32[]{:S(2)}, u32[]{:S(2)}) collective-permute-start(bf16[128,768]{1,0:T(8,128)(2,1)S(1)} %get-tuple-element.46), channel_id=1, source_target_pairs={{0,24},{4,28},{8,16},{12,20},{16,8},{20,12},{24,0},{28,4},{1,25},{... | collective-permute-start | bytes 589832 | tf_op jit(solution)/shard_map/ppermute | solution.py:35
  54.4 22.7 %collective-permute-start.1 = (bf16[128,1024]{1,0:T(8,128)(2,1)S(1)}, bf16[128,1024]{1,0:T(8,128)(2,1)S(1)}, u32[]{:S(2)}, u32[]{:S(2)}) collective-permute-start(bf16[128,1024]{1,0:T(8,128)(2,1)S(1)} %copy-done.10), channel_id=1, source_target_pairs={{0,1},{1,0},{2,3},{3,2},{4,5},{5,4},{6,7},{7,6},{8,9},{9,8},{10,11... | collective-permute-start | bytes 786440 | tf_op jit(solution)/shard_map/ppermute | solution.py:409
  62.0 21.4 %copy-start.6 = (bf16[128,1024]{1,0:T(8,128)(2,1)S(1)}, bf16[128,1024]{1,0:T(8,128)(2,1)}, u32[]{:S(2)}) copy-start(bf16[128,1024]{1,0:T(8,128)(2,1)} %get-tuple-element.30.refs_0_) | copy-start | bytes 786436
  63.3 20.2 %collective-permute-start.10 = (bf16[128,1024]{1,0:T(8,128)(2,1)S(1)}, bf16[128,1024]{1,0:T(8,128)(2,1)S(1)}, u32[]{:S(2)}, u32[]{:S(2)}) collective-permute-start(bf16[128,1024]{1,0:T(8,128)(2,1)S(1)} %get-tuple-element.55), channel_id=1, source_target_pairs={{0,2},{1,3},{2,0},{3,1},{4,6},{5,7},{6,4},{7,5},{8,10},{9,11},{10,... | collective-permute-start | bytes 786440 | tf_op jit(solution)/shard_map/ppermute | solution.py:409
  66.0 5.7 %collective-permute-start.12 = (bf16[128,768]{1,0:T(8,128)(2,1)S(1)}, bf16[128,768]{1,0:T(8,128)(2,1)S(1)}, u32[]{:S(2)}, u32[]{:S(2)}) collective-permute-start(bf16[128,768]{1,0:T(8,128)(2,1)S(1)} %shard_map.69.own_ref), channel_id=1, source_target_pairs={{0,8},{4,12},{8,0},{12,4},{16,24},{20,28},{24,16},{28,20},{1,9},{5... | collective-permute-start | bytes 589832 | tf_op jit(solution)/shard_map/ppermute | solution.py:35
  66.8 7.0 %collective-permute-start.13 = (bf16[128,768]{1,0:T(8,128)(2,1)S(1)}, bf16[128,768]{1,0:T(8,128)(2,1)S(1)}, u32[]{:S(2)}, u32[]{:S(2)}) collective-permute-start(bf16[128,768]{1,0:T(8,128)(2,1)S(1)} %shard_map.69.own_ref), channel_id=1, source_target_pairs={{0,16},{4,20},{8,24},{12,28},{16,0},{20,4},{24,8},{28,12},{1,17},{... | collective-permute-start | bytes 589832 | tf_op jit(solution)/shard_map/ppermute | solution.py:35
  68.3 8.7 %collective-permute-start.14 = (bf16[128,768]{1,0:T(8,128)(2,1)S(1)}, bf16[128,768]{1,0:T(8,128)(2,1)S(1)}, u32[]{:S(2)}, u32[]{:S(2)}) collective-permute-start(bf16[128,768]{1,0:T(8,128)(2,1)S(1)} %shard_map.69.own_ref), channel_id=1, source_target_pairs={{0,24},{4,28},{8,16},{12,20},{16,8},{20,12},{24,0},{28,4},{1,25},{... | collective-permute-start | bytes 589832 | tf_op jit(solution)/shard_map/ppermute | solution.py:35
  71.7 15.1 %collective-permute-start.17 = (bf16[128,1024]{1,0:T(8,128)(2,1)S(1)}, bf16[128,1024]{1,0:T(8,128)(2,1)S(1)}, u32[]{:S(2)}, u32[]{:S(2)}) collective-permute-start(bf16[128,1024]{1,0:T(8,128)(2,1)S(1)} %get-tuple-element.54), channel_id=1, source_target_pairs={{0,2},{1,3},{2,0},{3,1},{4,6},{5,7},{6,4},{7,5},{8,10},{9,11},{10,... | collective-permute-start | bytes 786440 | tf_op jit(solution)/shard_map/ppermute | solution.py:409
  73.8 13.0 %collective-permute-start.16 = (bf16[128,1024]{1,0:T(8,128)(2,1)S(1)}, bf16[128,1024]{1,0:T(8,128)(2,1)S(1)}, u32[]{:S(2)}, u32[]{:S(2)}) collective-permute-start(bf16[128,1024]{1,0:T(8,128)(2,1)S(1)} %copy-done.9), channel_id=1, source_target_pairs={{0,1},{1,0},{2,3},{3,2},{4,5},{5,4},{6,7},{7,6},{8,9},{9,8},{10,11... | collective-permute-start | bytes 786440 | tf_op jit(solution)/shard_map/ppermute | solution.py:409
  77.1 9.9 %collective-permute-start.15 = (bf16[512,768]{1,0:T(8,128)(2,1)S(1)}, bf16[512,768]{1,0:T(8,128)(2,1)S(1)}, u32[]{:S(2)}, u32[]{:S(2)}) collective-permute-start(bf16[512,768]{1,0:T(8,128)(2,1)S(1)} %shard_map.70.mine_ref), channel_id=1, source_target_pairs={{0,4},{4,0},{8,12},{12,8},{16,20},{20,16},{24,28},{28,24},{1,5},{5... | collective-permute-start | bytes 2359304 | tf_op jit(solution)/shard_map/ppermute | solution.py:35
  83.6 6.7 %collective-permute-start.11 = (bf16[128,1024]{1,0:T(8,128)(2,1)S(1)}, bf16[128,1024]{1,0:T(8,128)(2,1)S(1)}, u32[]{:S(2)}, u32[]{:S(2)}) collective-permute-start(bf16[128,1024]{1,0:T(8,128)(2,1)S(1)} %last_sum.2), channel_id=1, source_target_pairs={{0,4},{4,8},{8,12},{12,16},{16,20},{20,24},{24,28},{28,0},{1,5},{5... | collective-permute-start | bytes 786440 | tf_op jit(solution)/shard_map/ppermute | solution.py:30
  (5 other events, 26.6 us)

commit v5 on v4

--- a/solution.py
+++ b/solution.py
@@ -436,8 +436,8 @@
     )
     came = [swapped(part, 2 * (i + 1)) for i, part in enumerate(sent)]
 
-    in_both = after(in_both, own, *came)
-    out_next, out_this = add(next_c, in_both[:WIN]), add(this_c, in_both[WIN:])
+    in_both = after(in_both, own, came[0])
+    out_next, out_this = both_sums(next_c, this_c, in_both)
     more_this = hop(after(this_b, out_next), BESIDE)
     over_next, over_this = hop(out_next, ACROSS), hop(out_this, ACROSS)
 
@@ -466,6 +466,25 @@
     for ref in refs[1:-1]:
         total = total + ref[...].astype(jnp.float32)
     refs[-1][...] = total.astype(refs[-1].dtype)
+
+
+def both_kernel(next_ref, this_ref, came_ref, out_next_ref, out_this_ref):
+    came = came_ref[...].astype(jnp.float32)
+    out_next_ref[...] = (next_ref[...].astype(jnp.float32) + came[:WIN]).astype(out_next_ref.dtype)
+    out_this_ref[...] = (this_ref[...].astype(jnp.float32) + came[WIN:]).astype(out_this_ref.dtype)
+
+
+def both_sums(next_part, this_part, came):
+    shape = jax.ShapeDtypeStruct(next_part.shape, next_part.dtype)
+    return pl.pallas_call(
+        both_kernel,
+        in_specs=[VMEM] * 3,
+        out_specs=[VMEM] * 2,
+        out_shape=[shape, shape],
+        compiler_params=pltpu.CompilerParams(vmem_limit_bytes=SMALL_VMEM_BYTES),
+        cost_estimate=pl.CostEstimate(flops=1_000_000_000, bytes_accessed=1_000_000, transcendentals=0),
+        name="both_sums",
+    )(next_part, this_part, came)
 
 
 def last_sum(flops, *parts):

time: 91.7 us -> 89.5 us (0.976)
  waiting for transfers between devices: 24.6 us -> 21 us
  starting transfers between devices: 28.4 us -> 30.1 us
    ppermute x8, waiting for transfers between devices: 6.18 us -> 4.17 us  [swapped(): return lax.ppermute(shard, 'lon', [(i, i ^ bits) for i in range(size)])]
    ppermute x8, starting transfers between devices: 16.5 us -> 18.3 us  [hop(): lax.ppermute(x, 'head', [(i, i ^ bits) for i in range(lax.axis_size('head...]
    ppermute x2, waiting for transfers between devices: 1.51 us -> 0.01 us  [passed_along(): lax.ppermute(shard, axis, [(i, (i + by) % size) for i in range(size)])]
    convert_element_type x3 -> x2, other arithmetic: 2.99 us -> 2.53 us  [add(): return total.astype(jnp.bfloat16)]
  transfers between devices with their start and end apart: 18 -> 18, of which waited for: 10 -> 8; matrix products, arithmetic and copies ran while one was open for 3% -> 2% of each run, Pallas kernels for 34% -> 35%
where the time goes in v5:
time: 89.5 us; the launch traced here: 89.2 us
  Pallas kernels  33.6 us (38%)
  starting transfers between devices  30.1 us (34%)
  waiting for transfers between devices  21 us (23%)
  other arithmetic  3.56 us (4%)
    ppermute x8, starting transfers between devices, hop(): lax.ppermute(x, 'head', [(i, i ^ bits) for i in range(lax.axis_size('head...  18.3 us
    ppermute x8, waiting for transfers between devices, hop(): lax.ppermute(x, 'head', [(i, i ^ bits) for i in range(lax.axis_size('head...  16.8 us
    pallas_call x1, Pallas kernels, far_windows(): pl.pallas_call(far_kernel, in_specs=[SMEM] * 3 + [VMEM] * 3 + [ANYWHERE]...  16.4 us
    pallas_call x2, Pallas kernels, near_windows(): pl.pallas_call(functools.partial(near_kernel, start, steps), in_specs=spe...  12.3 us
    ppermute x8, starting transfers between devices, swapped(): return lax.ppermute(shard, 'lon', [(i, i ^ bits) for i in range(size)])  8.4 us
    ppermute x8, waiting for transfers between devices, swapped(): return lax.ppermute(shard, 'lon', [(i, i ^ bits) for i in range(size)])  4.17 us
    ppermute x2, starting transfers between devices, passed_along(): lax.ppermute(shard, axis, [(i, (i + by) % size) for i in range(size)])  3.44 us
    convert_element_type x2, other arithmetic, add(): return total.astype(jnp.bfloat16)  2.53 us
  transfers between devices with their start and end apart: 18, of which 8 were waited for; matrix products, arithmetic and copies ran while one was open for 2% of the time, Pallas kernels for 35%

profile of v5, /device:TPU:0, one launch (start us, length us, event | category | flops | bytes accessed | tf_op | source)
XLA Modules:
  0.0 89.2 jit_solution(9038542506006486707)
XLA Ops:
  0.7 2.5 %first_rows.1 = bf16[8,64,1280]{2,1,0:T(8,128)(2,1)} custom-call(bf16[8,256,1024]{2,1,0:T(8,128)(2,1)} %bitcast.13, bf16[8,256,256]{2,1,0:T(8,128)(2,1)} %bitcast.10), custom_call_target="tpu_custom_call" | custom-call | tf_op jit(solution)/shard_map/first_rows/pallas_call | solution.py:124
  3.2 3.4 %collective-permute-start = (bf16[8,64,1280]{2,1,0:T(8,128)(2,1)}, bf16[8,64,1280]{2,1,0:T(8,128)(2,1)}, u32[]{:S(2)}, u32[]{:S(2)}) collective-permute-start(bf16[8,64,1280]{2,1,0:T(8,128)(2,1)} %first_rows.1), channel_id=1, source_target_pairs={{0,28},{4,0},{8,4},{12,8},{16,12},{20,16},{24,20},{28,24},{1,29},{... | collective-permute-start | bytes 3932168 | tf_op jit(solution)/shard_map/ppermute | solution.py:30
  6.6 4.2 %near_windows.2 = (bf16[256,1024]{1,0:T(8,128)(2,1)S(1)}, bf16[12288,768]{1,0:T(8,128)(2,1)}) custom-call(s32[1]{0:T(128)} %bitcast.head_ref, s32[16]{0:T(128)S(1)} %copy-done.4, bf16[1024,768]{1,0:T(8,128)(2,1)S(1)} %copy-done.1, f32[4,128,128]{2,1,0:T(8,128)S(1)} %copy-done.2, bf16[2048,256]{1,0:T(8,128)(2,1)S(1)} %copy-done, bf16[8,256,1024]{2,1,0:T(8,128)(2,1)} %bitcast.14), custom_call_target="tpu_custom_call" | custom-call | flops 1000000 | bytes 100000 | tf_op jit(solution)/shard_map/near_windows/pallas_call | solution.py:207
  10.8 1.6 %collective-permute-start.3 = (bf16[256,1024]{1,0:T(8,128)(2,1)S(1)}, bf16[256,1024]{1,0:T(8,128)(2,1)S(1)}, u32[]{:S(2)}, u32[]{:S(2)}) collective-permute-start(bf16[256,1024]{1,0:T(8,128)(2,1)S(1)} %get-tuple-element.40), channel_id=1, source_target_pairs={{0,1},{1,0},{2,3},{3,2},{4,5},{5,4},{6,7},{7,6},{8,9},{9,8},{10,11... | collective-permute-start | bytes 1572872 | tf_op jit(solution)/shard_map/ppermute | solution.py:409
  12.4 8.1 %near_windows.3 = (bf16[256,1024]{1,0:T(8,128)(2,1)}, bf16[256,1024]{1,0:T(8,128)(2,1)S(1)}, bf16[256,1024]{1,0:T(8,128)(2,1)S(1)}, bf16[12288,768]{1,0:T(8,128)(2,1)}) custom-call(s32[1]{0:T(128)} %bitcast.head_ref, s32[16]{0:T(128)S(1)} %copy-done.4, bf16[1024,768]{1,0:T(8,128)(2,1)S(1)} %copy-done.1, ...), custom_call_target="tpu_custom_call", output_to_operand_aliasing={{3}: (6, {})} | custom-call | flops 1000000 | bytes 100000 | tf_op jit(solution)/shard_map/near_windows/pallas_call | solution.py:207
  20.5 2.6 %collective-permute-done.3 = bf16[256,1024]{1,0:T(8,128)(2,1)S(1)} collective-permute-done((bf16[256,1024]{1,0:T(8,128)(2,1)S(1)}, bf16[256,1024]{1,0:T(8,128)(2,1)S(1)}, u32[]{:S(2)}, u32[]{:S(2)}) %collective-permute-start.3) | collective-permute-done | bytes 524320 | tf_op jit(solution)/shard_map/ppermute | solution.py:409
  24.1 1.7 %collective-permute-start.4 = (bf16[256,1024]{1,0:T(8,128)(2,1)}, bf16[256,1024]{1,0:T(8,128)(2,1)}, u32[]{:S(2)}, u32[]{:S(2)}) collective-permute-start(bf16[256,1024]{1,0:T(8,128)(2,1)} %get-tuple-element.42), channel_id=1, source_target_pairs={{0,1},{1,0},{2,3},{3,2},{4,5},{5,4},{6,7},{7,6},{8,9},{9,8},{10,11... | collective-permute-start | bytes 1572872 | tf_op jit(solution)/shard_map/ppermute | solution.py:409
  25.9 2.6 %collective-permute-start.5 = (bf16[256,1024]{1,0:T(8,128)(2,1)}, bf16[256,1024]{1,0:T(8,128)(2,1)}, u32[]{:S(2)}, u32[]{:S(2)}) collective-permute-start(bf16[256,1024]{1,0:T(8,128)(2,1)} %add_convert_fusion.1), channel_id=1, source_target_pairs={{0,2},{1,3},{2,0},{3,1},{4,6},{5,7},{6,4},{7,5},{8,10},{9,11},{10,... | collective-permute-start | bytes 1572872 | tf_op jit(solution)/shard_map/ppermute | solution.py:409
  28.5 16.4 %far_windows.1 = (bf16[256,1024]{1,0:T(8,128)(2,1)}, bf16[128,1024]{1,0:T(8,128)(2,1)}, bf16[128,1024]{1,0:T(8,128)(2,1)}, bf16[128,1024]{1,0:T(8,128)(2,1)}, bf...) custom-call(s32[1]{0:T(128)} %bitcast.head_ref, ...), custom_call_target="tpu_custom_call" | custom-call | flops 1000000 | bytes 100000 | tf_op jit(solution)/shard_map/far_windows/pallas_call | solution.py:315
  45.4 2.9 %collective-permute-done.4 = bf16[256,1024]{1,0:T(8,128)(2,1)} collective-permute-done((bf16[256,1024]{1,0:T(8,128)(2,1)}, bf16[256,1024]{1,0:T(8,128)(2,1)}, u32[]{:S(2)}, u32[]{:S(2)}) %collective-permute-start.4) | collective-permute-done | bytes 524320 | tf_op jit(solution)/shard_map/ppermute | solution.py:409
  48.8 1.5 %add_convert_fusion = bf16[256,1024]{1,0:T(8,128)(2,1)S(1)} fusion(bf16[256,1024]{1,0:T(8,128)(2,1)} %collective-permute-done.5, bf16[256,1024]{1,0:T(8,128)(2,1)} %collective-permute-done.4, bf16[256,1024]{1,0:T(8,128)(2,1)S(1)} %get-tuple-element.37), kind=kLoop, calls=%fused_computation.1 | loop fusion | flops 1572864 | bytes 2097152 | tf_op jit(solution)/shard_map/convert_element_type | solution.py:398
  50.5 3.2 %collective-permute-start.7 = (bf16[128,768]{1,0:T(8,128)(2,1)S(1)}, bf16[128,768]{1,0:T(8,128)(2,1)S(1)}, u32[]{:S(2)}, u32[]{:S(2)}) collective-permute-start(bf16[128,768]{1,0:T(8,128)(2,1)S(1)} %get-tuple-element.47), channel_id=1, source_target_pairs={{0,8},{4,12},{8,0},{12,4},{16,24},{20,28},{24,16},{28,20},{1,9},{5... | collective-permute-start | bytes 589832 | tf_op jit(solution)/shard_map/ppermute | solution.py:35
  53.7 1.5 %collective-permute-start.10 = (bf16[128,768]{1,0:T(8,128)(2,1)S(1)}, bf16[128,768]{1,0:T(8,128)(2,1)S(1)}, u32[]{:S(2)}, u32[]{:S(2)}) collective-permute-start(bf16[128,768]{1,0:T(8,128)(2,1)S(1)} %get-tuple-element.52), channel_id=1, source_target_pairs={{0,16},{4,20},{8,24},{12,28},{16,0},{20,4},{24,8},{28,12},{1,17},{... | collective-permute-start | bytes 589832 | tf_op jit(solution)/shard_map/ppermute | solution.py:35
  55.2 3.4 %collective-permute-start.1 = (bf16[128,1024]{1,0:T(8,128)(2,1)S(1)}, bf16[128,1024]{1,0:T(8,128)(2,1)S(1)}, u32[]{:S(2)}, u32[]{:S(2)}) collective-permute-start(bf16[128,1024]{1,0:T(8,128)(2,1)S(1)} %copy-done.10), channel_id=1, source_target_pairs={{0,1},{1,0},{2,3},{3,2},{4,5},{5,4},{6,7},{7,6},{8,9},{9,8},{10,11... | collective-permute-start | bytes 786440 | tf_op jit(solution)/shard_map/ppermute | solution.py:409
  58.6 1.4 %collective-permute-done.2.came_ref = bf16[256,1024]{1,0:T(8,128)(2,1)S(1)} collective-permute-done((bf16[256,1024]{1,0:T(8,128)(2,1)}, bf16[256,1024]{1,0:T(8,128)(2,1)S(1)}, u32[]{:S(2)}, u32[]{:S(2)}) %collective-permute-start.2) | collective-permute-done | bytes 524320 | tf_op jit(solution)/shard_map/ppermute | solution.py:409
  60.2 4.5 %collective-permute-start.8 = (bf16[128,1024]{1,0:T(8,128)(2,1)S(1)}, bf16[128,1024]{1,0:T(8,128)(2,1)S(1)}, u32[]{:S(2)}, u32[]{:S(2)}) collective-permute-start(bf16[128,1024]{1,0:T(8,128)(2,1)S(1)} %get-tuple-element.49), channel_id=1, source_target_pairs={{0,2},{1,3},{2,0},{3,1},{4,6},{5,7},{6,4},{7,5},{8,10},{9,11},{10,... | collective-permute-start | bytes 786440 | tf_op jit(solution)/shard_map/ppermute | solution.py:409
  64.8 1.5 %collective-permute-start.12 = (bf16[128,768]{1,0:T(8,128)(2,1)S(1)}, bf16[128,768]{1,0:T(8,128)(2,1)S(1)}, u32[]{:S(2)}, u32[]{:S(2)}) collective-permute-start(bf16[128,768]{1,0:T(8,128)(2,1)S(1)} %shard_map.69.own_ref), channel_id=1, source_target_pairs={{0,8},{4,12},{8,0},{12,4},{16,24},{20,28},{24,16},{28,20},{1,9},{5... | collective-permute-start | bytes 589832 | tf_op jit(solution)/shard_map/ppermute | solution.py:35
  66.3 1.5 %collective-permute-start.13 = (bf16[128,768]{1,0:T(8,128)(2,1)S(1)}, bf16[128,768]{1,0:T(8,128)(2,1)S(1)}, u32[]{:S(2)}, u32[]{:S(2)}) collective-permute-start(bf16[128,768]{1,0:T(8,128)(2,1)S(1)} %shard_map.69.own_ref), channel_id=1, source_target_pairs={{0,16},{4,20},{8,24},{12,28},{16,0},{20,4},{24,8},{28,12},{1,17},{... | collective-permute-start | bytes 589832 | tf_op jit(solution)/shard_map/ppermute | solution.py:35
  68.4 2.9 %collective-permute-done.12.a_ref = bf16[128,768]{1,0:T(8,128)(2,1)S(1)} collective-permute-done((bf16[128,768]{1,0:T(8,128)(2,1)S(1)}, bf16[128,768]{1,0:T(8,128)(2,1)S(1)}, u32[]{:S(2)}, u32[]{:S(2)}) %collective-permute-start.12) | collective-permute-done | bytes 196640 | tf_op jit(solution)/shard_map/ppermute | solution.py:35
  72.1 1.2 %collective-permute-done.13.b_ref = bf16[128,768]{1,0:T(8,128)(2,1)S(1)} collective-permute-done((bf16[128,768]{1,0:T(8,128)(2,1)S(1)}, bf16[128,768]{1,0:T(8,128)(2,1)S(1)}, u32[]{:S(2)}, u32[]{:S(2)}) %collective-permute-start.13) | collective-permute-done | bytes 196640 | tf_op jit(solution)/shard_map/ppermute | solution.py:35
  73.3 3.2 %collective-permute-start.16 = (bf16[128,1024]{1,0:T(8,128)(2,1)S(1)}, bf16[128,1024]{1,0:T(8,128)(2,1)S(1)}, u32[]{:S(2)}, u32[]{:S(2)}) collective-permute-start(bf16[128,1024]{1,0:T(8,128)(2,1)S(1)} %copy-done.9), channel_id=1, source_target_pairs={{0,1},{1,0},{2,3},{3,2},{4,5},{5,4},{6,7},{7,6},{8,9},{9,8},{10,11... | collective-permute-start | bytes 786440 | tf_op jit(solution)/shard_map/ppermute | solution.py:409
  76.6 3.5 %collective-permute-done.8.refs_2_ = bf16[128,1024]{1,0:T(8,128)(2,1)S(1)} collective-permute-done((bf16[128,1024]{1,0:T(8,128)(2,1)S(1)}, bf16[128,1024]{1,0:T(8,128)(2,1)S(1)}, u32[]{:S(2)}, u32[]{:S(2)}) %collective-permute-start.8) | collective-permute-done | bytes 262176 | tf_op jit(solution)/shard_map/ppermute | solution.py:409
  80.3 5.9 %collective-permute-done.16.refs_1_ = bf16[128,1024]{1,0:T(8,128)(2,1)S(1)} collective-permute-done((bf16[128,1024]{1,0:T(8,128)(2,1)S(1)}, bf16[128,1024]{1,0:T(8,128)(2,1)S(1)}, u32[]{:S(2)}, u32[]{:S(2)}) %collective-permute-start.16) | collective-permute-done | bytes 262176 | tf_op jit(solution)/shard_map/ppermute | solution.py:409
  86.3 1.9 %shard_map.71 = f32[1024,768]{1,0:T(8,128)} custom-call(s32[1]{0:T(128)} %bitcast.1.core_ref, bf16[512,768]{1,0:T(8,128)(2,1)S(1)} %shard_map.70.mine_ref, bf16[512,768]{1,0:T(8,128)(2,1)S(1)} %collective-permute-done.15.theirs_ref), custom_call_target="tpu_custom_call" | custom-call | flops 1000000 | bytes 100000 | tf_op jit(solution)/shard_map/pallas_call | solution.py:380
  (48 shorter events, 5.2 us)
Async XLA Ops:
  3.2 20.0 %collective-permute-start = (bf16[8,64,1280]{2,1,0:T(8,128)(2,1)}, bf16[8,64,1280]{2,1,0:T(8,128)(2,1)}, u32[]{:S(2)}, u32[]{:S(2)}) collective-permute-start(bf16[8,64,1280]{2,1,0:T(8,128)(2,1)} %first_rows.1), channel_id=1, source_target_pairs={{0,28},{4,0},{8,4},{12,8},{16,12},{20,16},{24,20},{28,24},{1,29},{... | collective-permute-start | bytes 3932168 | tf_op jit(solution)/shard_map/ppermute | solution.py:30
  10.8 12.4 %collective-permute-start.3 = (bf16[256,1024]{1,0:T(8,128)(2,1)S(1)}, bf16[256,1024]{1,0:T(8,128)(2,1)S(1)}, u32[]{:S(2)}, u32[]{:S(2)}) collective-permute-start(bf16[256,1024]{1,0:T(8,128)(2,1)S(1)} %get-tuple-element.40), channel_id=1, source_target_pairs={{0,1},{1,0},{2,3},{3,2},{4,5},{5,4},{6,7},{7,6},{8,9},{9,8},{10,11... | collective-permute-start | bytes 1572872 | tf_op jit(solution)/shard_map/ppermute | solution.py:409
  24.1 24.2 %collective-permute-start.4 = (bf16[256,1024]{1,0:T(8,128)(2,1)}, bf16[256,1024]{1,0:T(8,128)(2,1)}, u32[]{:S(2)}, u32[]{:S(2)}) collective-permute-start(bf16[256,1024]{1,0:T(8,128)(2,1)} %get-tuple-element.42), channel_id=1, source_target_pairs={{0,1},{1,0},{2,3},{3,2},{4,5},{5,4},{6,7},{7,6},{8,9},{9,8},{10,11... | collective-permute-start | bytes 1572872 | tf_op jit(solution)/shard_map/ppermute | solution.py:409
  25.9 23.0 %collective-permute-start.5 = (bf16[256,1024]{1,0:T(8,128)(2,1)}, bf16[256,1024]{1,0:T(8,128)(2,1)}, u32[]{:S(2)}, u32[]{:S(2)}) collective-permute-start(bf16[256,1024]{1,0:T(8,128)(2,1)} %add_convert_fusion.1), channel_id=1, source_target_pairs={{0,2},{1,3},{2,0},{3,1},{4,6},{5,7},{6,4},{7,5},{8,10},{9,11},{10,... | collective-permute-start | bytes 1572872 | tf_op jit(solution)/shard_map/ppermute | solution.py:409
  44.8 5.5 %collective-permute-start.6 = (bf16[512,768]{1,0:T(8,128)(2,1)}, bf16[512,768]{1,0:T(8,128)(2,1)S(1)}, u32[]{:S(2)}, u32[]{:S(2)}) collective-permute-start(bf16[512,768]{1,0:T(8,128)(2,1)} %get-tuple-element.45), channel_id=1, source_target_pairs={{0,4},{4,0},{8,12},{12,8},{16,20},{20,16},{24,28},{28,24},{1,5},{5... | collective-permute-start | bytes 2359304 | tf_op jit(solution)/shard_map/ppermute | solution.py:35
  44.9 15.1 %collective-permute-start.2 = (bf16[256,1024]{1,0:T(8,128)(2,1)}, bf16[256,1024]{1,0:T(8,128)(2,1)S(1)}, u32[]{:S(2)}, u32[]{:S(2)}) collective-permute-start(bf16[256,1024]{1,0:T(8,128)(2,1)} %get-tuple-element.36), channel_id=1, source_target_pairs={{0,1},{1,0},{2,3},{3,2},{4,5},{5,4},{6,7},{7,6},{8,9},{9,8},{10,11... | collective-permute-start | bytes 1572872 | tf_op jit(solution)/shard_map/ppermute | solution.py:409
  48.8 6.4 %copy-start.10 = (bf16[128,1024]{1,0:T(8,128)(2,1)S(1)}, bf16[128,1024]{1,0:T(8,128)(2,1)}, u32[]{:S(2)}) copy-start(bf16[128,1024]{1,0:T(8,128)(2,1)} %get-tuple-element.33) | copy-start | bytes 786436
  48.8 11.2 %copy-start.7 = (bf16[128,1024]{1,0:T(8,128)(2,1)S(1)}, bf16[128,1024]{1,0:T(8,128)(2,1)}, u32[]{:S(2)}) copy-start(bf16[128,1024]{1,0:T(8,128)(2,1)} %get-tuple-element.34.next_ref) | copy-start | bytes 786436
  48.8 11.2 %copy-start.8 = (bf16[128,1024]{1,0:T(8,128)(2,1)S(1)}, bf16[128,1024]{1,0:T(8,128)(2,1)}, u32[]{:S(2)}) copy-start(bf16[128,1024]{1,0:T(8,128)(2,1)} %get-tuple-element.35.this_ref) | copy-start | bytes 786436
  50.5 9.5 %collective-permute-start.7 = (bf16[128,768]{1,0:T(8,128)(2,1)S(1)}, bf16[128,768]{1,0:T(8,128)(2,1)S(1)}, u32[]{:S(2)}, u32[]{:S(2)}) collective-permute-start(bf16[128,768]{1,0:T(8,128)(2,1)S(1)} %get-tuple-element.47), channel_id=1, source_target_pairs={{0,8},{4,12},{8,0},{12,4},{16,24},{20,28},{24,16},{28,20},{1,9},{5... | collective-permute-start | bytes 589832 | tf_op jit(solution)/shard_map/ppermute | solution.py:35
  53.7 11.0 %collective-permute-start.10 = (bf16[128,768]{1,0:T(8,128)(2,1)S(1)}, bf16[128,768]{1,0:T(8,128)(2,1)S(1)}, u32[]{:S(2)}, u32[]{:S(2)}) collective-permute-start(bf16[128,768]{1,0:T(8,128)(2,1)S(1)} %get-tuple-element.52), channel_id=1, source_target_pairs={{0,16},{4,20},{8,24},{12,28},{16,0},{20,4},{24,8},{28,12},{1,17},{... | collective-permute-start | bytes 589832 | tf_op jit(solution)/shard_map/ppermute | solution.py:35
  55.2 9.5 %collective-permute-start.11 = (bf16[128,768]{1,0:T(8,128)(2,1)S(1)}, bf16[128,768]{1,0:T(8,128)(2,1)S(1)}, u32[]{:S(2)}, u32[]{:S(2)}) collective-permute-start(bf16[128,768]{1,0:T(8,128)(2,1)S(1)} %get-tuple-element.53), channel_id=1, source_target_pairs={{0,24},{4,28},{8,16},{12,20},{16,8},{20,12},{24,0},{28,4},{1,25},{... | collective-permute-start | bytes 589832 | tf_op jit(solution)/shard_map/ppermute | solution.py:35
  55.2 21.4 %collective-permute-start.1 = (bf16[128,1024]{1,0:T(8,128)(2,1)S(1)}, bf16[128,1024]{1,0:T(8,128)(2,1)S(1)}, u32[]{:S(2)}, u32[]{:S(2)}) collective-permute-start(bf16[128,1024]{1,0:T(8,128)(2,1)S(1)} %copy-done.10), channel_id=1, source_target_pairs={{0,1},{1,0},{2,3},{3,2},{4,5},{5,4},{6,7},{7,6},{8,9},{9,8},{10,11... | collective-permute-start | bytes 786440 | tf_op jit(solution)/shard_map/ppermute | solution.py:409
  60.1 13.2 %copy-start.9 = (bf16[128,1024]{1,0:T(8,128)(2,1)S(1)}, bf16[128,1024]{1,0:T(8,128)(2,1)}, u32[]{:S(2)}) copy-start(bf16[128,1024]{1,0:T(8,128)(2,1)} %get-tuple-element.57) | copy-start | bytes 786436
  60.2 19.9 %copy-start.6 = (bf16[128,1024]{1,0:T(8,128)(2,1)S(1)}, bf16[128,1024]{1,0:T(8,128)(2,1)}, u32[]{:S(2)}) copy-start(bf16[128,1024]{1,0:T(8,128)(2,1)} %get-tuple-element.32.refs_0_) | copy-start | bytes 786436
  60.2 19.9 %collective-permute-start.8 = (bf16[128,1024]{1,0:T(8,128)(2,1)S(1)}, bf16[128,1024]{1,0:T(8,128)(2,1)S(1)}, u32[]{:S(2)}, u32[]{:S(2)}) collective-permute-start(bf16[128,1024]{1,0:T(8,128)(2,1)S(1)} %get-tuple-element.49), channel_id=1, source_target_pairs={{0,2},{1,3},{2,0},{3,1},{4,6},{5,7},{6,4},{7,5},{8,10},{9,11},{10,... | collective-permute-start | bytes 786440 | tf_op jit(solution)/shard_map/ppermute | solution.py:409
  64.8 6.5 %collective-permute-start.12 = (bf16[128,768]{1,0:T(8,128)(2,1)S(1)}, bf16[128,768]{1,0:T(8,128)(2,1)S(1)}, u32[]{:S(2)}, u32[]{:S(2)}) collective-permute-start(bf16[128,768]{1,0:T(8,128)(2,1)S(1)} %shard_map.69.own_ref), channel_id=1, source_target_pairs={{0,8},{4,12},{8,0},{12,4},{16,24},{20,28},{24,16},{28,20},{1,9},{5... | collective-permute-start | bytes 589832 | tf_op jit(solution)/shard_map/ppermute | solution.py:35
  66.3 7.0 %collective-permute-start.13 = (bf16[128,768]{1,0:T(8,128)(2,1)S(1)}, bf16[128,768]{1,0:T(8,128)(2,1)S(1)}, u32[]{:S(2)}, u32[]{:S(2)}) collective-permute-start(bf16[128,768]{1,0:T(8,128)(2,1)S(1)} %shard_map.69.own_ref), channel_id=1, source_target_pairs={{0,16},{4,20},{8,24},{12,28},{16,0},{20,4},{24,8},{28,12},{1,17},{... | collective-permute-start | bytes 589832 | tf_op jit(solution)/shard_map/ppermute | solution.py:35
  67.9 8.6 %collective-permute-start.14 = (bf16[128,768]{1,0:T(8,128)(2,1)S(1)}, bf16[128,768]{1,0:T(8,128)(2,1)S(1)}, u32[]{:S(2)}, u32[]{:S(2)}) collective-permute-start(bf16[128,768]{1,0:T(8,128)(2,1)S(1)} %shard_map.69.own_ref), channel_id=1, source_target_pairs={{0,24},{4,28},{8,16},{12,20},{16,8},{20,12},{24,0},{28,4},{1,25},{... | collective-permute-start | bytes 589832 | tf_op jit(solution)/shard_map/ppermute | solution.py:35
  71.3 14.9 %collective-permute-start.17 = (bf16[128,1024]{1,0:T(8,128)(2,1)S(1)}, bf16[128,1024]{1,0:T(8,128)(2,1)S(1)}, u32[]{:S(2)}, u32[]{:S(2)}) collective-permute-start(bf16[128,1024]{1,0:T(8,128)(2,1)S(1)} %get-tuple-element.50), channel_id=1, source_target_pairs={{0,2},{1,3},{2,0},{3,1},{4,6},{5,7},{6,4},{7,5},{8,10},{9,11},{10,... | collective-permute-start | bytes 786440 | tf_op jit(solution)/shard_map/ppermute | solution.py:409
  73.3 12.9 %collective-permute-start.16 = (bf16[128,1024]{1,0:T(8,128)(2,1)S(1)}, bf16[128,1024]{1,0:T(8,128)(2,1)S(1)}, u32[]{:S(2)}, u32[]{:S(2)}) collective-permute-start(bf16[128,1024]{1,0:T(8,128)(2,1)S(1)} %copy-done.9), channel_id=1, source_target_pairs={{0,1},{1,0},{2,3},{3,2},{4,5},{5,4},{6,7},{7,6},{8,9},{9,8},{10,11... | collective-permute-start | bytes 786440 | tf_op jit(solution)/shard_map/ppermute | solution.py:409
  76.5 9.8 %collective-permute-start.15 = (bf16[512,768]{1,0:T(8,128)(2,1)S(1)}, bf16[512,768]{1,0:T(8,128)(2,1)S(1)}, u32[]{:S(2)}, u32[]{:S(2)}) collective-permute-start(bf16[512,768]{1,0:T(8,128)(2,1)S(1)} %shard_map.70.mine_ref), channel_id=1, source_target_pairs={{0,4},{4,0},{8,12},{12,8},{16,20},{20,16},{24,28},{28,24},{1,5},{5... | collective-permute-start | bytes 2359304 | tf_op jit(solution)/shard_map/ppermute | solution.py:35
  80.1 6.1 %copy-start.5 = (bf16[128,1024]{1,0:T(8,128)(2,1)S(1)}, bf16[128,1024]{1,0:T(8,128)(2,1)}, u32[]{:S(2)}) copy-start(bf16[128,1024]{1,0:T(8,128)(2,1)} %get-tuple-element.55.refs_0_) | copy-start | bytes 786436
  80.2 8.0 %collective-permute-start.9 = (bf16[128,1024]{1,0:T(8,128)(2,1)S(1)}, bf16[128,1024]{1,0:T(8,128)(2,1)S(1)}, u32[]{:S(2)}, u32[]{:S(2)}) collective-permute-start(bf16[128,1024]{1,0:T(8,128)(2,1)S(1)} %last_sum.2), channel_id=1, source_target_pairs={{0,4},{4,8},{8,12},{12,16},{16,20},{20,24},{24,28},{28,0},{1,5},{5... | collective-permute-start | bytes 786440 | tf_op jit(solution)/shard_map/ppermute | solution.py:30
  (5 other events, 29.3 us)
